TPU v7x, 256 devices: a whole 4x4x8 slice. The times are simulated.
256 devices in a mesh: member: 8 (over y, core), space: 32 (over z, x).
Axes of the slice: x: 4, y: 4, z: 8, core: 2. Of those that a mesh axis runs over, the one named last changes fastest.
Arguments:
- state: float32 [256, 512, 1024], P('member', 'space'), may hold values from -8 to 8
- obs_index: int32 [32768], P('space'), may hold values from 0 to 16383
- obs_value: float32 [32768], P('space'), may hold values from -6 to 6
- obs_scale: float32 [32768], P('space'), may hold values from 0.3 to 3
- ksat: float32 [512, 1024], P('space'), may hold values from 0.05 to 0.2
- storage: float32 [512, 1024], P('space'), may hold values from 0.5 to 4
- recharge: float32 [512, 1024], P('space'), may hold values from -1.8 to 1.8
- newton_counts: int32 [256], replicated, may hold values from 1 to 8, as said below
Outputs:
- forecast: float32 [256, 512, 1024], P('member', 'space')
Inputs may be any that keep to these rules, and one draw needn't show every extreme that they name: `newton_counts`: A count of 8 occurs in every draw.
All inputs are finite; a program needn't handle non-finite values.
Results may differ from a plain program's by a relative error of at most 0.0003.
Values sent between devices are 32-bit elements; how exact they have to be, the bound alone decides.
No kernel may reach another device: no remote copies, remote signals or barrier semaphores. Data moves between devices by JAX's collectives and lax.ppermute only.
A program may use at most 64 MiB of HBM per device.

v0:
```python
import functools

import jax
import jax.numpy as jnp
from jax import lax
from jax.experimental import pallas as pl
from jax.experimental.pallas import tpu as pltpu
from jax.sharding import Mesh
from jax.sharding import PartitionSpec as P

NS_ITERS = 12
DAMPING = 0.3
MEMBER = ("member_0", "member_1")
SPACE = ("space_0", "space_1")
HIGHEST = lax.Precision.HIGHEST
F32 = jnp.float32

OWNERS = 8
HELD = 32
ROWS = 16
LANES = 128
MEMBERS = OWNERS * HELD
EDGE = ROWS
SENT_ROWS = ROWS + 1
OUTER = 36
OWN = 72


def shape(*dims, dtype=F32):
    return jax.ShapeDtypeStruct(dims, dtype)


def whole(count):
    return [pl.BlockSpec(memory_space=pltpu.VMEM)] * count


def params(mib):
    return pltpu.CompilerParams(vmem_limit_bytes=mib * 2**20)


SCALARS = pl.BlockSpec(memory_space=pltpu.SMEM)


def lane_ids(rows=8):
    return lax.broadcasted_iota(jnp.int32, (rows, LANES), 1)


def turned(array, amount):
    return pltpu.roll(array, amount % LANES, 1)


def dot(a, b, dims=((1,), (0,))):
    return lax.dot_general(a, b, (dims, ((), ())), precision=HIGHEST, preferred_element_type=F32)


def observe_kernel(index_ref, state_ref, seen_ref):
    values = state_ref[...]
    high = values.astype(jnp.bfloat16)
    rest = values - high.astype(F32)
    middle = rest.astype(jnp.bfloat16)
    low = (rest - middle.astype(F32)).astype(jnp.bfloat16)
    width = values.shape[1]
    step = 256
    for first in range(0, index_ref.shape[1], step):
        cell = index_ref[:, first : first + step]
        row = cell // width
        column = cell - row * width
        places = lax.broadcasted_iota(jnp.int32, (width, step), 0)
        chosen = (places == column).astype(F32).astype(jnp.bfloat16)
        picked = jnp.dot(low, chosen, preferred_element_type=F32)
        picked += jnp.dot(middle, chosen, preferred_element_type=F32)
        picked += jnp.dot(high, chosen, preferred_element_type=F32)
        picked = picked.reshape(HELD, ROWS, step)
        rows = lax.broadcasted_iota(jnp.int32, (ROWS, step), 0)
        seen_ref[:, first : first + step] = jnp.sum(
            jnp.where((rows == row)[None], picked, 0.0), axis=1
        )


def observed(state, obs_index):
    return pl.pallas_call(
        observe_kernel,
        out_shape=shape(HELD, obs_index.shape[1]),
        in_specs=whole(2),
        out_specs=whole(1)[0],
        compiler_params=params(32),
        name="observe",
    )(obs_index, state)


def pack_kernel(place_ref, state_ref, sent_ref, column_ref):
    own = place_ref[0]
    lane = lane_ids()
    even = lane % 2 == 0
    near_left = (lane < OUTER) & even
    near_right = (lane < OUTER) & ~even
    far_left = (lane >= OUTER) & (lane < OUTER + 2 * ROWS) & even
    far_right = (lane >= OUTER + 3) & (lane < OUTER + 3 + 2 * ROWS) & ~even

    def one_group(group, carry):
        near, far = [], []
        for block in range(OWNERS):
            slot = lax.rem(own - block + OWNERS, OWNERS)
            packed_near = jnp.zeros((8, LANES), F32)
            packed_far = jnp.zeros((8, LANES), F32)
            start = pl.multiple_of(group * 8 * ROWS, 8 * ROWS)
            column_ref[block] = state_ref[
                pl.ds(start, 8 * ROWS), block * LANES : (block + 1) * LANES
            ]
            for r in range(ROWS):
                value = column_ref[block, pl.ds(r, 8, stride=ROWS), :]
                sent_ref[slot, r, pl.ds(group * 8, 8)] = value
                at = 2 * (r + 1)
                packed_near = jnp.where(
                    (lane == at) | (lane == at + 1), turned(value, at + 1), packed_near
                )
                at = OUTER + 2 * r
                packed_far = jnp.where(
                    (lane == at) | (lane == at + 3), turned(value, at + 2), packed_far
                )
            near.append(packed_near)
            far.append(packed_far)
        nothing = jnp.zeros((8, LANES), F32)
        for block in range(OWNERS):
            slot = lax.rem(own - block + OWNERS, OWNERS)
            edge = turned(near[block], OWN)
            edge = jnp.where((lane >= OWN) & (lane < OWN + 2 * ROWS + 4), edge, nothing)
            if block > 0:
                edge = jnp.where(near_left, near[block - 1], edge)
                edge = jnp.where(far_left, far[block - 1], edge)
            if block < OWNERS - 1:
                edge = jnp.where(near_right, near[block + 1], edge)
                edge = jnp.where(far_right, far[block + 1], edge)
            sent_ref[slot, EDGE, pl.ds(group * 8, 8)] = edge
        return carry

    lax.fori_loop(0, HELD // 8, one_group, 0)


def packed_blocks(place, state):
    return pl.pallas_call(
        pack_kernel,
        out_shape=shape(OWNERS, SENT_ROWS, HELD, LANES),
        in_specs=[SCALARS] + whole(1),
        out_specs=whole(1)[0],
        scratch_shapes=[pltpu.VMEM((OWNERS, 8 * ROWS, LANES), F32)],
        compiler_params=params(16),
        name="pack",
    )(place, state)


def gram_kernel(place_ref, same_ref, other_ref, value_ref, scale_ref, out_ref):
    own = place_ref[0]
    total = jnp.sum(same_ref[...], axis=(0, 1)) + jnp.sum(other_ref[...], axis=(0, 1))
    mean = (total / MEMBERS)[None]
    scale = scale_ref[...]
    weight = scale / jnp.sqrt(F32(MEMBERS - 1))
    blocks = []
    for k in range(5):
        at = lax.rem(own + k, OWNERS) // 2
        block = same_ref[at] if k % 2 == 0 else other_ref[at]
        blocks.append((block - mean) * weight)
    innovation = scale * (value_ref[...] - mean)
    left = jnp.concatenate([blocks[0], jnp.broadcast_to(innovation, (8, mean.shape[1]))], axis=0)
    out_ref[0:40] = dot(left, jnp.concatenate(blocks[:4], axis=0), ((1,), (1,)))
    last = jnp.concatenate([blocks[4], jnp.zeros((96, mean.shape[1]), F32)], axis=0)
    opposite = dot(blocks[0], last, ((1,), (1,)))
    packed = opposite[0:8]
    for g in range(1, 4):
        packed += turned(opposite[8 * g : 8 * g + 8], HELD * g)
    out_ref[40:48] = packed


def gram_blocks(place, same, other, value, scale):
    return pl.pallas_call(
        gram_kernel,
        out_shape=shape(48, LANES),
        in_specs=[SCALARS] + whole(4),
        out_specs=whole(1)[0],
        compiler_params=params(16),
        name="gram",
    )(place, same, other, value, scale)


def root_kernel(place_ref, parts_ref, out_ref, half_ref):
    own = place_ref[0]
    lane = lane_ids()
    drive_row = jnp.zeros((8, MEMBERS), F32)
    nothing = jnp.zeros((8, LANES), F32)
    for i in range(OWNERS):
        at = lax.rem(own + i, OWNERS)
        for g in range(4):
            rows = parts_ref[at, 8 * g : 8 * g + 8]
            rows = jnp.where(lane < HELD, 0.5 * rows, rows)
            fifth = turned(parts_ref[at, 40:48], -HELD * g)
            fifth = jnp.where(lane < HELD, 0.5 * fifth, 0.0)
            line = jnp.concatenate([rows, fifth], axis=1)
            half_ref[i * HELD + 8 * g : i * HELD + 8 * g + 8] = pltpu.roll(line, HELD * i, 1)
        drive = jnp.where(lane < HELD, parts_ref[at, 32:40], 0.0)
        line = jnp.concatenate([drive, nothing], axis=1)
        drive_row += pltpu.roll(line, HELD * i, 1)
    half = half_ref[...]
    rows = lax.broadcasted_iota(jnp.int32, (MEMBERS, MEMBERS), 0)
    columns = lax.broadcasted_iota(jnp.int32, (MEMBERS, MEMBERS), 1)
    identity = (rows == columns).astype(F32)
    big = identity + (half + half.T)
    norm = jnp.sqrt(jnp.sum(big * big))
    upper = big / norm
    middle = 1.5 * identity - 0.5 * upper
    upper = dot(upper, middle)
    lower = middle
    for _ in range(NS_ITERS - 2):
        middle = 1.5 * identity - 0.5 * dot(lower, upper)
        upper = dot(upper, middle)
        lower = dot(middle, lower)
    middle = 1.5 * identity - 0.5 * dot(lower, upper)
    root = dot(middle, lower) / jnp.sqrt(norm)
    weights = dot(dot(drive_row, root, ((1,), (1,))), root, ((1,), (1,)))
    out_ref[...] = root + weights[0:1] / jnp.sqrt(F32(MEMBERS - 1))


def transform_of(place, parts):
    return pl.pallas_call(
        root_kernel,
        out_shape=shape(MEMBERS, MEMBERS),
        in_specs=[SCALARS] + whole(1),
        out_specs=whole(1)[0],
        scratch_shapes=[pltpu.VMEM((MEMBERS, MEMBERS), F32)],
        compiler_params=params(16),
        name="root",
    )(place, parts)


UNITS = ROWS + 5


def analyse_kernel(*refs):
    transform_ref = refs[0]
    piece_refs = refs[1 : 1 + OWNERS]
    above_ref, below_ref = refs[1 + OWNERS : 3 + OWNERS]
    out_refs = refs[3 + OWNERS :]
    transform = transform_ref[...]
    lane = lax.broadcasted_iota(jnp.int32, (MEMBERS, LANES), 1)

    def stacked(unit):
        if unit < SENT_ROWS:
            return jnp.concatenate([ref[unit] for ref in piece_refs], axis=0)
        if unit < SENT_ROWS + 2:
            return jnp.concatenate([above_ref[i, unit - SENT_ROWS] for i in range(OWNERS)], axis=0)
        return jnp.concatenate([below_ref[i, unit - SENT_ROWS - 2] for i in range(OWNERS)], axis=0)

    def cells(unit):
        found = stacked(unit)
        if unit == EDGE:
            top = jnp.concatenate([above_ref[i, 2] for i in range(OWNERS)], axis=0)
            low = jnp.concatenate([below_ref[i, 2] for i in range(OWNERS)], axis=0)
            first = (lane < 2) | ((lane >= OWN) & (lane < OWN + 2))
            last = 2 * ROWS + 2
            final = ((lane >= last) & (lane < last + 2)) | (
                (lane >= OWN + last) & (lane < OWN + last + 2)
            )
            found = jnp.where(first, turned(top, -2 * ROWS), found)
            found = jnp.where(final, turned(low, 2 * ROWS), found)
        return found

    for first in range(0, UNITS, 2):
        units = range(first, min(first + 2, UNITS))
        found = [cells(u) for u in units]
        joined = found[0] if len(found) == 1 else jnp.concatenate(found, axis=1)
        mean = jnp.sum(joined, axis=0, keepdims=True) / MEMBERS
        result = dot(transform, joined - mean) + mean
        for at, unit in enumerate(units):
            for i in range(OWNERS):
                out_refs[i][unit] = result[
                    i * HELD : (i + 1) * HELD, at * LANES : (at + 1) * LANES
                ]


def analysed(transform, pieces, above, below):
    return pl.pallas_call(
        analyse_kernel,
        out_shape=[shape(UNITS, HELD, LANES)] * OWNERS,
        in_specs=whole(3 + OWNERS),
        out_specs=whole(OWNERS),
        compiler_params=params(24),
        name="analyse",
    )(transform, *pieces, above, below)


FIELD_ROWS = 20
NEAR_K, INNER_K, OUTER_K, NEAR_S, NEAR_R, NEAR_MASK = range(6)


def field_kernel(place_ref, ksat_ref, storage_ref, recharge_ref, above_ref, below_ref, out_ref, edge_ref):
    own = place_ref[0]
    lane = lane_ids(1)
    even = lane % 2 == 0
    start = pl.multiple_of(own * LANES, LANES)
    left_start = pl.multiple_of(jnp.maximum(own - 1, 0) * LANES, LANES)
    right_start = pl.multiple_of(jnp.minimum(own + 1, OWNERS - 1) * LANES, LANES)
    has_left = own > 0
    has_right = own < OWNERS - 1
    packed = [jnp.zeros((1, LANES), F32) for _ in range(5)]
    for which, ref in enumerate((ksat_ref, storage_ref, recharge_ref)):
        for place in range(FIELD_ROWS):
            r = place - 2

            def row_of(first):
                if r < 0:
                    return above_ref[which, r + 2 : r + 3, pl.ds(first, LANES)]
                if r >= ROWS:
                    return below_ref[which, r - ROWS : r - ROWS + 1, pl.ds(first, LANES)]
                return ref[r : r + 1, pl.ds(first, LANES)]

            mine = row_of(start)
            out_ref[which, place] = jnp.broadcast_to(mine, (8, LANES))
            if r < -1 or r > ROWS:
                continue
            at = 2 * (r + 1)
            here = (lane == at) | (lane == at + 1)
            left = jnp.where(has_left, row_of(left_start), 0.0)
            right = jnp.where(has_right, row_of(right_start), 0.0)
            near = jnp.where(lane < LANES // 2, right, left)
            near = turned(near, at + 1)
            if which == 0:
                inner = jnp.where(even, turned(mine, at), turned(mine, at + 2))
                outer = jnp.where(even, turned(left, at + 2), turned(right, at))
                packed[NEAR_K] = jnp.where(here, near, packed[NEAR_K])
                packed[INNER_K] = jnp.where(here, inner, packed[INNER_K])
                packed[OUTER_K] = jnp.where(here, outer, packed[OUTER_K])
            elif which == 1:
                packed[NEAR_S] = jnp.where(here, near, packed[NEAR_S])
            else:
                packed[NEAR_R] = jnp.where(here, near, packed[NEAR_R])
    for n in range(5):
        edge_ref[n] = jnp.broadcast_to(packed[n], (8, LANES))
    lane = lane_ids()
    keep = jnp.where(lane % 2 == 0, has_left.astype(F32), has_right.astype(F32))
    edge_ref[NEAR_MASK] = jnp.where((lane >= 2) & (lane < 2 * ROWS + 2), keep, 0.0)


def block_fields(place, ksat, storage, recharge, above, below):
    return pl.pallas_call(
        field_kernel,
        out_shape=[shape(3, FIELD_ROWS, 8, LANES), shape(6, 8, LANES)],
        in_specs=[SCALARS] + whole(5),
        out_specs=whole(2),
        compiler_params=params(8),
        name="fields",
    )(place, ksat, storage, recharge, above, below)


def logistic(x):
    return 0.5 * jnp.tanh(0.5 * x) + 0.5


def forecast_kernel(shift, place_ref, counts_ref, wide_ref, field_ref, edge_field_ref, cells_ref, out_ref, iterate, goal, edge_row):
    own = place_ref[0]
    has_above = place_ref[1].astype(F32)
    has_below = place_ref[2].astype(F32)
    owner = lax.rem(own + shift, OWNERS)
    lane = lane_ids()
    even = lane % 2 == 0
    first_lane = lane == 0
    ends = first_lane | (lane == LANES - 1)
    sat, store, rain = 0, 1, 2

    def face(level, other, cond, other_cond):
        return 0.5 * (cond + other_cond) * (other - level)

    def swapped(packed):
        return jnp.where(even, turned(packed, -1), turned(packed, 1))

    def one_group(group, carry):
        first_member = owner * HELD + group * 8
        most = counts_ref[first_member]
        for n in range(1, 8):
            most = jnp.maximum(most, counts_ref[first_member + n])
        counts = wide_ref[pl.ds(pl.multiple_of(first_member, 8), 8)]

        def begun(level, flux, storage):
            bend = jnp.tanh(level)
            held = storage * bend
            return level + DAMPING * flux / (1.0 + storage * (1.0 - bend * bend)), level + held + flux

        def swept(value, target, storage, sweep):
            bend = jnp.tanh(value)
            derivative = 1.0 + storage * (1.0 - bend * bend)
            moved = value - DAMPING * (value + storage * bend - target) / derivative
            return jnp.where(counts > sweep, moved, value)

        def cell_at(r):
            if r < 0:
                at = SENT_ROWS + r + 2
            elif r >= ROWS:
                at = SENT_ROWS + 2 + r - ROWS
            else:
                at = r
            return cells_ref[at, pl.ds(pl.multiple_of(group * 8, 8), 8)]

        packed = cells_ref[EDGE, pl.ds(pl.multiple_of(group * 8, 8), 8)]
        near = jnp.where(lane < OUTER, packed, 0.0)
        inner = jnp.where(even, turned(packed, -OWN - 1), turned(packed, -OWN + 1))
        outer = jnp.where(even, turned(packed, 2 - OUTER), turned(packed, -OUTER))
        near_k = edge_field_ref[NEAR_K] * logistic(near)
        inner_k = edge_field_ref[INNER_K] * logistic(inner)
        outer_k = edge_field_ref[OUTER_K] * logistic(outer)
        inward = face(near, inner, near_k, inner_k)
        side = swapped(inward)
        flux = inward + face(near, outer, near_k, outer_k)
        flux += face(near, turned(near, 2), near_k, turned(near_k, 2))
        flux += face(near, turned(near, -2), near_k, turned(near_k, -2))
        flux += edge_field_ref[NEAR_R]
        value, target = begun(near, flux, edge_field_ref[NEAR_S])
        edge_row[0] = value
        edge_row[1] = target

        def conduct(level, r):
            return field_ref[sat, r + 2] * logistic(level)

        level, cond = cell_at(-1), conduct(cell_at(-1), -1)
        above = face(cell_at(-2), level, conduct(cell_at(-2), -2), cond)
        for r in range(-1, ROWS + 1):
            lower_level = cell_at(r + 1)
            lower_cond = conduct(lower_level, r + 1)
            under = face(level, lower_level, cond, lower_cond)
            across = face(turned(level, 1), level, turned(cond, 1), cond)
            across = jnp.where(first_lane, 0.0, across)
            flux = under - above + (turned(across, -1) - across)
            flux -= jnp.where(ends, turned(side, -2 * (r + 1) - 1), 0.0)
            flux += field_ref[rain, r + 2]
            iterate[r + 1], goal[r + 1] = begun(level, flux, field_ref[store, r + 2])
            level, cond, above = lower_level, lower_cond, under

        def first_sweep(sweep, carry):
            for n in range(ROWS + 2):
                iterate[n] = swept(iterate[n], goal[n], field_ref[store, n + 1], sweep)
            edge_row[0] = swept(edge_row[0], edge_row[1], edge_field_ref[NEAR_S], sweep)
            return carry

        lax.fori_loop(1, most, first_sweep, 0)

        near = edge_row[0] * edge_field_ref[NEAR_MASK]
        near_k = edge_field_ref[NEAR_K] * logistic(near)
        side = swapped(near)
        side_k = swapped(near_k)
        level = iterate[1]
        cond = conduct(level, 0)
        before = iterate[0] * has_above
        above = face(before, level, conduct(before, -1), cond)
        for r in range(ROWS):
            lower_level = iterate[r + 2]
            if r == ROWS - 1:
                lower_level = lower_level * has_below
            lower_cond = conduct(lower_level, r + 1)
            under = face(level, lower_level, cond, lower_cond)
            across = face(turned(level, 1), level, turned(cond, 1), cond)
            across = jnp.where(first_lane, 0.0, across)
            flux = under - above + (turned(across, -1) - across)
            turn = -2 * (r + 1) - 1
            entering = face(level, turned(side, turn), cond, turned(side_k, turn))
            flux += jnp.where(ends, entering, 0.0)
            flux += field_ref[rain, r + 2]
            iterate[r + 1], goal[r + 1] = begun(level, flux, field_ref[store, r + 2])
            level, cond, above = lower_level, lower_cond, under

        def second_sweep(sweep, carry):
            for n in range(1, ROWS + 1):
                iterate[n] = swept(iterate[n], goal[n], field_ref[store, n + 1], sweep)
            return carry

        lax.fori_loop(1, most, second_sweep, 0)
        for r in range(ROWS):
            out_ref[pl.ds(group * 8 * ROWS + r, 8, stride=ROWS), :] = iterate[r + 1]
        return carry

    lax.fori_loop(0, HELD // 8, one_group, 0)


def forecast_of(shift, place, counts, wide_counts, fields, edge_fields, cells):
    return pl.pallas_call(
        functools.partial(forecast_kernel, shift),
        out_shape=shape(HELD * ROWS, LANES),
        in_specs=[SCALARS, SCALARS] + whole(4),
        out_specs=whole(1)[0],
        scratch_shapes=[
            pltpu.VMEM((ROWS + 2, 8, LANES), F32),
            pltpu.VMEM((ROWS + 2, 8, LANES), F32),
            pltpu.VMEM((2, 8, LANES), F32),
        ],
        compiler_params=params(8),
        name="forecast",
    )(place, counts, wide_counts, fields, edge_fields, cells)


def unpack_kernel(place_ref, *refs):
    own = place_ref[0]
    pieces, out_ref, sems = refs[:OWNERS], refs[OWNERS], refs[OWNERS + 1]
    copies = []
    for i, piece in enumerate(pieces):
        block = lax.rem(own - i + OWNERS, OWNERS)
        start = pl.multiple_of(block * LANES, LANES)
        copies.append(
            pltpu.make_async_copy(piece, out_ref.at[:, pl.ds(start, LANES)], sems.at[i])
        )
    for copy in copies:
        copy.start()
    for copy in copies:
        copy.wait()


def unpacked(place, pieces):
    anywhere = pl.BlockSpec(memory_space=pl.ANY)
    return pl.pallas_call(
        unpack_kernel,
        out_shape=shape(HELD * ROWS, OWNERS * LANES),
        in_specs=[SCALARS] + [anywhere] * OWNERS,
        out_specs=anywhere,
        scratch_shapes=[pltpu.SemaphoreType.DMA((OWNERS,))],
        name="unpack",
    )(place, *pieces)


def shared(array, axis):
    peers = lax.axis_size(axis)
    copies = jnp.broadcast_to(array, (peers, *array.shape))
    return lax.all_to_all(copies, axis, split_axis=0, concat_axis=0, tiled=True)


def along(array, axis, step):
    peers = lax.axis_size(axis)
    return lax.ppermute(array, axis, [(i, (i + step) % peers) for i in range(peers)])


def to_strips_beside(array, step):
    peers = lax.axis_size(SPACE)
    pairs = [(i, i + step) for i in range(peers) if 0 <= i + step < peers]
    return lax.ppermute(array, SPACE, pairs)


def on_device(state, obs_index, obs_value, obs_scale, ksat, storage, recharge, newton_counts):
    members, rows, columns = state.shape
    flat = state.reshape(members * rows, columns)
    own = lax.axis_index(MEMBER)
    strip = lax.axis_index(SPACE)
    place = jnp.stack(
        [own, (strip > 0).astype(jnp.int32), (strip < lax.axis_size(SPACE) - 1).astype(jnp.int32)]
    ).astype(jnp.int32)

    seen = observed(flat, obs_index[None])
    same = shared(seen, MEMBER[0])
    other = along(same, MEMBER[1], 1)

    blocks = packed_blocks(place, flat)
    pieces = [blocks[0]]
    for i in range(1, OWNERS):
        pieces.append(along(blocks[i], MEMBER, -i))

    part = gram_blocks(place, same, other, obs_value[None], obs_scale[None])
    part = jnp.sum(shared(part, SPACE[0]), axis=0)
    part = jnp.sum(shared(part, SPACE[1]), axis=0)
    transform = transform_of(place, shared(part, MEMBER))

    cell_fields = jnp.stack([ksat, storage, recharge])
    fields_above = to_strips_beside(cell_fields[:, -2:], 1)
    fields_below = to_strips_beside(cell_fields[:, :2], -1)
    fields, edge_fields = block_fields(place, ksat, storage, recharge, fields_above, fields_below)
    wide_counts = jnp.broadcast_to(newton_counts[:, None], (MEMBERS, LANES))

    above = to_strips_beside(jnp.stack([p[ROWS - 2 :] for p in pieces]), 1)
    below = to_strips_beside(
        jnp.stack([jnp.concatenate([p[:2], p[EDGE:]], axis=0) for p in pieces]), -1
    )
    cells = analysed(transform, pieces, above, below)

    arrived = [None] * OWNERS
    for i in (2, 6, 3, 5, 4, 1, 7, 0):
        moved = forecast_of(i, place, newton_counts, wide_counts, fields, edge_fields, cells[i])
        arrived[i] = along(moved, MEMBER, i) if i else moved
    return unpacked(place, arrived).reshape(members, rows, columns)


def solution(mesh):
    x = 4
    finer = Mesh(
        mesh.devices.reshape(4, 2, -1, x), ("member_0", "member_1", "space_0", "space_1")
    )
    placed = (
        P(MEMBER, SPACE, None),
        P(SPACE),
        P(SPACE),
        P(SPACE),
        P(SPACE, None),
        P(SPACE, None),
        P(SPACE, None),
        P(),
    )
    return jax.shard_map(
        on_device, mesh=finer, in_specs=placed, out_specs=P(MEMBER, SPACE, None), check_vma=False
    )
```

profile of v0, /device:TPU:102, one launch (start us, length us, event | category | flops | bytes accessed | tf_op | source)
XLA Modules:
  0.0 234.6 jit_solution(11598883444107871068)
XLA Ops:
  8.9 2.9 %collective-permute-start.6 = (f32[17,32,128]{2,1,0:T(8,128)}, f32[17,32,128]{2,1,0:T(8,128)}, u32[]{:S(2)}, u32[]{:S(2)}) collective-permute-start(f32[17,32,128]{2,1,0:T(8,128)} %get-tuple-element.28), channel_id=1, source_target_pairs={{0,128},{32,160},{64,192},{96,224},{128,0},{160,32},{192,64},{224,... | collective-permute-start | bytes 835592 | tf_op jit(solution)/shard_map/ppermute | solution.py:532
  11.8 3.7 %observe.1 = f32[32,1024]{1,0:T(8,128)S(1)} custom-call(s32[1,1024]{1,0:T(1,128)S(1)} %bitcast.96, f32[512,1024]{1,0:T(8,128)S(1)} %bitcast.92), custom_call_target="tpu_custom_call" | custom-call | tf_op jit(solution)/shard_map/observe/pallas_call | solution.py:81
  16.4 4.1 %all-to-all-start = ((f32[4,32,1024]{2,1,0:T(8,128)}), f32[4,32,1024]{2,1,0:T(8,128)S(1)}, u32[]{:S(2)}, u32[]{:S(2)}) async-start(f32[4,32,1024]{2,1,0:T(8,128)} %broadcast_in_dim.29), calls=%async_computation | async-start | bytes 1048576 | tf_op jit(solution)/shard_map/all_to_all | solution.py:527
  23.8 9.1 %collective-permute-done.4.refs_3_ = f32[17,32,128]{2,1,0:T(8,128)} collective-permute-done((f32[17,32,128]{2,1,0:T(8,128)}, f32[17,32,128]{2,1,0:T(8,128)}, u32[]{:S(2)}, u32[]{:S(2)}) %collective-permute-start.4) | collective-permute-done | bytes 278560 | tf_op jit(solution)/shard_map/ppermute | solution.py:532
  44.6 2.7 %collective-permute-start.11 = (f32[8,3,32,128]{3,2,1,0:T(8,128)}, f32[8,3,32,128]{3,2,1,0:T(8,128)S(1)}, u32[]{:S(2)}, u32[]{:S(2)}) collective-permute-start(f32[8,3,32,128]{3,2,1,0:T(8,128)} %fusion.14), channel_id=1, source_target_pairs={{1,0},{2,1},{3,2},{4,3},{5,4},{6,5},{7,6},{8,7},{9,8},{10,9},{11,1... | collective-permute-start | bytes 1179656 | tf_op jit(solution)/shard_map/ppermute | solution.py:538
  56.4 7.7 %all-to-all-start.1 = ((f32[8,48,128]{2,1,0:T(8,128)}), f32[8,48,128]{2,1,0:T(8,128)S(1)}, u32[]{:S(2)}, u32[]{:S(2)}) async-start(f32[8,48,128]{2,1,0:T(8,128)} %broadcast_in_dim.32), calls=%async_computation.1 | async-start | bytes 393216 | tf_op jit(solution)/shard_map/all_to_all | solution.py:527
  64.6 6.4 %collective-permute-start.10 = (f32[8,3,32,128]{3,2,1,0:T(8,128)}, f32[8,3,32,128]{3,2,1,0:T(8,128)S(1)}, u32[]{:S(2)}, u32[]{:S(2)}) collective-permute-start(f32[8,3,32,128]{3,2,1,0:T(8,128)} %fusion), channel_id=1, source_target_pairs={{0,1},{1,2},{2,3},{3,4},{4,5},{5,6},{6,7},{7,8},{8,9},{9,10},{10,1... | collective-permute-start | bytes 1179656 | tf_op jit(solution)/shard_map/ppermute | solution.py:538
  71.7 8.5 %all_to_all.20 = f32[4,48,128]{2,1,0:T(8,128)S(1)} all-to-all(f32[4,48,128]{2,1,0:T(8,128)S(1)} %broadcast_in_dim.33), channel_id=1, replica_groups=mesh['member_0'=4,'member_1'=2,'space_0'=8,'space_1'=4] {'space_1'}, dimensions={0} | all-to-all | bytes 196608 | tf_op jit(solution)/shard_map/all_to_all | solution.py:527
  80.9 4.7 %all-to-all-start.3 = ((f32[8,48,128]{2,1,0:T(8,128)}), f32[8,48,128]{2,1,0:T(8,128)S(1)}, u32[]{:S(2)}, u32[]{:S(2)}) async-start(f32[8,48,128]{2,1,0:T(8,128)} %broadcast_in_dim.34), calls=%async_computation.3 | async-start | bytes 393216 | tf_op jit(solution)/shard_map/all_to_all | solution.py:527
  85.7 8.2 %collective-permute-start = (f32[3,2,1024]{2,1,0:T(2,128)S(1)}, f32[3,2,1024]{2,1,0:T(2,128)S(1)}, u32[]{:S(2)}, u32[]{:S(2)}) collective-permute-start(f32[3,2,1024]{2,1,0:T(2,128)S(1)} %get-tuple-element.34), channel_id=1, source_target_pairs={{0,1},{1,2},{2,3},{3,4},{4,5},{5,6},{6,7},{7,8},{8,9},{9,10},{10,1... | collective-permute-start | bytes 73736 | tf_op jit(solution)/shard_map/ppermute | solution.py:538
  96.0 6.9 %collective-permute-done.1.below_ref = f32[3,2,1024]{2,1,0:T(2,128)S(1)} collective-permute-done((f32[3,2,1024]{2,1,0:T(2,128)S(1)}, f32[3,2,1024]{2,1,0:T(2,128)S(1)}, u32[]{:S(2)}, u32[]{:S(2)}) %collective-permute-start.1) | collective-permute-done | bytes 24608 | tf_op jit(solution)/shard_map/ppermute | solution.py:538
  103.7 14.3 %root.1.refs_0_ = f32[256,256]{1,0:T(8,128)S(1)} custom-call(s32[3]{0:T(128)S(1)} %pad_add_fusion.place_ref, f32[8,48,128]{2,1,0:T(8,128)S(1)} %all-to-all-done.3.parts_ref), custom_call_target="tpu_custom_call" | custom-call | tf_op jit(solution)/shard_map/root/pallas_call | solution.py:223
  118.0 4.2 %analyse.1 = (f32[21,32,128]{2,1,0:T(8,128)S(1)}, f32[21,32,128]{2,1,0:T(8,128)S(1)}, f32[21,32,128]{2,1,0:T(8,128)S(1)}, f32[21,32,128]{2,1,0:T(8,128)S(1)}, f3...) custom-call(f32[256,256]{1,0:T(8,128)S(1)} %root.1.refs_0_, ...), custom_call_target="tpu_custom_call" | custom-call | tf_op jit(solution)/shard_map/analyse/pallas_call | solution.py:280
  122.3 5.1 %forecast.11 = f32[512,128]{1,0:T(8,128)S(1)} custom-call(s32[3]{0:T(128)S(1)} %pad_add_fusion.place_ref, s32[256]{0:T(256)S(1)} %copy-done.7, s32[256,128]{1,0:T(8,128)S(1)} %broadcast_in_dim.27.wide_ref, f32[3,20,8,128]{3,2,1,0:T(8,128)S(1)} %get-tuple-element.15.field_ref, f32[6,8,128]{2,1,0:T(8,128)S(1)} %get-tuple-element.16.edge_field_ref, ...), custom_call_target="tpu_custom_call" | custom-call | tf_op jit(solution)/shard_map/forecast/pallas_call | solution.py:481
  127.4 3.2 %forecast.12 = f32[512,128]{1,0:T(8,128)S(1)} custom-call(s32[3]{0:T(128)S(1)} %pad_add_fusion.place_ref, s32[256]{0:T(256)S(1)} %copy-done.7, s32[256,128]{1,0:T(8,128)S(1)} %broadcast_in_dim.27.wide_ref, f32[3,20,8,128]{3,2,1,0:T(8,128)S(1)} %get-tuple-element.15.field_ref, f32[6,8,128]{2,1,0:T(8,128)S(1)} %get-tuple-element.16.edge_field_ref, ...), custom_call_target="tpu_custom_call" | custom-call | tf_op jit(solution)/shard_map/forecast/pallas_call | solution.py:481
  132.4 3.2 %forecast.13 = f32[512,128]{1,0:T(8,128)S(1)} custom-call(s32[3]{0:T(128)S(1)} %pad_add_fusion.place_ref, s32[256]{0:T(256)S(1)} %copy-done.7, s32[256,128]{1,0:T(8,128)S(1)} %broadcast_in_dim.27.wide_ref, f32[3,20,8,128]{3,2,1,0:T(8,128)S(1)} %get-tuple-element.15.field_ref, f32[6,8,128]{2,1,0:T(8,128)S(1)} %get-tuple-element.16.edge_field_ref, ...), custom_call_target="tpu_custom_call" | custom-call | tf_op jit(solution)/shard_map/forecast/pallas_call | solution.py:481
  135.6 3.5 %collective-permute-start.16 = (f32[512,128]{1,0:T(8,128)S(1)}, f32[512,128]{1,0:T(8,128)S(1)}, u32[]{:S(2)}, u32[]{:S(2)}) collective-permute-start(f32[512,128]{1,0:T(8,128)S(1)} %forecast.13), channel_id=1, source_target_pairs={{0,160},{32,192},{64,224},{96,0},{128,32},{160,64},{192,96},{224,1... | collective-permute-start | bytes 786440 | tf_op jit(solution)/shard_map/ppermute | solution.py:532
  139.1 3.2 %forecast.14 = f32[512,128]{1,0:T(8,128)S(1)} custom-call(s32[3]{0:T(128)S(1)} %pad_add_fusion.place_ref, s32[256]{0:T(256)S(1)} %copy-done.7, s32[256,128]{1,0:T(8,128)S(1)} %broadcast_in_dim.27.wide_ref, f32[3,20,8,128]{3,2,1,0:T(8,128)S(1)} %get-tuple-element.15.field_ref, f32[6,8,128]{2,1,0:T(8,128)S(1)} %get-tuple-element.16.edge_field_ref, ...), custom_call_target="tpu_custom_call" | custom-call | tf_op jit(solution)/shard_map/forecast/pallas_call | solution.py:481
  144.9 3.2 %forecast.15 = f32[512,128]{1,0:T(8,128)S(1)} custom-call(s32[3]{0:T(128)S(1)} %pad_add_fusion.place_ref, s32[256]{0:T(256)S(1)} %copy-done.7, s32[256,128]{1,0:T(8,128)S(1)} %broadcast_in_dim.27.wide_ref, f32[3,20,8,128]{3,2,1,0:T(8,128)S(1)} %get-tuple-element.15.field_ref, f32[6,8,128]{2,1,0:T(8,128)S(1)} %get-tuple-element.16.edge_field_ref, ...), custom_call_target="tpu_custom_call" | custom-call | tf_op jit(solution)/shard_map/forecast/pallas_call | solution.py:481
  148.1 3.7 %forecast.10 = f32[512,128]{1,0:T(8,128)S(1)} custom-call(s32[3]{0:T(128)S(1)} %pad_add_fusion.place_ref, s32[256]{0:T(256)S(1)} %copy-done.7, s32[256,128]{1,0:T(8,128)S(1)} %broadcast_in_dim.27.wide_ref, f32[3,20,8,128]{3,2,1,0:T(8,128)S(1)} %get-tuple-element.15.field_ref, f32[6,8,128]{2,1,0:T(8,128)S(1)} %get-tuple-element.16.edge_field_ref, ...), custom_call_target="tpu_custom_call" | custom-call | tf_op jit(solution)/shard_map/forecast/pallas_call | solution.py:481
  151.8 3.2 %forecast.9 = f32[512,128]{1,0:T(8,128)S(1)} custom-call(s32[3]{0:T(128)S(1)} %pad_add_fusion.place_ref, s32[256]{0:T(256)S(1)} %copy-done.7, s32[256,128]{1,0:T(8,128)S(1)} %broadcast_in_dim.27.wide_ref, f32[3,20,8,128]{3,2,1,0:T(8,128)S(1)} %get-tuple-element.15.field_ref, f32[6,8,128]{2,1,0:T(8,128)S(1)} %get-tuple-element.16.edge_field_ref, ...), custom_call_target="tpu_custom_call" | custom-call | tf_op jit(solution)/shard_map/forecast/pallas_call | solution.py:481
  157.5 3.2 %forecast.8.refs_0_ = f32[512,128]{1,0:T(8,128)S(1)} custom-call(s32[3]{0:T(128)S(1)} %pad_add_fusion.place_ref, s32[256]{0:T(256)S(1)} %copy-done.7, s32[256,128]{1,0:T(8,128)S(1)} %broadcast_in_dim.27.wide_ref, f32[3,20,8,128]{3,2,1,0:T(8,128)S(1)} %get-tuple-element.15.field_ref, f32[6,8,128]{2,1,0:T(8,128)S(1)} %get-tuple-element.16.edge_field_ref, ...), custom_call_target="tpu_custom_call" | custom-call | tf_op jit(solution)/shard_map/forecast/pallas_call | solution.py:481
  164.0 4.2 %collective-permute-done.12.refs_1_ = f32[512,128]{1,0:T(8,128)S(1)} collective-permute-done((f32[512,128]{1,0:T(8,128)S(1)}, f32[512,128]{1,0:T(8,128)S(1)}, u32[]{:S(2)}, u32[]{:S(2)}) %collective-permute-start.12) | collective-permute-done | bytes 262176 | tf_op jit(solution)/shard_map/ppermute | solution.py:532
  169.0 65.4 %unpack.1 = f32[512,1024]{1,0:T(8,128)} custom-call(s32[3]{0:T(128)} %copy-done.6, f32[512,128]{1,0:T(8,128)} %copy-done.2, f32[512,128]{1,0:T(8,128)} %copy-done.17, f32[512,128]{1,0:T(8,128)} %copy-done.16, f32[512,128]{1,0:T(8,128)} %copy-done.11, f32[512,128]{1,0:T(8,128)} %copy-done.12, f32[512,128]{1,0:T(8,128)} %copy-done.13, f32[512,128]{1,0:T(8,128)} %copy-done.14, ...), custom_call_target="tpu_custom_call" | custom-call | tf_op jit(solution)/shard_map/unpack/pallas_call | solution.py:514
  (114 shorter events, 49.6 us)
Async XLA Ops:
  0.1 157.4 %copy-start.6 = (s32[3]{0:T(128)}, s32[3]{0:T(128)S(1)}, u32[]{:S(2)}) copy-start(s32[3]{0:T(128)S(1)} %pad_add_fusion.place_ref) | copy-start | bytes 40
  5.4 16.3 %collective-permute-start.3 = (f32[17,32,128]{2,1,0:T(8,128)}, f32[17,32,128]{2,1,0:T(8,128)S(1)}, u32[]{:S(2)}, u32[]{:S(2)}) collective-permute-start(f32[17,32,128]{2,1,0:T(8,128)} %get-tuple-element.31), channel_id=1, source_target_pairs={{0,224},{32,0},{64,32},{96,64},{128,96},{160,128},{192,160},{224,1... | collective-permute-start | bytes 835592 | tf_op jit(solution)/shard_map/ppermute | solution.py:532
  7.9 25.0 %collective-permute-start.4 = (f32[17,32,128]{2,1,0:T(8,128)}, f32[17,32,128]{2,1,0:T(8,128)}, u32[]{:S(2)}, u32[]{:S(2)}) collective-permute-start(f32[17,32,128]{2,1,0:T(8,128)} %get-tuple-element.30), channel_id=1, source_target_pairs={{0,192},{32,224},{64,0},{96,32},{128,64},{160,96},{192,128},{224,1... | collective-permute-start | bytes 835592 | tf_op jit(solution)/shard_map/ppermute | solution.py:532
  8.6 27.0 %collective-permute-start.5 = (f32[17,32,128]{2,1,0:T(8,128)}, f32[17,32,128]{2,1,0:T(8,128)}, u32[]{:S(2)}, u32[]{:S(2)}) collective-permute-start(f32[17,32,128]{2,1,0:T(8,128)} %get-tuple-element.29), channel_id=1, source_target_pairs={{0,160},{32,192},{64,224},{96,0},{128,32},{160,64},{192,96},{224,1... | collective-permute-start | bytes 835592 | tf_op jit(solution)/shard_map/ppermute | solution.py:532
  8.9 28.2 %collective-permute-start.6 = (f32[17,32,128]{2,1,0:T(8,128)}, f32[17,32,128]{2,1,0:T(8,128)}, u32[]{:S(2)}, u32[]{:S(2)}) collective-permute-start(f32[17,32,128]{2,1,0:T(8,128)} %get-tuple-element.28), channel_id=1, source_target_pairs={{0,128},{32,160},{64,192},{96,224},{128,0},{160,32},{192,64},{224,... | collective-permute-start | bytes 835592 | tf_op jit(solution)/shard_map/ppermute | solution.py:532
  11.8 28.0 %collective-permute-start.7 = (f32[17,32,128]{2,1,0:T(8,128)}, f32[17,32,128]{2,1,0:T(8,128)}, u32[]{:S(2)}, u32[]{:S(2)}) collective-permute-start(f32[17,32,128]{2,1,0:T(8,128)} %get-tuple-element.27), channel_id=1, source_target_pairs={{0,96},{32,128},{64,160},{96,192},{128,224},{160,0},{192,32},{224,... | collective-permute-start | bytes 835592 | tf_op jit(solution)/shard_map/ppermute | solution.py:532
  16.4 34.4 %all-to-all-start = ((f32[4,32,1024]{2,1,0:T(8,128)}), f32[4,32,1024]{2,1,0:T(8,128)S(1)}, u32[]{:S(2)}, u32[]{:S(2)}) async-start(f32[4,32,1024]{2,1,0:T(8,128)} %broadcast_in_dim.29), calls=%async_computation | async-start | bytes 1048576 | tf_op jit(solution)/shard_map/all_to_all | solution.py:527
  21.7 21.0 %collective-permute-start.8 = (f32[17,32,128]{2,1,0:T(8,128)}, f32[17,32,128]{2,1,0:T(8,128)S(1)}, u32[]{:S(2)}, u32[]{:S(2)}) collective-permute-start(f32[17,32,128]{2,1,0:T(8,128)} %get-tuple-element.26), channel_id=1, source_target_pairs={{0,64},{32,96},{64,128},{96,160},{128,192},{160,224},{192,0},{224,... | collective-permute-start | bytes 835592 | tf_op jit(solution)/shard_map/ppermute | solution.py:532
  32.9 11.1 %collective-permute-start.9 = (f32[17,32,128]{2,1,0:T(8,128)}, f32[17,32,128]{2,1,0:T(8,128)S(1)}, u32[]{:S(2)}, u32[]{:S(2)}) collective-permute-start(f32[17,32,128]{2,1,0:T(8,128)} %get-tuple-element.25), channel_id=1, source_target_pairs={{0,32},{32,64},{64,96},{96,128},{128,160},{160,192},{192,224},{224... | collective-permute-start | bytes 835592 | tf_op jit(solution)/shard_map/ppermute | solution.py:532
  38.6 47.1 %copy-start.5 = (f32[16,1024]{1,0:T(8,128)S(1)}, f32[16,1024]{1,0:T(8,128)}, u32[]{:S(2)}) copy-start(f32[16,1024]{1,0:T(8,128)} %recharge_ref.1) | copy-start | bytes 196612
  44.6 73.4 %collective-permute-start.11 = (f32[8,3,32,128]{3,2,1,0:T(8,128)}, f32[8,3,32,128]{3,2,1,0:T(8,128)S(1)}, u32[]{:S(2)}, u32[]{:S(2)}) collective-permute-start(f32[8,3,32,128]{3,2,1,0:T(8,128)} %fusion.14), channel_id=1, source_target_pairs={{1,0},{2,1},{3,2},{4,3},{5,4},{6,5},{7,6},{8,7},{9,8},{10,9},{11,1... | collective-permute-start | bytes 1179656 | tf_op jit(solution)/shard_map/ppermute | solution.py:538
  50.8 3.5 %collective-permute-start.2 = (f32[4,32,1024]{2,1,0:T(8,128)S(1)}, f32[4,32,1024]{2,1,0:T(8,128)S(1)}, u32[]{:S(2)}, u32[]{:S(2)}) collective-permute-start(f32[4,32,1024]{2,1,0:T(8,128)S(1)} %all-to-all-done.same_ref), channel_id=1, source_target_pairs={{0,32},{32,0},{1,33},{33,1},{2,34},{34,2},{3,35},{35,3},{4,36},{36... | collective-permute-start | bytes 1572872 | tf_op jit(solution)/shard_map/ppermute | solution.py:532
  56.4 15.3 %all-to-all-start.1 = ((f32[8,48,128]{2,1,0:T(8,128)}), f32[8,48,128]{2,1,0:T(8,128)S(1)}, u32[]{:S(2)}, u32[]{:S(2)}) async-start(f32[8,48,128]{2,1,0:T(8,128)} %broadcast_in_dim.32), calls=%async_computation.1 | async-start | bytes 393216 | tf_op jit(solution)/shard_map/all_to_all | solution.py:527
  64.6 53.4 %collective-permute-start.10 = (f32[8,3,32,128]{3,2,1,0:T(8,128)}, f32[8,3,32,128]{3,2,1,0:T(8,128)S(1)}, u32[]{:S(2)}, u32[]{:S(2)}) collective-permute-start(f32[8,3,32,128]{3,2,1,0:T(8,128)} %fusion), channel_id=1, source_target_pairs={{0,1},{1,2},{2,3},{3,4},{4,5},{5,6},{6,7},{7,8},{8,9},{9,10},{10,1... | collective-permute-start | bytes 1179656 | tf_op jit(solution)/shard_map/ppermute | solution.py:538
  80.9 22.8 %all-to-all-start.3 = ((f32[8,48,128]{2,1,0:T(8,128)}), f32[8,48,128]{2,1,0:T(8,128)S(1)}, u32[]{:S(2)}, u32[]{:S(2)}) async-start(f32[8,48,128]{2,1,0:T(8,128)} %broadcast_in_dim.34), calls=%async_computation.3 | async-start | bytes 393216 | tf_op jit(solution)/shard_map/all_to_all | solution.py:527
  85.7 10.3 %collective-permute-start = (f32[3,2,1024]{2,1,0:T(2,128)S(1)}, f32[3,2,1024]{2,1,0:T(2,128)S(1)}, u32[]{:S(2)}, u32[]{:S(2)}) collective-permute-start(f32[3,2,1024]{2,1,0:T(2,128)S(1)} %get-tuple-element.34), channel_id=1, source_target_pairs={{0,1},{1,2},{2,3},{3,4},{4,5},{5,6},{6,7},{7,8},{8,9},{9,10},{10,1... | collective-permute-start | bytes 73736 | tf_op jit(solution)/shard_map/ppermute | solution.py:538
  93.9 9.0 %collective-permute-start.1 = (f32[3,2,1024]{2,1,0:T(2,128)S(1)}, f32[3,2,1024]{2,1,0:T(2,128)S(1)}, u32[]{:S(2)}, u32[]{:S(2)}) collective-permute-start(f32[3,2,1024]{2,1,0:T(2,128)S(1)} %get-tuple-element.33), channel_id=1, source_target_pairs={{1,0},{2,1},{3,2},{4,3},{5,4},{6,5},{7,6},{8,7},{9,8},{10,9},{11,1... | collective-permute-start | bytes 73736 | tf_op jit(solution)/shard_map/ppermute | solution.py:538
  127.3 27.6 %collective-permute-start.14 = (f32[512,128]{1,0:T(8,128)S(1)}, f32[512,128]{1,0:T(8,128)S(1)}, u32[]{:S(2)}, u32[]{:S(2)}) collective-permute-start(f32[512,128]{1,0:T(8,128)S(1)} %forecast.11), channel_id=1, source_target_pairs={{0,96},{32,128},{64,160},{96,192},{128,224},{160,0},{192,32},{224,... | collective-permute-start | bytes 786440 | tf_op jit(solution)/shard_map/ppermute | solution.py:532
  130.6 25.3 %collective-permute-start.15 = (f32[512,128]{1,0:T(8,128)S(1)}, f32[512,128]{1,0:T(8,128)S(1)}, u32[]{:S(2)}, u32[]{:S(2)}) collective-permute-start(f32[512,128]{1,0:T(8,128)S(1)} %forecast.12), channel_id=1, source_target_pairs={{0,128},{32,160},{64,192},{96,224},{128,0},{160,32},{192,64},{224,... | collective-permute-start | bytes 786440 | tf_op jit(solution)/shard_map/ppermute | solution.py:532
  135.6 25.8 %collective-permute-start.16 = (f32[512,128]{1,0:T(8,128)S(1)}, f32[512,128]{1,0:T(8,128)S(1)}, u32[]{:S(2)}, u32[]{:S(2)}) collective-permute-start(f32[512,128]{1,0:T(8,128)S(1)} %forecast.13), channel_id=1, source_target_pairs={{0,160},{32,192},{64,224},{96,0},{128,32},{160,64},{192,96},{224,1... | collective-permute-start | bytes 786440 | tf_op jit(solution)/shard_map/ppermute | solution.py:532
  142.3 19.1 %collective-permute-start.17 = (f32[512,128]{1,0:T(8,128)S(1)}, f32[512,128]{1,0:T(8,128)S(1)}, u32[]{:S(2)}, u32[]{:S(2)}) collective-permute-start(f32[512,128]{1,0:T(8,128)S(1)} %forecast.14), channel_id=1, source_target_pairs={{0,192},{32,224},{64,0},{96,32},{128,64},{160,96},{192,128},{224,1... | collective-permute-start | bytes 786440 | tf_op jit(solution)/shard_map/ppermute | solution.py:532
  148.1 13.3 %collective-permute-start.18 = (f32[512,128]{1,0:T(8,128)S(1)}, f32[512,128]{1,0:T(8,128)S(1)}, u32[]{:S(2)}, u32[]{:S(2)}) collective-permute-start(f32[512,128]{1,0:T(8,128)S(1)} %forecast.15), channel_id=1, source_target_pairs={{0,224},{32,0},{64,32},{96,64},{128,96},{160,128},{192,160},{224,1... | collective-permute-start | bytes 786440 | tf_op jit(solution)/shard_map/ppermute | solution.py:532
  155.0 9.0 %collective-permute-start.13 = (f32[512,128]{1,0:T(8,128)S(1)}, f32[512,128]{1,0:T(8,128)S(1)}, u32[]{:S(2)}, u32[]{:S(2)}) collective-permute-start(f32[512,128]{1,0:T(8,128)S(1)} %forecast.10), channel_id=1, source_target_pairs={{0,64},{32,96},{64,128},{96,160},{128,192},{160,224},{192,0},{224,... | collective-permute-start | bytes 786440 | tf_op jit(solution)/shard_map/ppermute | solution.py:532
  155.9 12.3 %collective-permute-start.12 = (f32[512,128]{1,0:T(8,128)S(1)}, f32[512,128]{1,0:T(8,128)S(1)}, u32[]{:S(2)}, u32[]{:S(2)}) collective-permute-start(f32[512,128]{1,0:T(8,128)S(1)} %forecast.9), channel_id=1, source_target_pairs={{0,32},{32,64},{64,96},{96,128},{128,160},{160,192},{192,224},{224... | collective-permute-start | bytes 786440 | tf_op jit(solution)/shard_map/ppermute | solution.py:532
  (16 other events, 281.9 us)
where the time goes:
time: 235 us
  Pallas kernels  120 us (51%)
  starting transfers between devices  54.8 us (23%)
  waiting for transfers between devices  24.9 us (11%)
  local copies, waits for them, and re-layouts  20.8 us (9%)
  blocking collectives  8.51 us (4%)
  other arithmetic  5.08 us (2%)
    pallas_call x1, Pallas kernels, unpacked(): pl.pallas_call(unpack_kernel, out_shape=shape(HELD * ROWS, OWNERS * LANES...  65.4 us
    pallas_call x8, Pallas kernels, forecast_of(): pl.pallas_call(functools.partial(forecast_kernel, shift), out_shape=shape...  27.9 us
    ppermute x4, starting transfers between devices, to_strips_beside(): return lax.ppermute(array, SPACE, pairs)  19.4 us
    ppermute x15, starting transfers between devices, along(): lax.ppermute(array, axis, [(i, (i + step) % peers) for i in range(peers)])  18.9 us
    ppermute x15, waiting for transfers between devices, along(): lax.ppermute(array, axis, [(i, (i + step) % peers) for i in range(peers)])  17.4 us
    all_to_all x3, starting transfers between devices, shared(): return lax.all_to_all(copies, axis, split_axis=0, concat_axis=0, tiled=True)  16.5 us
    pallas_call x1, Pallas kernels, transform_of(): pl.pallas_call(root_kernel, out_shape=shape(MEMBERS, MEMBERS), in_specs=[...  14.3 us
    unnamed x43, local copies, waits for them, and re-layouts  10.6 us
  transfers between devices with their start and end apart: 22, of which 6 were waited for; matrix products, arithmetic and copies ran while one was open for 9% of the time, Pallas kernels for 18%

commit v1 on v0

--- a/solution.py
+++ b/solution.py
@@ -88,28 +88,34 @@
     )(obs_index, state)
 
 
-def pack_kernel(place_ref, state_ref, sent_ref, column_ref):
+ORDER = (0, 1, EDGE, ROWS - 2, ROWS - 1) + tuple(range(2, ROWS - 2))
+PLACE = {unit: at for at, unit in enumerate(ORDER)}
+
+
+def pack_kernel(place_ref, state_ref, after_ref, *refs):
     own = place_ref[0]
+    sent_refs, column_ref = refs[:OWNERS], refs[OWNERS]
     lane = lane_ids()
     even = lane % 2 == 0
     near_left = (lane < OUTER) & even
     near_right = (lane < OUTER) & ~even
     far_left = (lane >= OUTER) & (lane < OUTER + 2 * ROWS) & even
     far_right = (lane >= OUTER + 3) & (lane < OUTER + 3 + 2 * ROWS) & ~even
+    own_lanes = (lane >= OWN) & (lane < OWN + 2 * ROWS + 4)
 
     def one_group(group, carry):
         near, far = [], []
-        for block in range(OWNERS):
-            slot = lax.rem(own - block + OWNERS, OWNERS)
+        members = pl.ds(pl.multiple_of(group * 8, 8), 8)
+        lines = pl.ds(pl.multiple_of(group * 8 * ROWS, 8 * ROWS), 8 * ROWS)
+        for slot in range(OWNERS):
+            block = lax.rem(own - slot + OWNERS, OWNERS)
             packed_near = jnp.zeros((8, LANES), F32)
             packed_far = jnp.zeros((8, LANES), F32)
-            start = pl.multiple_of(group * 8 * ROWS, 8 * ROWS)
-            column_ref[block] = state_ref[
-                pl.ds(start, 8 * ROWS), block * LANES : (block + 1) * LANES
-            ]
+            start = pl.multiple_of(block * LANES, LANES)
+            column_ref[slot] = state_ref[lines, pl.ds(start, LANES)]
             for r in range(ROWS):
-                value = column_ref[block, pl.ds(r, 8, stride=ROWS), :]
-                sent_ref[slot, r, pl.ds(group * 8, 8)] = value
+                value = column_ref[slot, pl.ds(r, 8, stride=ROWS), :]
+                sent_refs[slot][PLACE[r], members] = value
                 at = 2 * (r + 1)
                 packed_near = jnp.where(
                     (lane == at) | (lane == at + 1), turned(value, at + 1), packed_near
@@ -120,33 +126,51 @@
                 )
             near.append(packed_near)
             far.append(packed_far)
-        nothing = jnp.zeros((8, LANES), F32)
-        for block in range(OWNERS):
-            slot = lax.rem(own - block + OWNERS, OWNERS)
-            edge = turned(near[block], OWN)
-            edge = jnp.where((lane >= OWN) & (lane < OWN + 2 * ROWS + 4), edge, nothing)
-            if block > 0:
-                edge = jnp.where(near_left, near[block - 1], edge)
-                edge = jnp.where(far_left, far[block - 1], edge)
-            if block < OWNERS - 1:
-                edge = jnp.where(near_right, near[block + 1], edge)
-                edge = jnp.where(far_right, far[block + 1], edge)
-            sent_ref[slot, EDGE, pl.ds(group * 8, 8)] = edge
+        for slot in range(OWNERS):
+            block = lax.rem(own - slot + OWNERS, OWNERS)
+            left, right = (slot + 1) % OWNERS, (slot - 1) % OWNERS
+            has_left = (block > 0).astype(F32)
+            has_right = (block < OWNERS - 1).astype(F32)
+            edge = jnp.where(own_lanes, turned(near[slot], OWN), 0.0)
+            edge = jnp.where(near_left, near[left] * has_left, edge)
+            edge = jnp.where(far_left, far[left] * has_left, edge)
+            edge = jnp.where(near_right, near[right] * has_right, edge)
+            edge = jnp.where(far_right, far[right] * has_right, edge)
+            sent_refs[slot][PLACE[EDGE], members] = edge
         return carry
 
     lax.fori_loop(0, HELD // 8, one_group, 0)
 
 
-def packed_blocks(place, state):
+def packed_blocks(place, state, after):
     return pl.pallas_call(
         pack_kernel,
-        out_shape=shape(OWNERS, SENT_ROWS, HELD, LANES),
-        in_specs=[SCALARS] + whole(1),
-        out_specs=whole(1)[0],
+        out_shape=[shape(SENT_ROWS, HELD, LANES)] * OWNERS,
+        in_specs=[SCALARS] + whole(1) + [pl.BlockSpec(memory_space=pl.ANY)],
+        out_specs=whole(OWNERS),
         scratch_shapes=[pltpu.VMEM((OWNERS, 8 * ROWS, LANES), F32)],
         compiler_params=params(16),
         name="pack",
-    )(place, state)
+    )(place, state, after)
+
+
+def border_kernel(*refs):
+    pieces, down_ref, up_ref = refs[:OWNERS], refs[OWNERS], refs[OWNERS + 1]
+    for i, piece in enumerate(pieces):
+        down_ref[i] = piece[0:3]
+        up_ref[i] = piece[2:5]
+
+
+def borders(pieces):
+    return pl.pallas_call(
+        border_kernel,
+        grid=(1,),
+        out_shape=[shape(OWNERS, 3, HELD, LANES)] * 2,
+        in_specs=[pl.BlockSpec((5, HELD, LANES), lambda g: (0, 0, 0))] * OWNERS,
+        out_specs=[pl.BlockSpec((OWNERS, 3, HELD, LANES), lambda g: (0, 0, 0, 0))] * 2,
+        compiler_params=params(8),
+        name="borders",
+    )(*pieces)
 
 
 def gram_kernel(place_ref, same_ref, other_ref, value_ref, scale_ref, out_ref):
@@ -234,41 +258,50 @@
 UNITS = ROWS + 5
 
 
+def halves(array):
+    high = array.astype(jnp.bfloat16)
+    return high, (array - high.astype(F32)).astype(jnp.bfloat16)
+
+
 def analyse_kernel(*refs):
     transform_ref = refs[0]
     piece_refs = refs[1 : 1 + OWNERS]
     above_ref, below_ref = refs[1 + OWNERS : 3 + OWNERS]
     out_refs = refs[3 + OWNERS :]
-    transform = transform_ref[...]
+    high, low = halves(transform_ref[...])
     lane = lax.broadcasted_iota(jnp.int32, (MEMBERS, LANES), 1)
 
-    def stacked(unit):
-        if unit < SENT_ROWS:
-            return jnp.concatenate([ref[unit] for ref in piece_refs], axis=0)
-        if unit < SENT_ROWS + 2:
-            return jnp.concatenate([above_ref[i, unit - SENT_ROWS] for i in range(OWNERS)], axis=0)
-        return jnp.concatenate([below_ref[i, unit - SENT_ROWS - 2] for i in range(OWNERS)], axis=0)
+    def joined(find):
+        return jnp.concatenate([find(i) for i in range(OWNERS)], axis=0)
 
     def cells(unit):
-        found = stacked(unit)
+        if unit > SENT_ROWS + 1:
+            return joined(lambda i: below_ref[i, unit - SENT_ROWS - 2])
+        if unit >= SENT_ROWS:
+            return joined(lambda i: above_ref[i, unit - SENT_ROWS + 1])
+        found = joined(lambda i: piece_refs[i][PLACE[unit]])
         if unit == EDGE:
-            top = jnp.concatenate([above_ref[i, 2] for i in range(OWNERS)], axis=0)
-            low = jnp.concatenate([below_ref[i, 2] for i in range(OWNERS)], axis=0)
+            top = joined(lambda i: above_ref[i, 0])
+            bottom = joined(lambda i: below_ref[i, 2])
             first = (lane < 2) | ((lane >= OWN) & (lane < OWN + 2))
             last = 2 * ROWS + 2
             final = ((lane >= last) & (lane < last + 2)) | (
                 (lane >= OWN + last) & (lane < OWN + last + 2)
             )
             found = jnp.where(first, turned(top, -2 * ROWS), found)
-            found = jnp.where(final, turned(low, 2 * ROWS), found)
+            found = jnp.where(final, turned(bottom, 2 * ROWS), found)
         return found
+
+    def product(a, b):
+        return jnp.dot(a, b, preferred_element_type=F32)
 
     for first in range(0, UNITS, 2):
         units = range(first, min(first + 2, UNITS))
         found = [cells(u) for u in units]
-        joined = found[0] if len(found) == 1 else jnp.concatenate(found, axis=1)
-        mean = jnp.sum(joined, axis=0, keepdims=True) / MEMBERS
-        result = dot(transform, joined - mean) + mean
+        state = found[0] if len(found) == 1 else jnp.concatenate(found, axis=1)
+        mean = jnp.sum(state, axis=0, keepdims=True) / MEMBERS
+        large, small = halves(state - mean)
+        result = product(low, large) + product(high, small) + product(high, large) + mean
         for at, unit in enumerate(units):
             for i in range(OWNERS):
                 out_refs[i][unit] = result[
@@ -315,6 +348,9 @@
             mine = row_of(start)
             out_ref[which, place] = jnp.broadcast_to(mine, (8, LANES))
             if r < -1 or r > ROWS:
+                if which == 0:
+                    out_ref[3, place] = jnp.zeros((8, LANES), F32)
+                    out_ref[4, place] = jnp.zeros((8, LANES), F32)
                 continue
             at = 2 * (r + 1)
             here = (lane == at) | (lane == at + 1)
@@ -323,6 +359,9 @@
             near = jnp.where(lane < LANES // 2, right, left)
             near = turned(near, at + 1)
             if which == 0:
+                out_ref[3, place] = jnp.broadcast_to(turned(mine, 1), (8, LANES))
+                beyond = jnp.where(lane == 0, turned(left, 1), turned(right, -1))
+                out_ref[4, place] = jnp.broadcast_to(beyond, (8, LANES))
                 inner = jnp.where(even, turned(mine, at), turned(mine, at + 2))
                 outer = jnp.where(even, turned(left, at + 2), turned(right, at))
                 packed[NEAR_K] = jnp.where(here, near, packed[NEAR_K])
@@ -342,7 +381,7 @@
 def block_fields(place, ksat, storage, recharge, above, below):
     return pl.pallas_call(
         field_kernel,
-        out_shape=[shape(3, FIELD_ROWS, 8, LANES), shape(6, 8, LANES)],
+        out_shape=[shape(5, FIELD_ROWS, 8, LANES), shape(6, 8, LANES)],
         in_specs=[SCALARS] + whole(5),
         out_specs=whole(2),
         compiler_params=params(8),
@@ -352,6 +391,9 @@
 
 def logistic(x):
     return 0.5 * jnp.tanh(0.5 * x) + 0.5
+
+
+BATCH = 16
 
 
 def forecast_kernel(shift, place_ref, counts_ref, wide_ref, field_ref, edge_field_ref, cells_ref, out_ref, iterate, goal, edge_row):
@@ -363,20 +405,26 @@
     even = lane % 2 == 0
     first_lane = lane == 0
     ends = first_lane | (lane == LANES - 1)
-    sat, store, rain = 0, 1, 2
+    sat, store, rain, left, ghosts = range(5)
+    tiles = BATCH // 8
+
+    def rolled(array, amount):
+        return pltpu.roll(array, amount % LANES, 2)
 
     def face(level, other, cond, other_cond):
         return 0.5 * (cond + other_cond) * (other - level)
 
     def swapped(packed):
-        return jnp.where(even, turned(packed, -1), turned(packed, 1))
-
-    def one_group(group, carry):
-        first_member = owner * HELD + group * 8
+        return jnp.where(even, rolled(packed, -1), rolled(packed, 1))
+
+    def one_batch(batch, carry):
+        first_member = owner * HELD + batch * BATCH
         most = counts_ref[first_member]
-        for n in range(1, 8):
+        for n in range(1, BATCH):
             most = jnp.maximum(most, counts_ref[first_member + n])
-        counts = wide_ref[pl.ds(pl.multiple_of(first_member, 8), 8)]
+        counts = wide_ref[pl.ds(pl.multiple_of(first_member, BATCH), BATCH)]
+        counts = counts.reshape(tiles, 8, LANES)
+        members = pl.ds(pl.multiple_of(batch * BATCH, BATCH), BATCH)
 
         def begun(level, flux, storage):
             bend = jnp.tanh(level)
@@ -389,27 +437,28 @@
             moved = value - DAMPING * (value + storage * bend - target) / derivative
             return jnp.where(counts > sweep, moved, value)
 
+        def unit_at(unit):
+            return cells_ref[unit, members].reshape(tiles, 8, LANES)
+
         def cell_at(r):
             if r < 0:
-                at = SENT_ROWS + r + 2
-            elif r >= ROWS:
-                at = SENT_ROWS + 2 + r - ROWS
-            else:
-                at = r
-            return cells_ref[at, pl.ds(pl.multiple_of(group * 8, 8), 8)]
-
-        packed = cells_ref[EDGE, pl.ds(pl.multiple_of(group * 8, 8), 8)]
+                return unit_at(SENT_ROWS + r + 2)
+            if r >= ROWS:
+                return unit_at(SENT_ROWS + 2 + r - ROWS)
+            return unit_at(r)
+
+        packed = unit_at(EDGE)
         near = jnp.where(lane < OUTER, packed, 0.0)
-        inner = jnp.where(even, turned(packed, -OWN - 1), turned(packed, -OWN + 1))
-        outer = jnp.where(even, turned(packed, 2 - OUTER), turned(packed, -OUTER))
+        inner = jnp.where(even, rolled(packed, -OWN - 1), rolled(packed, -OWN + 1))
+        outer = jnp.where(even, rolled(packed, 2 - OUTER), rolled(packed, -OUTER))
         near_k = edge_field_ref[NEAR_K] * logistic(near)
         inner_k = edge_field_ref[INNER_K] * logistic(inner)
         outer_k = edge_field_ref[OUTER_K] * logistic(outer)
         inward = face(near, inner, near_k, inner_k)
         side = swapped(inward)
         flux = inward + face(near, outer, near_k, outer_k)
-        flux += face(near, turned(near, 2), near_k, turned(near_k, 2))
-        flux += face(near, turned(near, -2), near_k, turned(near_k, -2))
+        flux += face(near, rolled(near, 2), near_k, rolled(near_k, 2))
+        flux += face(near, rolled(near, -2), near_k, rolled(near_k, -2))
         flux += edge_field_ref[NEAR_R]
         value, target = begun(near, flux, edge_field_ref[NEAR_S])
         edge_row[0] = value
@@ -424,10 +473,11 @@
             lower_level = cell_at(r + 1)
             lower_cond = conduct(lower_level, r + 1)
             under = face(level, lower_level, cond, lower_cond)
-            across = face(turned(level, 1), level, turned(cond, 1), cond)
+            beside = rolled(level, 1)
+            across = face(beside, level, field_ref[left, r + 2] * logistic(beside), cond)
             across = jnp.where(first_lane, 0.0, across)
-            flux = under - above + (turned(across, -1) - across)
-            flux -= jnp.where(ends, turned(side, -2 * (r + 1) - 1), 0.0)
+            flux = under - above + (rolled(across, -1) - across)
+            flux -= jnp.where(ends, rolled(side, -2 * (r + 1) - 1), 0.0)
             flux += field_ref[rain, r + 2]
             iterate[r + 1], goal[r + 1] = begun(level, flux, field_ref[store, r + 2])
             level, cond, above = lower_level, lower_cond, under
@@ -441,9 +491,7 @@
         lax.fori_loop(1, most, first_sweep, 0)
 
         near = edge_row[0] * edge_field_ref[NEAR_MASK]
-        near_k = edge_field_ref[NEAR_K] * logistic(near)
         side = swapped(near)
-        side_k = swapped(near_k)
         level = iterate[1]
         cond = conduct(level, 0)
         before = iterate[0] * has_above
@@ -454,11 +502,12 @@
                 lower_level = lower_level * has_below
             lower_cond = conduct(lower_level, r + 1)
             under = face(level, lower_level, cond, lower_cond)
-            across = face(turned(level, 1), level, turned(cond, 1), cond)
+            beside = rolled(level, 1)
+            across = face(beside, level, field_ref[left, r + 2] * logistic(beside), cond)
             across = jnp.where(first_lane, 0.0, across)
-            flux = under - above + (turned(across, -1) - across)
-            turn = -2 * (r + 1) - 1
-            entering = face(level, turned(side, turn), cond, turned(side_k, turn))
+            flux = under - above + (rolled(across, -1) - across)
+            ghost = rolled(side, -2 * (r + 1) - 1)
+            entering = face(level, ghost, cond, field_ref[ghosts, r + 2] * logistic(ghost))
             flux += jnp.where(ends, entering, 0.0)
             flux += field_ref[rain, r + 2]
             iterate[r + 1], goal[r + 1] = begun(level, flux, field_ref[store, r + 2])
@@ -471,10 +520,12 @@
 
         lax.fori_loop(1, most, second_sweep, 0)
         for r in range(ROWS):
-            out_ref[pl.ds(group * 8 * ROWS + r, 8, stride=ROWS), :] = iterate[r + 1]
+            for tile in range(tiles):
+                start = (batch * BATCH + tile * 8) * ROWS + r
+                out_ref[pl.ds(start, 8, stride=ROWS), :] = iterate[r + 1, tile]
         return carry
 
-    lax.fori_loop(0, HELD // 8, one_group, 0)
+    lax.fori_loop(0, HELD // BATCH, one_batch, 0)
 
 
 def forecast_of(shift, place, counts, wide_counts, fields, edge_fields, cells):
@@ -484,9 +535,9 @@
         in_specs=[SCALARS, SCALARS] + whole(4),
         out_specs=whole(1)[0],
         scratch_shapes=[
-            pltpu.VMEM((ROWS + 2, 8, LANES), F32),
-            pltpu.VMEM((ROWS + 2, 8, LANES), F32),
-            pltpu.VMEM((2, 8, LANES), F32),
+            pltpu.VMEM((ROWS + 2, BATCH // 8, 8, LANES), F32),
+            pltpu.VMEM((ROWS + 2, BATCH // 8, 8, LANES), F32),
+            pltpu.VMEM((2, BATCH // 8, 8, LANES), F32),
         ],
         compiler_params=params(8),
         name="forecast",
@@ -495,28 +546,23 @@
 
 def unpack_kernel(place_ref, *refs):
     own = place_ref[0]
-    pieces, out_ref, sems = refs[:OWNERS], refs[OWNERS], refs[OWNERS + 1]
-    copies = []
+    pieces, out_ref = refs[:OWNERS], refs[OWNERS]
     for i, piece in enumerate(pieces):
         block = lax.rem(own - i + OWNERS, OWNERS)
         start = pl.multiple_of(block * LANES, LANES)
-        copies.append(
-            pltpu.make_async_copy(piece, out_ref.at[:, pl.ds(start, LANES)], sems.at[i])
-        )
-    for copy in copies:
-        copy.start()
-    for copy in copies:
-        copy.wait()
+        out_ref[:, pl.ds(start, LANES)] = piece[...]
 
 
 def unpacked(place, pieces):
-    anywhere = pl.BlockSpec(memory_space=pl.ANY)
+    parts = 4
+    size = HELD * ROWS // parts
     return pl.pallas_call(
         unpack_kernel,
+        grid=(parts,),
         out_shape=shape(HELD * ROWS, OWNERS * LANES),
-        in_specs=[SCALARS] + [anywhere] * OWNERS,
-        out_specs=anywhere,
-        scratch_shapes=[pltpu.SemaphoreType.DMA((OWNERS,))],
+        in_specs=[SCALARS] + [pl.BlockSpec((size, LANES), lambda g: (g, 0))] * OWNERS,
+        out_specs=pl.BlockSpec((size, OWNERS * LANES), lambda g: (g, 0)),
+        compiler_params=params(8),
         name="unpack",
     )(place, *pieces)
 
@@ -549,28 +595,32 @@
 
     seen = observed(flat, obs_index[None])
     same = shared(seen, MEMBER[0])
+
+    cell_fields, _ = lax.optimization_barrier((jnp.stack([ksat, storage, recharge]), seen))
+    fields_above = to_strips_beside(cell_fields[:, -2:], 1)
+    fields_below = to_strips_beside(cell_fields[:, :2], -1)
+    blocks = packed_blocks(place, flat, seen)
+    fields, edge_fields = block_fields(place, ksat, storage, recharge, fields_above, fields_below)
+    wide_counts = jnp.broadcast_to(newton_counts[:, None], (MEMBERS, LANES))
+    same, blocks, fields, edge_fields, wide_counts = lax.optimization_barrier(
+        (same, blocks, fields, edge_fields, wide_counts)
+    )
     other = along(same, MEMBER[1], 1)
 
-    blocks = packed_blocks(place, flat)
-    pieces = [blocks[0]]
-    for i in range(1, OWNERS):
-        pieces.append(along(blocks[i], MEMBER, -i))
-
+    pieces = [blocks[0]] + [None] * (OWNERS - 1)
+    for i in (2, 6):
+        pieces[i] = along(blocks[i], MEMBER, -i)
     part = gram_blocks(place, same, other, obs_value[None], obs_scale[None])
+    part, blocks = lax.optimization_barrier((part, blocks))
+    for i in (3, 5, 4, 1, 7):
+        pieces[i] = along(blocks[i], MEMBER, -i)
     part = jnp.sum(shared(part, SPACE[0]), axis=0)
     part = jnp.sum(shared(part, SPACE[1]), axis=0)
+    part, pieces = lax.optimization_barrier((part, pieces))
+    down, up = borders(pieces)
+    above = to_strips_beside(up, 1)
+    below = to_strips_beside(down, -1)
     transform = transform_of(place, shared(part, MEMBER))
-
-    cell_fields = jnp.stack([ksat, storage, recharge])
-    fields_above = to_strips_beside(cell_fields[:, -2:], 1)
-    fields_below = to_strips_beside(cell_fields[:, :2], -1)
-    fields, edge_fields = block_fields(place, ksat, storage, recharge, fields_above, fields_below)
-    wide_counts = jnp.broadcast_to(newton_counts[:, None], (MEMBERS, LANES))
-
-    above = to_strips_beside(jnp.stack([p[ROWS - 2 :] for p in pieces]), 1)
-    below = to_strips_beside(
-        jnp.stack([jnp.concatenate([p[:2], p[EDGE:]], axis=0) for p in pieces]), -1
-    )
     cells = analysed(transform, pieces, above, below)
 
     arrived = [None] * OWNERS

time: 235 us -> 148 us (0.63)
  the two profiles are of different devices: /device:TPU:102 before, /device:TPU:33 now
where the time goes in v1:
time: 148 us; the launch traced here: 145 us
  Pallas kernels  47.9 us (32%)
  starting transfers between devices  47.6 us (32%)
  waiting for transfers between devices  25.5 us (17%)
  blocking collectives  18.4 us (12%)
  local copies, waits for them, and re-layouts  5.57 us (4%)
    ppermute x15, waiting for transfers between devices, along(): lax.ppermute(array, axis, [(i, (i + step) % peers) for i in range(peers)])  23.5 us
    pallas_call x8, Pallas kernels, forecast_of(): pl.pallas_call(functools.partial(forecast_kernel, shift), out_shape=shape...  21.4 us
    ppermute x15, starting transfers between devices, along(): lax.ppermute(array, axis, [(i, (i + step) % peers) for i in range(peers)])  20.8 us
    all_to_all x2, blocking collectives, shared(): return lax.all_to_all(copies, axis, split_axis=0, concat_axis=0, tiled=True)  18.4 us
    pallas_call x1, Pallas kernels, transform_of(): pl.pallas_call(root_kernel, out_shape=shape(MEMBERS, MEMBERS), in_specs=[...  14.3 us
    all_to_all x2, starting transfers between devices, shared(): return lax.all_to_all(copies, axis, split_axis=0, concat_axis=0, tiled=True)  13.6 us
    ppermute x4, starting transfers between devices, to_strips_beside(): return lax.ppermute(array, SPACE, pairs)  13.2 us
    unnamed x32, local copies, waits for them, and re-layouts  3.89 us
  transfers between devices with their start and end apart: 21, of which 8 were waited for; matrix products, arithmetic and copies ran while one was open for 1% of the time, Pallas kernels for 25%

profile of v1, /device:TPU:33, one launch (start us, length us, event | category | flops | bytes accessed | tf_op | source)
XLA Modules:
  0.0 145.3 jit_solution(3281934419930788562)
XLA Ops:
  2.3 3.7 %observe.1.after_ref = f32[32,1024]{1,0:T(8,128)S(1)} custom-call(s32[1,1024]{1,0:T(1,128)S(1)} %bitcast.16, f32[512,1024]{1,0:T(8,128)S(1)} %bitcast.11), custom_call_target="tpu_custom_call" | custom-call | tf_op jit(solution)/shard_map/observe/pallas_call | solution.py:81
  6.8 4.3 %all-to-all-start = ((f32[4,32,1024]{2,1,0:T(8,128)}), f32[4,32,1024]{2,1,0:T(8,128)S(1)}, u32[]{:S(2)}, u32[]{:S(2)}) async-start(f32[4,32,1024]{2,1,0:T(8,128)} %broadcast_in_dim.28), calls=%async_computation | async-start | bytes 1048576 | tf_op jit(solution)/shard_map/all_to_all | solution.py:573
  11.2 3.9 %collective-permute-start.1 = (f32[3,2,1024]{2,1,0:T(2,128)S(1)}, f32[3,2,1024]{2,1,0:T(2,128)S(1)}, u32[]{:S(2)}, u32[]{:S(2)}) collective-permute-start(f32[3,2,1024]{2,1,0:T(2,128)S(1)} %get-tuple-element.101), channel_id=1, source_target_pairs={{1,0},{2,1},{3,2},{4,3},{5,4},{6,5},{7,6},{8,7},{9,8},{10,9},{11,1... | collective-permute-start | bytes 73736 | tf_op jit(solution)/shard_map/ppermute | solution.py:584
  25.3 3.0 %collective-permute-start.4 = (f32[17,32,128]{2,1,0:T(8,128)}, f32[17,32,128]{2,1,0:T(8,128)S(1)}, u32[]{:S(2)}, u32[]{:S(2)}) collective-permute-start(f32[17,32,128]{2,1,0:T(8,128)} %copy-done.15), channel_id=1, source_target_pairs={{0,192},{32,224},{64,0},{96,32},{128,64},{160,96},{192,128},{224,1... | collective-permute-start | bytes 835592 | tf_op jit(solution)/shard_map/ppermute | solution.py:578
  30.4 9.2 %all-to-all-start.1 = ((f32[8,48,128]{2,1,0:T(8,128)}), f32[8,48,128]{2,1,0:T(8,128)S(1)}, u32[]{:S(2)}, u32[]{:S(2)}) async-start(f32[8,48,128]{2,1,0:T(8,128)} %broadcast_in_dim.32), calls=%async_computation.1 | async-start | bytes 393216 | tf_op jit(solution)/shard_map/all_to_all | solution.py:573
  40.5 2.8 %collective-permute-start.5 = (f32[17,32,128]{2,1,0:T(8,128)}, f32[17,32,128]{2,1,0:T(8,128)S(1)}, u32[]{:S(2)}, u32[]{:S(2)}) collective-permute-start(f32[17,32,128]{2,1,0:T(8,128)} %copy-done.12), channel_id=1, source_target_pairs={{0,160},{32,192},{64,224},{96,0},{128,32},{160,64},{192,96},{224,1... | collective-permute-start | bytes 835592 | tf_op jit(solution)/shard_map/ppermute | solution.py:578
  43.4 2.7 %collective-permute-start.7 = (f32[17,32,128]{2,1,0:T(8,128)}, f32[17,32,128]{2,1,0:T(8,128)S(1)}, u32[]{:S(2)}, u32[]{:S(2)}) collective-permute-start(f32[17,32,128]{2,1,0:T(8,128)} %copy-done.10), channel_id=1, source_target_pairs={{0,96},{32,128},{64,160},{96,192},{128,224},{160,0},{192,32},{224,... | collective-permute-start | bytes 835592 | tf_op jit(solution)/shard_map/ppermute | solution.py:578
  47.4 8.1 %all_to_all.20 = f32[4,48,128]{2,1,0:T(8,128)S(1)} all-to-all(f32[4,48,128]{2,1,0:T(8,128)S(1)} %broadcast_in_dim.33), channel_id=1, replica_groups=mesh['member_0'=4,'member_1'=2,'space_0'=8,'space_1'=4] {'space_1'}, dimensions={0} | all-to-all | bytes 196608 | tf_op jit(solution)/shard_map/all_to_all | solution.py:573
  55.5 6.1 %collective-permute-done.5.refs_3_.refs_4_ = f32[17,32,128]{2,1,0:T(8,128)S(1)} collective-permute-done((f32[17,32,128]{2,1,0:T(8,128)}, f32[17,32,128]{2,1,0:T(8,128)S(1)}, u32[]{:S(2)}, u32[]{:S(2)}) %collective-permute-start.5) | collective-permute-done | bytes 278560 | tf_op jit(solution)/shard_map/ppermute | solution.py:578
  65.4 5.5 %collective-permute-start.11 = (f32[8,3,32,128]{3,2,1,0:T(8,128)S(1)}, f32[8,3,32,128]{3,2,1,0:T(8,128)S(1)}, u32[]{:S(2)}, u32[]{:S(2)}) collective-permute-start(f32[8,3,32,128]{3,2,1,0:T(8,128)S(1)} %get-tuple-element.92), channel_id=1, source_target_pairs={{1,0},{2,1},{3,2},{4,3},{5,4},{6,5},{7,6},{8,7},{9,8},{10,9},{11,1... | collective-permute-start | bytes 1179656 | tf_op jit(solution)/shard_map/ppermute | solution.py:584
  70.9 10.2 %all_to_all.21.parts_ref = f32[8,48,128]{2,1,0:T(8,128)S(1)} all-to-all(f32[8,48,128]{2,1,0:T(8,128)S(1)} %broadcast_in_dim.34), channel_id=1, replica_groups=mesh['member_0'=4,'member_1'=2,'space_0'=8,'space_1'=4] {'member_0','mem..., dimensions={0} | all-to-all | bytes 393216 | tf_op jit(solution)/shard_map/all_to_all | solution.py:573
  81.1 14.3 %root.1.refs_0_ = f32[256,256]{1,0:T(8,128)S(1)} custom-call(s32[3]{0:T(128)S(1)} %pad_add_fusion.place_ref, f32[8,48,128]{2,1,0:T(8,128)S(1)} %all_to_all.21.parts_ref), custom_call_target="tpu_custom_call" | custom-call | tf_op jit(solution)/shard_map/root/pallas_call | solution.py:247
  96.9 4.1 %forecast.15 = f32[512,128]{1,0:T(8,128)S(1)} custom-call(s32[3]{0:T(128)S(1)} %pad_add_fusion.place_ref, s32[256]{0:T(256)S(1)} %copy-done.5, s32[256,128]{1,0:T(8,128)S(1)} %broadcast_in_dim.29.wide_ref, f32[5,20,8,128]{3,2,1,0:T(8,128)S(1)} %get-tuple-element.65.field_ref, f32[6,8,128]{2,1,0:T(8,128)S(1)} %get-tuple-element.66.edge_field_ref, ...), custom_call_target="tpu_custom_call" | custom-call | tf_op jit(solution)/shard_map/forecast/pallas_call | solution.py:532
  101.3 3.1 %forecast.14 = f32[512,128]{1,0:T(8,128)S(1)} custom-call(s32[3]{0:T(128)S(1)} %pad_add_fusion.place_ref, s32[256]{0:T(256)S(1)} %copy-done.5, s32[256,128]{1,0:T(8,128)S(1)} %broadcast_in_dim.29.wide_ref, f32[5,20,8,128]{3,2,1,0:T(8,128)S(1)} %get-tuple-element.65.field_ref, f32[6,8,128]{2,1,0:T(8,128)S(1)} %get-tuple-element.66.edge_field_ref, ...), custom_call_target="tpu_custom_call" | custom-call | tf_op jit(solution)/shard_map/forecast/pallas_call | solution.py:532
  104.5 2.4 %forecast.9 = f32[512,128]{1,0:T(8,128)S(1)} custom-call(s32[3]{0:T(128)S(1)} %pad_add_fusion.place_ref, s32[256]{0:T(256)S(1)} %copy-done.5, s32[256,128]{1,0:T(8,128)S(1)} %broadcast_in_dim.29.wide_ref, f32[5,20,8,128]{3,2,1,0:T(8,128)S(1)} %get-tuple-element.65.field_ref, f32[6,8,128]{2,1,0:T(8,128)S(1)} %get-tuple-element.66.edge_field_ref, ...), custom_call_target="tpu_custom_call" | custom-call | tf_op jit(solution)/shard_map/forecast/pallas_call | solution.py:532
  106.9 2.4 %forecast.10 = f32[512,128]{1,0:T(8,128)S(1)} custom-call(s32[3]{0:T(128)S(1)} %pad_add_fusion.place_ref, s32[256]{0:T(256)S(1)} %copy-done.5, s32[256,128]{1,0:T(8,128)S(1)} %broadcast_in_dim.29.wide_ref, f32[5,20,8,128]{3,2,1,0:T(8,128)S(1)} %get-tuple-element.65.field_ref, f32[6,8,128]{2,1,0:T(8,128)S(1)} %get-tuple-element.66.edge_field_ref, ...), custom_call_target="tpu_custom_call" | custom-call | tf_op jit(solution)/shard_map/forecast/pallas_call | solution.py:532
  109.2 2.4 %forecast.11 = f32[512,128]{1,0:T(8,128)S(1)} custom-call(s32[3]{0:T(128)S(1)} %pad_add_fusion.place_ref, s32[256]{0:T(256)S(1)} %copy-done.5, s32[256,128]{1,0:T(8,128)S(1)} %broadcast_in_dim.29.wide_ref, f32[5,20,8,128]{3,2,1,0:T(8,128)S(1)} %get-tuple-element.65.field_ref, f32[6,8,128]{2,1,0:T(8,128)S(1)} %get-tuple-element.66.edge_field_ref, ...), custom_call_target="tpu_custom_call" | custom-call | tf_op jit(solution)/shard_map/forecast/pallas_call | solution.py:532
  111.6 2.4 %forecast.12 = f32[512,128]{1,0:T(8,128)S(1)} custom-call(s32[3]{0:T(128)S(1)} %pad_add_fusion.place_ref, s32[256]{0:T(256)S(1)} %copy-done.5, s32[256,128]{1,0:T(8,128)S(1)} %broadcast_in_dim.29.wide_ref, f32[5,20,8,128]{3,2,1,0:T(8,128)S(1)} %get-tuple-element.65.field_ref, f32[6,8,128]{2,1,0:T(8,128)S(1)} %get-tuple-element.66.edge_field_ref, ...), custom_call_target="tpu_custom_call" | custom-call | tf_op jit(solution)/shard_map/forecast/pallas_call | solution.py:532
  114.0 2.4 %forecast.13 = f32[512,128]{1,0:T(8,128)S(1)} custom-call(s32[3]{0:T(128)S(1)} %pad_add_fusion.place_ref, s32[256]{0:T(256)S(1)} %copy-done.5, s32[256,128]{1,0:T(8,128)S(1)} %broadcast_in_dim.29.wide_ref, f32[5,20,8,128]{3,2,1,0:T(8,128)S(1)} %get-tuple-element.65.field_ref, f32[6,8,128]{2,1,0:T(8,128)S(1)} %get-tuple-element.66.edge_field_ref, ...), custom_call_target="tpu_custom_call" | custom-call | tf_op jit(solution)/shard_map/forecast/pallas_call | solution.py:532
  116.3 2.8 %collective-permute-start.16 = (f32[512,128]{1,0:T(8,128)S(1)}, f32[512,128]{1,0:T(8,128)S(1)}, u32[]{:S(2)}, u32[]{:S(2)}) collective-permute-start(f32[512,128]{1,0:T(8,128)S(1)} %forecast.13), channel_id=1, source_target_pairs={{0,160},{32,192},{64,224},{96,0},{128,32},{160,64},{192,96},{224,1... | collective-permute-start | bytes 786440 | tf_op jit(solution)/shard_map/ppermute | solution.py:578
  127.2 3.0 %collective-permute-done.16.refs_5_ = f32[512,128]{1,0:T(8,128)S(1)} collective-permute-done((f32[512,128]{1,0:T(8,128)S(1)}, f32[512,128]{1,0:T(8,128)S(1)}, u32[]{:S(2)}, u32[]{:S(2)}) %collective-permute-start.16) | collective-permute-done | bytes 262176 | tf_op jit(solution)/shard_map/ppermute | solution.py:578
  130.2 9.6 %collective-permute-done.14.refs_3_ = f32[512,128]{1,0:T(8,128)S(1)} collective-permute-done((f32[512,128]{1,0:T(8,128)S(1)}, f32[512,128]{1,0:T(8,128)S(1)}, u32[]{:S(2)}, u32[]{:S(2)}) %collective-permute-start.14) | collective-permute-done | bytes 262176 | tf_op jit(solution)/shard_map/ppermute | solution.py:578
  140.3 2.5 %collective-permute-done.12.refs_1_ = f32[512,128]{1,0:T(8,128)S(1)} collective-permute-done((f32[512,128]{1,0:T(8,128)S(1)}, f32[512,128]{1,0:T(8,128)S(1)}, u32[]{:S(2)}, u32[]{:S(2)}) %collective-permute-start.12) | collective-permute-done | bytes 262176 | tf_op jit(solution)/shard_map/ppermute | solution.py:578
  142.8 2.5 %unpack.1 = f32[512,1024]{1,0:T(8,128)} custom-call(s32[3]{0:T(128)S(1)} %pad_add_fusion.place_ref, f32[512,128]{1,0:T(8,128)S(1)} %forecast.8.refs_0_, f32[512,128]{1,0:T(8,128)S(1)} %collective-permute-done.12.refs_1_, f32[512,128]{1,0:T(8,128)S(1)} %collective-permute-done.13.refs_2_, f32[512,128]{1,0:T(8,128)S(1)} %collective-permute-done.14.refs_3_, ...), custom_call_target="tpu_custom_call" | custom-call | tf_op jit(solution)/shard_map/unpack/pallas_call | solution.py:559
  (78 shorter events, 31.7 us)
Async XLA Ops:
  6.8 16.0 %copy-start.5 = (s32[256]{0:T(256)S(1)}, s32[256]{0:T(256)}, u32[]{:S(2)}) copy-start(s32[256]{0:T(256)} %counts_ref.15) | copy-start | bytes 3076
  6.8 21.4 %copy-start.7 = (f32[1024]{0:T(1024)S(1)}, f32[1024]{0:T(1024)}, u32[]{:S(2)}) copy-start(f32[1024]{0:T(1024)} %param.10) | copy-start | bytes 12292
  6.8 21.4 %copy-start.8 = (f32[1024]{0:T(1024)S(1)}, f32[1024]{0:T(1024)}, u32[]{:S(2)}) copy-start(f32[1024]{0:T(1024)} %param.11) | copy-start | bytes 12292
  6.8 16.0 %all-to-all-start = ((f32[4,32,1024]{2,1,0:T(8,128)}), f32[4,32,1024]{2,1,0:T(8,128)S(1)}, u32[]{:S(2)}, u32[]{:S(2)}) async-start(f32[4,32,1024]{2,1,0:T(8,128)} %broadcast_in_dim.28), calls=%async_computation | async-start | bytes 1048576 | tf_op jit(solution)/shard_map/all_to_all | solution.py:573
  11.2 9.7 %collective-permute-start.1 = (f32[3,2,1024]{2,1,0:T(2,128)S(1)}, f32[3,2,1024]{2,1,0:T(2,128)S(1)}, u32[]{:S(2)}, u32[]{:S(2)}) collective-permute-start(f32[3,2,1024]{2,1,0:T(2,128)S(1)} %get-tuple-element.101), channel_id=1, source_target_pairs={{1,0},{2,1},{3,2},{4,3},{5,4},{6,5},{7,6},{8,7},{9,8},{10,9},{11,1... | collective-permute-start | bytes 73736 | tf_op jit(solution)/shard_map/ppermute | solution.py:584
  15.1 6.7 %collective-permute-start = (f32[3,2,1024]{2,1,0:T(2,128)S(1)}, f32[3,2,1024]{2,1,0:T(2,128)S(1)}, u32[]{:S(2)}, u32[]{:S(2)}) collective-permute-start(f32[3,2,1024]{2,1,0:T(2,128)S(1)} %get-tuple-element.102), channel_id=1, source_target_pairs={{0,1},{1,2},{2,3},{3,4},{4,5},{5,6},{6,7},{7,8},{8,9},{9,10},{10,1... | collective-permute-start | bytes 73736 | tf_op jit(solution)/shard_map/ppermute | solution.py:584
  22.9 5.3 %collective-permute-start.2 = (f32[4,32,1024]{2,1,0:T(8,128)S(1)}, f32[4,32,1024]{2,1,0:T(8,128)S(1)}, u32[]{:S(2)}, u32[]{:S(2)}) collective-permute-start(f32[4,32,1024]{2,1,0:T(8,128)S(1)} %all-to-all-done.same_ref), channel_id=1, source_target_pairs={{0,32},{32,0},{1,33},{33,1},{2,34},{34,2},{3,35},{35,3},{4,36},{36... | collective-permute-start | bytes 1572872 | tf_op jit(solution)/shard_map/ppermute | solution.py:578
  25.3 18.1 %collective-permute-start.4 = (f32[17,32,128]{2,1,0:T(8,128)}, f32[17,32,128]{2,1,0:T(8,128)S(1)}, u32[]{:S(2)}, u32[]{:S(2)}) collective-permute-start(f32[17,32,128]{2,1,0:T(8,128)} %copy-done.15), channel_id=1, source_target_pairs={{0,192},{32,224},{64,0},{96,32},{128,64},{160,96},{192,128},{224,1... | collective-permute-start | bytes 835592 | tf_op jit(solution)/shard_map/ppermute | solution.py:578
  28.2 17.9 %collective-permute-start.8 = (f32[17,32,128]{2,1,0:T(8,128)}, f32[17,32,128]{2,1,0:T(8,128)S(1)}, u32[]{:S(2)}, u32[]{:S(2)}) collective-permute-start(f32[17,32,128]{2,1,0:T(8,128)} %copy-done.14), channel_id=1, source_target_pairs={{0,64},{32,96},{64,128},{96,160},{128,192},{160,224},{192,0},{224,... | collective-permute-start | bytes 835592 | tf_op jit(solution)/shard_map/ppermute | solution.py:578
  30.4 16.9 %all-to-all-start.1 = ((f32[8,48,128]{2,1,0:T(8,128)}), f32[8,48,128]{2,1,0:T(8,128)S(1)}, u32[]{:S(2)}, u32[]{:S(2)}) async-start(f32[8,48,128]{2,1,0:T(8,128)} %broadcast_in_dim.32), calls=%async_computation.1 | async-start | bytes 393216 | tf_op jit(solution)/shard_map/all_to_all | solution.py:573
  39.6 15.9 %collective-permute-start.3 = (f32[17,32,128]{2,1,0:T(8,128)}, f32[17,32,128]{2,1,0:T(8,128)S(1)}, u32[]{:S(2)}, u32[]{:S(2)}) collective-permute-start(f32[17,32,128]{2,1,0:T(8,128)} %copy-done.13), channel_id=1, source_target_pairs={{0,224},{32,0},{64,32},{96,64},{128,96},{160,128},{192,160},{224,1... | collective-permute-start | bytes 835592 | tf_op jit(solution)/shard_map/ppermute | solution.py:578
  40.5 21.1 %collective-permute-start.5 = (f32[17,32,128]{2,1,0:T(8,128)}, f32[17,32,128]{2,1,0:T(8,128)S(1)}, u32[]{:S(2)}, u32[]{:S(2)}) collective-permute-start(f32[17,32,128]{2,1,0:T(8,128)} %copy-done.12), channel_id=1, source_target_pairs={{0,160},{32,192},{64,224},{96,0},{128,32},{160,64},{192,96},{224,1... | collective-permute-start | bytes 835592 | tf_op jit(solution)/shard_map/ppermute | solution.py:578
  43.4 18.2 %collective-permute-start.6 = (f32[17,32,128]{2,1,0:T(8,128)}, f32[17,32,128]{2,1,0:T(8,128)S(1)}, u32[]{:S(2)}, u32[]{:S(2)}) collective-permute-start(f32[17,32,128]{2,1,0:T(8,128)} %copy-done.11), channel_id=1, source_target_pairs={{0,128},{32,160},{64,192},{96,224},{128,0},{160,32},{192,64},{224,... | collective-permute-start | bytes 835592 | tf_op jit(solution)/shard_map/ppermute | solution.py:578
  43.4 20.0 %collective-permute-start.7 = (f32[17,32,128]{2,1,0:T(8,128)}, f32[17,32,128]{2,1,0:T(8,128)S(1)}, u32[]{:S(2)}, u32[]{:S(2)}) collective-permute-start(f32[17,32,128]{2,1,0:T(8,128)} %copy-done.10), channel_id=1, source_target_pairs={{0,96},{32,128},{64,160},{96,192},{128,224},{160,0},{192,32},{224,... | collective-permute-start | bytes 835592 | tf_op jit(solution)/shard_map/ppermute | solution.py:578
  46.1 17.3 %collective-permute-start.9 = (f32[17,32,128]{2,1,0:T(8,128)}, f32[17,32,128]{2,1,0:T(8,128)S(1)}, u32[]{:S(2)}, u32[]{:S(2)}) collective-permute-start(f32[17,32,128]{2,1,0:T(8,128)} %copy-done.9), channel_id=1, source_target_pairs={{0,32},{32,64},{64,96},{96,128},{128,160},{160,192},{192,224},{224... | collective-permute-start | bytes 835592 | tf_op jit(solution)/shard_map/ppermute | solution.py:578
  63.5 31.9 %collective-permute-start.10 = (f32[8,3,32,128]{3,2,1,0:T(8,128)S(1)}, f32[8,3,32,128]{3,2,1,0:T(8,128)S(1)}, u32[]{:S(2)}, u32[]{:S(2)}) collective-permute-start(f32[8,3,32,128]{3,2,1,0:T(8,128)S(1)} %get-tuple-element.91), channel_id=1, source_target_pairs={{0,1},{1,2},{2,3},{3,4},{4,5},{5,6},{6,7},{7,8},{8,9},{9,10},{10,1... | collective-permute-start | bytes 1179656 | tf_op jit(solution)/shard_map/ppermute | solution.py:584
  65.4 30.0 %collective-permute-start.11 = (f32[8,3,32,128]{3,2,1,0:T(8,128)S(1)}, f32[8,3,32,128]{3,2,1,0:T(8,128)S(1)}, u32[]{:S(2)}, u32[]{:S(2)}) collective-permute-start(f32[8,3,32,128]{3,2,1,0:T(8,128)S(1)} %get-tuple-element.92), channel_id=1, source_target_pairs={{1,0},{2,1},{3,2},{4,3},{5,4},{6,5},{7,6},{8,7},{9,8},{10,9},{11,1... | collective-permute-start | bytes 1179656 | tf_op jit(solution)/shard_map/ppermute | solution.py:584
  101.1 22.3 %collective-permute-start.18 = (f32[512,128]{1,0:T(8,128)S(1)}, f32[512,128]{1,0:T(8,128)S(1)}, u32[]{:S(2)}, u32[]{:S(2)}) collective-permute-start(f32[512,128]{1,0:T(8,128)S(1)} %forecast.15), channel_id=1, source_target_pairs={{0,224},{32,0},{64,32},{96,64},{128,96},{160,128},{192,160},{224,1... | collective-permute-start | bytes 786440 | tf_op jit(solution)/shard_map/ppermute | solution.py:578
  104.4 19.6 %collective-permute-start.17 = (f32[512,128]{1,0:T(8,128)S(1)}, f32[512,128]{1,0:T(8,128)S(1)}, u32[]{:S(2)}, u32[]{:S(2)}) collective-permute-start(f32[512,128]{1,0:T(8,128)S(1)} %forecast.14), channel_id=1, source_target_pairs={{0,192},{32,224},{64,0},{96,32},{128,64},{160,96},{192,128},{224,1... | collective-permute-start | bytes 786440 | tf_op jit(solution)/shard_map/ppermute | solution.py:578
  116.3 13.9 %collective-permute-start.16 = (f32[512,128]{1,0:T(8,128)S(1)}, f32[512,128]{1,0:T(8,128)S(1)}, u32[]{:S(2)}, u32[]{:S(2)}) collective-permute-start(f32[512,128]{1,0:T(8,128)S(1)} %forecast.13), channel_id=1, source_target_pairs={{0,160},{32,192},{64,224},{96,0},{128,32},{160,64},{192,96},{224,1... | collective-permute-start | bytes 786440 | tf_op jit(solution)/shard_map/ppermute | solution.py:578
  119.1 11.1 %collective-permute-start.15 = (f32[512,128]{1,0:T(8,128)S(1)}, f32[512,128]{1,0:T(8,128)S(1)}, u32[]{:S(2)}, u32[]{:S(2)}) collective-permute-start(f32[512,128]{1,0:T(8,128)S(1)} %forecast.12), channel_id=1, source_target_pairs={{0,128},{32,160},{64,192},{96,224},{128,0},{160,32},{192,64},{224,... | collective-permute-start | bytes 786440 | tf_op jit(solution)/shard_map/ppermute | solution.py:578
  121.3 18.5 %collective-permute-start.14 = (f32[512,128]{1,0:T(8,128)S(1)}, f32[512,128]{1,0:T(8,128)S(1)}, u32[]{:S(2)}, u32[]{:S(2)}) collective-permute-start(f32[512,128]{1,0:T(8,128)S(1)} %forecast.11), channel_id=1, source_target_pairs={{0,96},{32,128},{64,160},{96,192},{128,224},{160,0},{192,32},{224,... | collective-permute-start | bytes 786440 | tf_op jit(solution)/shard_map/ppermute | solution.py:578
  123.3 17.0 %collective-permute-start.13 = (f32[512,128]{1,0:T(8,128)S(1)}, f32[512,128]{1,0:T(8,128)S(1)}, u32[]{:S(2)}, u32[]{:S(2)}) collective-permute-start(f32[512,128]{1,0:T(8,128)S(1)} %forecast.10), channel_id=1, source_target_pairs={{0,64},{32,96},{64,128},{96,160},{128,192},{160,224},{192,0},{224,... | collective-permute-start | bytes 786440 | tf_op jit(solution)/shard_map/ppermute | solution.py:578
  124.0 18.8 %collective-permute-start.12 = (f32[512,128]{1,0:T(8,128)S(1)}, f32[512,128]{1,0:T(8,128)S(1)}, u32[]{:S(2)}, u32[]{:S(2)}) collective-permute-start(f32[512,128]{1,0:T(8,128)S(1)} %forecast.9), channel_id=1, source_target_pairs={{0,32},{32,64},{64,96},{96,128},{128,160},{160,192},{192,224},{224... | collective-permute-start | bytes 786440 | tf_op jit(solution)/shard_map/ppermute | solution.py:578
  (13 other events, 50.1 us)

commit v2 on v1

--- a/solution.py
+++ b/solution.py
@@ -83,7 +83,7 @@
         out_shape=shape(HELD, obs_index.shape[1]),
         in_specs=whole(2),
         out_specs=whole(1)[0],
-        compiler_params=params(32),
+        compiler_params=params(20),
         name="observe",
     )(obs_index, state)
 
@@ -149,28 +149,42 @@
         in_specs=[SCALARS] + whole(1) + [pl.BlockSpec(memory_space=pl.ANY)],
         out_specs=whole(OWNERS),
         scratch_shapes=[pltpu.VMEM((OWNERS, 8 * ROWS, LANES), F32)],
-        compiler_params=params(16),
+        compiler_params=params(8),
         name="pack",
     )(place, state, after)
 
 
+BORDER = OWNERS * 3 * HELD
+FIELD_LINES = 3 * 2 * OWNERS
+
+
 def border_kernel(*refs):
-    pieces, down_ref, up_ref = refs[:OWNERS], refs[OWNERS], refs[OWNERS + 1]
+    pieces, fields = refs[:OWNERS], refs[OWNERS : OWNERS + 3]
+    down_ref, up_ref = refs[OWNERS + 3 :]
+    size = 3 * HELD
     for i, piece in enumerate(pieces):
-        down_ref[i] = piece[0:3]
-        up_ref[i] = piece[2:5]
-
-
-def borders(pieces):
+        down_ref[i * size : (i + 1) * size] = piece[0:3].reshape(size, LANES)
+        up_ref[i * size : (i + 1) * size] = piece[2:5].reshape(size, LANES)
+    for which, ref in enumerate(fields):
+        for block in range(OWNERS):
+            at = BORDER + (which * OWNERS + block) * 2
+            lanes = slice(block * LANES, (block + 1) * LANES)
+            down_ref[at : at + 2] = ref[0:2, lanes]
+            up_ref[at : at + 2] = ref[ROWS - 2 : ROWS, lanes]
+
+
+def borders(pieces, fields):
+    size = BORDER + FIELD_LINES
     return pl.pallas_call(
         border_kernel,
         grid=(1,),
-        out_shape=[shape(OWNERS, 3, HELD, LANES)] * 2,
-        in_specs=[pl.BlockSpec((5, HELD, LANES), lambda g: (0, 0, 0))] * OWNERS,
-        out_specs=[pl.BlockSpec((OWNERS, 3, HELD, LANES), lambda g: (0, 0, 0, 0))] * 2,
-        compiler_params=params(8),
+        out_shape=[shape(size, LANES)] * 2,
+        in_specs=[pl.BlockSpec((5, HELD, LANES), lambda g: (0, 0, 0))] * OWNERS
+        + [pl.BlockSpec((ROWS, OWNERS * LANES), lambda g: (0, 0))] * 3,
+        out_specs=[pl.BlockSpec((size, LANES), lambda g: (0, 0))] * 2,
+        compiler_params=params(6),
         name="borders",
-    )(*pieces)
+    )(*pieces, *fields)
 
 
 def gram_kernel(place_ref, same_ref, other_ref, value_ref, scale_ref, out_ref):
@@ -201,9 +215,24 @@
         out_shape=shape(48, LANES),
         in_specs=[SCALARS] + whole(4),
         out_specs=whole(1)[0],
-        compiler_params=params(16),
+        compiler_params=params(8),
         name="gram",
     )(place, same, other, value, scale)
+
+
+def thirds(array):
+    high = array.astype(jnp.bfloat16)
+    rest = array - high.astype(F32)
+    middle = rest.astype(jnp.bfloat16)
+    return high, middle, (rest - middle.astype(F32)).astype(jnp.bfloat16)
+
+
+def six_products(a, b):
+    def product(i, j):
+        return jnp.dot(a[i], b[j], preferred_element_type=F32)
+
+    small = product(0, 2) + product(2, 0) + product(1, 1)
+    return (small + (product(0, 1) + product(1, 0))) + product(0, 0)
 
 
 def root_kernel(place_ref, parts_ref, out_ref, half_ref):
@@ -231,14 +260,18 @@
     norm = jnp.sqrt(jnp.sum(big * big))
     upper = big / norm
     middle = 1.5 * identity - 0.5 * upper
-    upper = dot(upper, middle)
+    middle_parts = thirds(middle)
+    upper = six_products(thirds(upper), middle_parts)
     lower = middle
+    lower_parts = middle_parts
     for _ in range(NS_ITERS - 2):
-        middle = 1.5 * identity - 0.5 * dot(lower, upper)
-        upper = dot(upper, middle)
-        lower = dot(middle, lower)
-    middle = 1.5 * identity - 0.5 * dot(lower, upper)
-    root = dot(middle, lower) / jnp.sqrt(norm)
+        upper_parts = thirds(upper)
+        middle_parts = thirds(1.5 * identity - 0.5 * six_products(lower_parts, upper_parts))
+        upper = six_products(upper_parts, middle_parts)
+        lower = six_products(middle_parts, lower_parts)
+        lower_parts = thirds(lower)
+    middle = 1.5 * identity - 0.5 * six_products(lower_parts, thirds(upper))
+    root = six_products(thirds(middle), lower_parts) / jnp.sqrt(norm)
     weights = dot(dot(drive_row, root, ((1,), (1,))), root, ((1,), (1,)))
     out_ref[...] = root + weights[0:1] / jnp.sqrt(F32(MEMBERS - 1))
 
@@ -250,7 +283,8 @@
         in_specs=[SCALARS] + whole(1),
         out_specs=whole(1)[0],
         scratch_shapes=[pltpu.VMEM((MEMBERS, MEMBERS), F32)],
-        compiler_params=params(16),
+        compiler_params=params(12),
+        cost_estimate=pl.CostEstimate(flops=10**10, bytes_accessed=10**6, transcendentals=0),
         name="root",
     )(place, parts)
 
@@ -274,15 +308,18 @@
     def joined(find):
         return jnp.concatenate([find(i) for i in range(OWNERS)], axis=0)
 
+    def border(ref, n):
+        return joined(lambda i: ref[(i * 3 + n) * HELD : (i * 3 + n + 1) * HELD])
+
     def cells(unit):
         if unit > SENT_ROWS + 1:
-            return joined(lambda i: below_ref[i, unit - SENT_ROWS - 2])
+            return border(below_ref, unit - SENT_ROWS - 2)
         if unit >= SENT_ROWS:
-            return joined(lambda i: above_ref[i, unit - SENT_ROWS + 1])
+            return border(above_ref, unit - SENT_ROWS + 1)
         found = joined(lambda i: piece_refs[i][PLACE[unit]])
         if unit == EDGE:
-            top = joined(lambda i: above_ref[i, 0])
-            bottom = joined(lambda i: below_ref[i, 2])
+            top = border(above_ref, 0)
+            bottom = border(below_ref, 2)
             first = (lane < 2) | ((lane >= OWN) & (lane < OWN + 2))
             last = 2 * ROWS + 2
             final = ((lane >= last) & (lane < last + 2)) | (
@@ -315,7 +352,7 @@
         out_shape=[shape(UNITS, HELD, LANES)] * OWNERS,
         in_specs=whole(3 + OWNERS),
         out_specs=whole(OWNERS),
-        compiler_params=params(24),
+        compiler_params=params(14),
         name="analyse",
     )(transform, *pieces, above, below)
 
@@ -328,9 +365,8 @@
     own = place_ref[0]
     lane = lane_ids(1)
     even = lane % 2 == 0
-    start = pl.multiple_of(own * LANES, LANES)
-    left_start = pl.multiple_of(jnp.maximum(own - 1, 0) * LANES, LANES)
-    right_start = pl.multiple_of(jnp.minimum(own + 1, OWNERS - 1) * LANES, LANES)
+    left_block = jnp.maximum(own - 1, 0)
+    right_block = jnp.minimum(own + 1, OWNERS - 1)
     has_left = own > 0
     has_right = own < OWNERS - 1
     packed = [jnp.zeros((1, LANES), F32) for _ in range(5)]
@@ -338,14 +374,15 @@
         for place in range(FIELD_ROWS):
             r = place - 2
 
-            def row_of(first):
+            def row_of(block):
+                line = (which * OWNERS + block) * 2
                 if r < 0:
-                    return above_ref[which, r + 2 : r + 3, pl.ds(first, LANES)]
+                    return above_ref[pl.ds(line + r + 2, 1)]
                 if r >= ROWS:
-                    return below_ref[which, r - ROWS : r - ROWS + 1, pl.ds(first, LANES)]
-                return ref[r : r + 1, pl.ds(first, LANES)]
-
-            mine = row_of(start)
+                    return below_ref[pl.ds(line + r - ROWS, 1)]
+                return ref[r : r + 1, pl.ds(pl.multiple_of(block * LANES, LANES), LANES)]
+
+            mine = row_of(own)
             out_ref[which, place] = jnp.broadcast_to(mine, (8, LANES))
             if r < -1 or r > ROWS:
                 if which == 0:
@@ -354,8 +391,8 @@
                 continue
             at = 2 * (r + 1)
             here = (lane == at) | (lane == at + 1)
-            left = jnp.where(has_left, row_of(left_start), 0.0)
-            right = jnp.where(has_right, row_of(right_start), 0.0)
+            left = jnp.where(has_left, row_of(left_block), 0.0)
+            right = jnp.where(has_right, row_of(right_block), 0.0)
             near = jnp.where(lane < LANES // 2, right, left)
             near = turned(near, at + 1)
             if which == 0:
@@ -379,12 +416,18 @@
 
 
 def block_fields(place, ksat, storage, recharge, above, below):
+    last = pl.BlockSpec((FIELD_LINES, LANES), lambda g: (BORDER // FIELD_LINES, 0))
+    mine = pl.BlockSpec((ROWS, OWNERS * LANES), lambda g: (0, 0))
     return pl.pallas_call(
         field_kernel,
+        grid=(1,),
         out_shape=[shape(5, FIELD_ROWS, 8, LANES), shape(6, 8, LANES)],
-        in_specs=[SCALARS] + whole(5),
-        out_specs=whole(2),
-        compiler_params=params(8),
+        in_specs=[SCALARS] + [mine] * 3 + [last] * 2,
+        out_specs=[
+            pl.BlockSpec((5, FIELD_ROWS, 8, LANES), lambda g: (0, 0, 0, 0)),
+            pl.BlockSpec((6, 8, LANES), lambda g: (0, 0, 0)),
+        ],
+        compiler_params=params(6),
         name="fields",
     )(place, ksat, storage, recharge, above, below)
 
@@ -396,11 +439,12 @@
 BATCH = 16
 
 
-def forecast_kernel(shift, place_ref, counts_ref, wide_ref, field_ref, edge_field_ref, cells_ref, out_ref, iterate, goal, edge_row):
+def forecast_kernel(shifts, place_ref, counts_ref, wide_ref, field_ref, edge_field_ref, *refs):
+    cells_refs, out_refs = refs[: len(shifts)], refs[len(shifts) : 2 * len(shifts)]
+    iterate, goal, edge_row = refs[2 * len(shifts) :]
     own = place_ref[0]
     has_above = place_ref[1].astype(F32)
     has_below = place_ref[2].astype(F32)
-    owner = lax.rem(own + shift, OWNERS)
     lane = lane_ids()
     even = lane % 2 == 0
     first_lane = lane == 0
@@ -417,7 +461,9 @@
     def swapped(packed):
         return jnp.where(even, rolled(packed, -1), rolled(packed, 1))
 
-    def one_batch(batch, carry):
+    def one_batch(which, batch, carry):
+        cells_ref, out_ref = cells_refs[which], out_refs[which]
+        owner = lax.rem(own + shifts[which], OWNERS)
         first_member = owner * HELD + batch * BATCH
         most = counts_ref[first_member]
         for n in range(1, BATCH):
@@ -525,23 +571,26 @@
                 out_ref[pl.ds(start, 8, stride=ROWS), :] = iterate[r + 1, tile]
         return carry
 
-    lax.fori_loop(0, HELD // BATCH, one_batch, 0)
-
-
-def forecast_of(shift, place, counts, wide_counts, fields, edge_fields, cells):
-    return pl.pallas_call(
-        functools.partial(forecast_kernel, shift),
-        out_shape=shape(HELD * ROWS, LANES),
-        in_specs=[SCALARS, SCALARS] + whole(4),
-        out_specs=whole(1)[0],
+    for which in range(len(shifts)):
+        lax.fori_loop(0, HELD // BATCH, functools.partial(one_batch, which), 0)
+
+
+def forecasts(shifts, place, counts, wide_counts, fields, edge_fields, cells):
+    many = len(shifts)
+    return pl.pallas_call(
+        functools.partial(forecast_kernel, shifts),
+        out_shape=[shape(HELD * ROWS, LANES)] * many,
+        in_specs=[SCALARS, SCALARS] + whole(3 + many),
+        out_specs=whole(many),
         scratch_shapes=[
             pltpu.VMEM((ROWS + 2, BATCH // 8, 8, LANES), F32),
             pltpu.VMEM((ROWS + 2, BATCH // 8, 8, LANES), F32),
             pltpu.VMEM((2, BATCH // 8, 8, LANES), F32),
         ],
-        compiler_params=params(8),
+        compiler_params=params(6),
+        cost_estimate=pl.CostEstimate(flops=1, bytes_accessed=1, transcendentals=0),
         name="forecast",
-    )(place, counts, wide_counts, fields, edge_fields, cells)
+    )(place, counts, wide_counts, fields, edge_fields, *cells)
 
 
 def unpack_kernel(place_ref, *refs):
@@ -596,15 +645,9 @@
     seen = observed(flat, obs_index[None])
     same = shared(seen, MEMBER[0])
 
-    cell_fields, _ = lax.optimization_barrier((jnp.stack([ksat, storage, recharge]), seen))
-    fields_above = to_strips_beside(cell_fields[:, -2:], 1)
-    fields_below = to_strips_beside(cell_fields[:, :2], -1)
     blocks = packed_blocks(place, flat, seen)
-    fields, edge_fields = block_fields(place, ksat, storage, recharge, fields_above, fields_below)
     wide_counts = jnp.broadcast_to(newton_counts[:, None], (MEMBERS, LANES))
-    same, blocks, fields, edge_fields, wide_counts = lax.optimization_barrier(
-        (same, blocks, fields, edge_fields, wide_counts)
-    )
+    same, blocks, wide_counts = lax.optimization_barrier((same, blocks, wide_counts))
     other = along(same, MEMBER[1], 1)
 
     pieces = [blocks[0]] + [None] * (OWNERS - 1)
@@ -617,16 +660,23 @@
     part = jnp.sum(shared(part, SPACE[0]), axis=0)
     part = jnp.sum(shared(part, SPACE[1]), axis=0)
     part, pieces = lax.optimization_barrier((part, pieces))
-    down, up = borders(pieces)
+    parts = shared(part, MEMBER)
+    down, up = borders(pieces, (ksat, storage, recharge))
+    parts, down, up = lax.optimization_barrier((parts, down, up))
     above = to_strips_beside(up, 1)
     below = to_strips_beside(down, -1)
-    transform = transform_of(place, shared(part, MEMBER))
+    transform = transform_of(place, parts)
+    fields, edge_fields = block_fields(place, ksat, storage, recharge, above, below)
     cells = analysed(transform, pieces, above, below)
 
     arrived = [None] * OWNERS
-    for i in (2, 6, 3, 5, 4, 1, 7, 0):
-        moved = forecast_of(i, place, newton_counts, wide_counts, fields, edge_fields, cells[i])
-        arrived[i] = along(moved, MEMBER, i) if i else moved
+    for shifts in ((2,), (6,), (3, 5), (4, 1), (7, 0)):
+        moved = forecasts(
+            shifts, place, newton_counts, wide_counts, fields, edge_fields, [cells[i] for i in shifts]
+        )
+        moved, cells = lax.optimization_barrier((moved, cells))
+        for i, field in zip(shifts, moved):
+            arrived[i] = along(field, MEMBER, i) if i else field
     return unpacked(place, arrived).reshape(members, rows, columns)
 
 

time: 148 us -> 134 us (0.905); the launches traced: 145 us -> 134 us
  blocking collectives: 18.4 us -> 8.76 us
  local copies, waits for them, and re-layouts: 5.57 us -> 9.66 us
  starting transfers between devices: 47.6 us -> 43.9 us
  Pallas kernels: 47.9 us -> 45.9 us
    all_to_all x2 -> x1, blocking collectives: 18.4 us -> 8.76 us  [shared(): return lax.all_to_all(copies, axis, split_axis=0, concat_axis=0, tiled=True)]
    all_to_all x2 -> x3, waiting for transfers between devices: 1.02 us -> 7.93 us  [shared(): return lax.all_to_all(copies, axis, split_axis=0, concat_axis=0, tiled=True)]
    ppermute x15, waiting for transfers between devices: 23.5 us -> 17.3 us  [along(): lax.ppermute(array, axis, [(i, (i + step) % peers) for i in range(peers)])]
    ppermute x4 -> x2, starting transfers between devices: 13.2 us -> 7.56 us  [to_strips_beside(): return lax.ppermute(array, SPACE, pairs)]
    unnamed x32, local copies, waits for them, and re-layouts: 3.89 us -> 7.33 us
    all_to_all x2 -> x3, starting transfers between devices: 13.6 us -> 15.9 us  [shared(): return lax.all_to_all(copies, axis, split_axis=0, concat_axis=0, tiled=True)]
    pallas_call x10 -> x7, Pallas kernels: 22.3 us -> 20.7 us  [the longest x5 19.8 us: forecasts(): pl.pallas_call(functools.partial(forecast_kernel, shifts), out_shape=[sha...]
  transfers between devices with their start and end apart: 21 -> 20, of which waited for: 8 -> 8; matrix products, arithmetic and copies ran while one was open for 1% -> 1% of each run, Pallas kernels for 25% -> 24%
where the time goes in v2:
time: 134 us
  Pallas kernels  45.9 us (34%)
  starting transfers between devices  43.9 us (33%)
  waiting for transfers between devices  25.2 us (19%)
  local copies, waits for them, and re-layouts  9.66 us (7%)
  blocking collectives  8.76 us (7%)
    ppermute x15, starting transfers between devices, along(): lax.ppermute(array, axis, [(i, (i + step) % peers) for i in range(peers)])  20.5 us
    pallas_call x5, Pallas kernels, forecasts(): pl.pallas_call(functools.partial(forecast_kernel, shifts), out_shape=[sha...  19.8 us
    ppermute x15, waiting for transfers between devices, along(): lax.ppermute(array, axis, [(i, (i + step) % peers) for i in range(peers)])  17.3 us
    all_to_all x3, starting transfers between devices, shared(): return lax.all_to_all(copies, axis, split_axis=0, concat_axis=0, tiled=True)  15.9 us
    pallas_call x1, Pallas kernels, transform_of(): pl.pallas_call(root_kernel, out_shape=shape(MEMBERS, MEMBERS), in_specs=[...  13.9 us
    all_to_all x1, blocking collectives, shared(): return lax.all_to_all(copies, axis, split_axis=0, concat_axis=0, tiled=True)  8.76 us
    all_to_all x3, waiting for transfers between devices, shared(): return lax.all_to_all(copies, axis, split_axis=0, concat_axis=0, tiled=True)  7.93 us
    ppermute x2, starting transfers between devices, to_strips_beside(): return lax.ppermute(array, SPACE, pairs)  7.56 us
  transfers between devices with their start and end apart: 20, of which 8 were waited for; matrix products, arithmetic and copies ran while one was open for 1% of the time, Pallas kernels for 24%

profile of v2, /device:TPU:33, one launch (start us, length us, event | category | flops | bytes accessed | tf_op | source)
XLA Modules:
  0.0 133.8 jit_solution(7404771764675098027)
XLA Ops:
  2.3 3.7 %observe.1.after_ref = f32[32,1024]{1,0:T(8,128)S(1)} custom-call(s32[1,1024]{1,0:T(1,128)S(1)} %bitcast.10, f32[512,1024]{1,0:T(8,128)S(1)} %bitcast.8), custom_call_target="tpu_custom_call" | custom-call | tf_op jit(solution)/shard_map/observe/pallas_call | solution.py:81
  6.9 4.2 %all-to-all-start = ((f32[4,32,1024]{2,1,0:T(8,128)}), f32[4,32,1024]{2,1,0:T(8,128)S(1)}, u32[]{:S(2)}, u32[]{:S(2)}) async-start(f32[4,32,1024]{2,1,0:T(8,128)} %broadcast_in_dim.28), calls=%async_computation | async-start | bytes 1048576 | tf_op jit(solution)/shard_map/all_to_all | solution.py:622
  11.1 2.3 %pack.1 = (f32[17,32,128]{2,1,0:T(8,128)S(1)}, f32[17,32,128]{2,1,0:T(8,128)S(1)}, f32[17,32,128]{2,1,0:T(8,128)S(1)}, f32[17,32,128]{2,1,0:T(8,128)S(1)}, f32[1...) custom-call(s32[3]{0:T(128)S(1)} %pad_add_fusion.place_ref, ...), custom_call_target="tpu_custom_call" | custom-call | tf_op jit(solution)/shard_map/pack/pallas_call | solution.py:146
  19.4 2.2 %collective-permute-start = (f32[4,32,1024]{2,1,0:T(8,128)S(1)}, f32[4,32,1024]{2,1,0:T(8,128)S(1)}, u32[]{:S(2)}, u32[]{:S(2)}) collective-permute-start(f32[4,32,1024]{2,1,0:T(8,128)S(1)} %all-to-all-done.same_ref), channel_id=1, source_target_pairs={{0,32},{32,0},{1,33},{33,1},{2,34},{34,2},{3,35},{35,3},{4,36},{36... | collective-permute-start | bytes 1572872 | tf_op jit(solution)/shard_map/ppermute | solution.py:627
  25.3 8.0 %all-to-all-start.1 = ((f32[8,48,128]{2,1,0:T(8,128)}), f32[8,48,128]{2,1,0:T(8,128)S(1)}, u32[]{:S(2)}, u32[]{:S(2)}) async-start(f32[8,48,128]{2,1,0:T(8,128)} %broadcast_in_dim.32), calls=%async_computation.1 | async-start | bytes 393216 | tf_op jit(solution)/shard_map/all_to_all | solution.py:622
  34.5 2.0 %collective-permute-start.3 = (f32[17,32,128]{2,1,0:T(8,128)}, f32[17,32,128]{2,1,0:T(8,128)S(1)}, u32[]{:S(2)}, u32[]{:S(2)}) collective-permute-start(f32[17,32,128]{2,1,0:T(8,128)} %copy-done.12), channel_id=1, source_target_pairs={{0,160},{32,192},{64,224},{96,0},{128,32},{160,64},{192,96},{224,1... | collective-permute-start | bytes 835592 | tf_op jit(solution)/shard_map/ppermute | solution.py:627
  36.9 2.1 %collective-permute-start.5 = (f32[17,32,128]{2,1,0:T(8,128)}, f32[17,32,128]{2,1,0:T(8,128)S(1)}, u32[]{:S(2)}, u32[]{:S(2)}) collective-permute-start(f32[17,32,128]{2,1,0:T(8,128)} %copy-done.10), channel_id=1, source_target_pairs={{0,96},{32,128},{64,160},{96,192},{128,224},{160,0},{192,32},{224,... | collective-permute-start | bytes 835592 | tf_op jit(solution)/shard_map/ppermute | solution.py:627
  40.7 8.8 %all_to_all.20 = f32[4,48,128]{2,1,0:T(8,128)S(1)} all-to-all(f32[4,48,128]{2,1,0:T(8,128)S(1)} %broadcast_in_dim.33), channel_id=1, replica_groups=mesh['member_0'=4,'member_1'=2,'space_0'=8,'space_1'=4] {'space_1'}, dimensions={0} | all-to-all | bytes 196608 | tf_op jit(solution)/shard_map/all_to_all | solution.py:622
  49.5 5.2 %collective-permute-done.3.refs_3_.refs_4_ = f32[17,32,128]{2,1,0:T(8,128)S(1)} collective-permute-done((f32[17,32,128]{2,1,0:T(8,128)}, f32[17,32,128]{2,1,0:T(8,128)S(1)}, u32[]{:S(2)}, u32[]{:S(2)}) %collective-permute-start.3) | collective-permute-done | bytes 278560 | tf_op jit(solution)/shard_map/ppermute | solution.py:627
  54.7 2.7 %collective-permute-done.5.refs_5_.refs_6_ = f32[17,32,128]{2,1,0:T(8,128)S(1)} collective-permute-done((f32[17,32,128]{2,1,0:T(8,128)}, f32[17,32,128]{2,1,0:T(8,128)S(1)}, u32[]{:S(2)}, u32[]{:S(2)}) %collective-permute-start.5) | collective-permute-done | bytes 278560 | tf_op jit(solution)/shard_map/ppermute | solution.py:627
  58.1 3.7 %all-to-all-start.3 = ((f32[8,48,128]{2,1,0:T(8,128)}), f32[8,48,128]{2,1,0:T(8,128)S(1)}, u32[]{:S(2)}, u32[]{:S(2)}) async-start(f32[8,48,128]{2,1,0:T(8,128)} %broadcast_in_dim.34), calls=%async_computation.3 | async-start | bytes 393216 | tf_op jit(solution)/shard_map/all_to_all | solution.py:622
  62.6 5.1 %all-to-all-done.3.parts_ref = f32[8,48,128]{2,1,0:T(8,128)S(1)} async-done(((f32[8,48,128]{2,1,0:T(8,128)}), f32[8,48,128]{2,1,0:T(8,128)S(1)}, u32[]{:S(2)}, u32[]{:S(2)}) %all-to-all-start.3) | async-done | bytes 196640 | tf_op jit(solution)/shard_map/all_to_all | solution.py:622
  67.7 3.1 %collective-permute-start.8 = (f32[816,128]{1,0:T(8,128)}, f32[816,128]{1,0:T(8,128)S(1)}, u32[]{:S(2)}, u32[]{:S(2)}) collective-permute-start(f32[816,128]{1,0:T(8,128)} %copy-done.9), channel_id=1, source_target_pairs={{0,1},{1,2},{2,3},{3,4},{4,5},{5,6},{6,7},{7,8},{8,9},{9,10},{10,1... | collective-permute-start | bytes 1253384 | tf_op jit(solution)/shard_map/ppermute | solution.py:633
  70.8 4.5 %collective-permute-start.9 = (f32[816,128]{1,0:T(8,128)S(1)}, f32[816,128]{1,0:T(8,128)S(1)}, u32[]{:S(2)}, u32[]{:S(2)}) collective-permute-start(f32[816,128]{1,0:T(8,128)S(1)} %get-tuple-element.122), channel_id=1, source_target_pairs={{1,0},{2,1},{3,2},{4,3},{5,4},{6,5},{7,6},{8,7},{9,8},{10,9},{11,1... | collective-permute-start | bytes 1253384 | tf_op jit(solution)/shard_map/ppermute | solution.py:633
  75.2 13.9 %root.1.refs_0_ = f32[256,256]{1,0:T(8,128)S(1)} custom-call(s32[3]{0:T(128)S(1)} %pad_add_fusion.place_ref, f32[8,48,128]{2,1,0:T(8,128)S(1)} %all-to-all-done.3.parts_ref), custom_call_target="tpu_custom_call" | custom-call | flops 10000000000 | bytes 1000000 | tf_op jit(solution)/shard_map/root/pallas_call | solution.py:280
  91.4 2.4 %forecast.5 = f32[512,128]{1,0:T(8,128)S(1)} custom-call(s32[3]{0:T(128)S(1)} %pad_add_fusion.place_ref, s32[256]{0:T(256)S(1)} %copy-done.5, s32[256,128]{1,0:T(8,128)S(1)} %broadcast_in_dim.29.wide_ref, f32[5,20,8,128]{3,2,1,0:T(8,128)S(1)} %get-tuple-element.123.field_ref, f32[6,8,128]{2,1,0:T(8,128)S(1)} %get-tuple-element.124.edge_field_ref, ...), custom_call_target="tpu_custom_call" | custom-call | flops 1 | bytes 1 | tf_op jit(solution)/shard_map/forecast/pallas_call | solution.py:580
  93.8 2.4 %forecast.6 = f32[512,128]{1,0:T(8,128)S(1)} custom-call(s32[3]{0:T(128)S(1)} %pad_add_fusion.place_ref, s32[256]{0:T(256)S(1)} %copy-done.5, s32[256,128]{1,0:T(8,128)S(1)} %broadcast_in_dim.29.wide_ref, f32[5,20,8,128]{3,2,1,0:T(8,128)S(1)} %get-tuple-element.123.field_ref, f32[6,8,128]{2,1,0:T(8,128)S(1)} %get-tuple-element.124.edge_field_ref, ...), custom_call_target="tpu_custom_call" | custom-call | flops 1 | bytes 1 | tf_op jit(solution)/shard_map/forecast/pallas_call | solution.py:580
  96.2 2.5 %collective-permute-start.15 = (f32[512,128]{1,0:T(8,128)S(1)}, f32[512,128]{1,0:T(8,128)S(1)}, u32[]{:S(2)}, u32[]{:S(2)}) collective-permute-start(f32[512,128]{1,0:T(8,128)S(1)} %forecast.6), channel_id=1, source_target_pairs={{0,192},{32,224},{64,0},{96,32},{128,64},{160,96},{192,128},{224,1... | collective-permute-start | bytes 786440 | tf_op jit(solution)/shard_map/ppermute | solution.py:627
  98.8 5.0 %forecast.7 = (f32[512,128]{1,0:T(8,128)S(1)}, f32[512,128]{1,0:T(8,128)S(1)}) custom-call(s32[3]{0:T(128)S(1)} %pad_add_fusion.place_ref, s32[256]{0:T(256)S(1)} %copy-done.5, s32[256,128]{1,0:T(8,128)S(1)} %broadcast_in_dim.29.wide_ref, f32[5,20,8,128]{3,2,1,0:T(8,128)S(1)} %get-tuple-element.123.field_ref, ...), custom_call_target="tpu_custom_call" | custom-call | flops 1 | bytes 1 | tf_op jit(solution)/shard_map/forecast/pallas_call | solution.py:580
  106.8 5.8 %forecast.8 = (f32[512,128]{1,0:T(8,128)S(1)}, f32[512,128]{1,0:T(8,128)S(1)}) custom-call(s32[3]{0:T(128)S(1)} %pad_add_fusion.place_ref, s32[256]{0:T(256)S(1)} %copy-done.5, s32[256,128]{1,0:T(8,128)S(1)} %broadcast_in_dim.29.wide_ref, f32[5,20,8,128]{3,2,1,0:T(8,128)S(1)} %get-tuple-element.123.field_ref, ...), custom_call_target="tpu_custom_call" | custom-call | flops 1 | bytes 1 | tf_op jit(solution)/shard_map/forecast/pallas_call | solution.py:580
  112.6 4.2 %forecast.9 = (f32[512,128]{1,0:T(8,128)S(1)}, f32[512,128]{1,0:T(8,128)S(1)}) custom-call(s32[3]{0:T(128)S(1)} %pad_add_fusion.place_ref, s32[256]{0:T(256)S(1)} %copy-done.5, s32[256,128]{1,0:T(8,128)S(1)} %broadcast_in_dim.29.wide_ref, f32[5,20,8,128]{3,2,1,0:T(8,128)S(1)} %get-tuple-element.123.field_ref, ...), custom_call_target="tpu_custom_call" | custom-call | flops 1 | bytes 1 | tf_op jit(solution)/shard_map/forecast/pallas_call | solution.py:580
  118.7 3.3 %collective-permute-start.13 = (f32[512,128]{1,0:T(8,128)S(1)}, f32[512,128]{1,0:T(8,128)S(1)}, u32[]{:S(2)}, u32[]{:S(2)}) collective-permute-start(f32[512,128]{1,0:T(8,128)S(1)} %get-tuple-element.163), channel_id=1, source_target_pairs={{0,128},{32,160},{64,192},{96,224},{128,0},{160,32},{192,64},{224,... | collective-permute-start | bytes 786440 | tf_op jit(solution)/shard_map/ppermute | solution.py:627
  123.3 8.1 %collective-permute-done.13.refs_4_ = f32[512,128]{1,0:T(8,128)S(1)} collective-permute-done((f32[512,128]{1,0:T(8,128)S(1)}, f32[512,128]{1,0:T(8,128)S(1)}, u32[]{:S(2)}, u32[]{:S(2)}) %collective-permute-start.13) | collective-permute-done | bytes 262176 | tf_op jit(solution)/shard_map/ppermute | solution.py:627
  131.4 2.5 %unpack.1 = f32[512,1024]{1,0:T(8,128)} custom-call(s32[3]{0:T(128)S(1)} %pad_add_fusion.place_ref, f32[512,128]{1,0:T(8,128)S(1)} %get-tuple-element.159.refs_0_, f32[512,128]{1,0:T(8,128)S(1)} %collective-permute-done.10.refs_1_, f32[512,128]{1,0:T(8,128)S(1)} %collective-permute-done.11.refs_2_, f32[512,128]{1,0:T(8,128)S(1)} %collective-permute-done.12.refs_3_, ...), custom_call_target="tpu_custom_call" | custom-call | tf_op jit(solution)/shard_map/unpack/pallas_call | solution.py:608
  (70 shorter events, 26.1 us)
Async XLA Ops:
  6.0 17.2 %copy-start.7 = (f32[1024]{0:T(1024)S(1)}, f32[1024]{0:T(1024)}, u32[]{:S(2)}) copy-start(f32[1024]{0:T(1024)} %param.10) | copy-start | bytes 12292
  6.9 12.5 %all-to-all-start = ((f32[4,32,1024]{2,1,0:T(8,128)}), f32[4,32,1024]{2,1,0:T(8,128)S(1)}, u32[]{:S(2)}, u32[]{:S(2)}) async-start(f32[4,32,1024]{2,1,0:T(8,128)} %broadcast_in_dim.28), calls=%async_computation | async-start | bytes 1048576 | tf_op jit(solution)/shard_map/all_to_all | solution.py:622
  17.7 44.0 %copy-start.2 = (f32[16,1024]{1,0:T(8,128)S(1)}, f32[16,1024]{1,0:T(8,128)}, u32[]{:S(2)}) copy-start(f32[16,1024]{1,0:T(8,128)} %ksat_ref.1) | copy-start | bytes 196612
  17.7 44.0 %copy-start.3 = (f32[16,1024]{1,0:T(8,128)S(1)}, f32[16,1024]{1,0:T(8,128)}, u32[]{:S(2)}) copy-start(f32[16,1024]{1,0:T(8,128)} %storage_ref.1) | copy-start | bytes 196612
  17.7 44.0 %copy-start.4 = (f32[16,1024]{1,0:T(8,128)S(1)}, f32[16,1024]{1,0:T(8,128)}, u32[]{:S(2)}) copy-start(f32[16,1024]{1,0:T(8,128)} %recharge_ref.1) | copy-start | bytes 196612
  19.4 3.8 %collective-permute-start = (f32[4,32,1024]{2,1,0:T(8,128)S(1)}, f32[4,32,1024]{2,1,0:T(8,128)S(1)}, u32[]{:S(2)}, u32[]{:S(2)}) collective-permute-start(f32[4,32,1024]{2,1,0:T(8,128)S(1)} %all-to-all-done.same_ref), channel_id=1, source_target_pairs={{0,32},{32,0},{1,33},{33,1},{2,34},{34,2},{3,35},{35,3},{4,36},{36... | collective-permute-start | bytes 1572872 | tf_op jit(solution)/shard_map/ppermute | solution.py:627
  21.7 15.2 %collective-permute-start.2 = (f32[17,32,128]{2,1,0:T(8,128)}, f32[17,32,128]{2,1,0:T(8,128)S(1)}, u32[]{:S(2)}, u32[]{:S(2)}) collective-permute-start(f32[17,32,128]{2,1,0:T(8,128)} %copy-done.15), channel_id=1, source_target_pairs={{0,192},{32,224},{64,0},{96,32},{128,64},{160,96},{192,128},{224,1... | collective-permute-start | bytes 835592 | tf_op jit(solution)/shard_map/ppermute | solution.py:627
  22.6 16.3 %collective-permute-start.6 = (f32[17,32,128]{2,1,0:T(8,128)}, f32[17,32,128]{2,1,0:T(8,128)S(1)}, u32[]{:S(2)}, u32[]{:S(2)}) collective-permute-start(f32[17,32,128]{2,1,0:T(8,128)} %copy-done.14), channel_id=1, source_target_pairs={{0,64},{32,96},{64,128},{96,160},{128,192},{160,224},{192,0},{224,... | collective-permute-start | bytes 835592 | tf_op jit(solution)/shard_map/ppermute | solution.py:627
  25.3 15.4 %all-to-all-start.1 = ((f32[8,48,128]{2,1,0:T(8,128)}), f32[8,48,128]{2,1,0:T(8,128)S(1)}, u32[]{:S(2)}, u32[]{:S(2)}) async-start(f32[8,48,128]{2,1,0:T(8,128)} %broadcast_in_dim.32), calls=%async_computation.1 | async-start | bytes 393216 | tf_op jit(solution)/shard_map/all_to_all | solution.py:622
  33.3 16.2 %collective-permute-start.1 = (f32[17,32,128]{2,1,0:T(8,128)}, f32[17,32,128]{2,1,0:T(8,128)S(1)}, u32[]{:S(2)}, u32[]{:S(2)}) collective-permute-start(f32[17,32,128]{2,1,0:T(8,128)} %copy-done.13), channel_id=1, source_target_pairs={{0,224},{32,0},{64,32},{96,64},{128,96},{160,128},{192,160},{224,1... | collective-permute-start | bytes 835592 | tf_op jit(solution)/shard_map/ppermute | solution.py:627
  34.5 20.2 %collective-permute-start.3 = (f32[17,32,128]{2,1,0:T(8,128)}, f32[17,32,128]{2,1,0:T(8,128)S(1)}, u32[]{:S(2)}, u32[]{:S(2)}) collective-permute-start(f32[17,32,128]{2,1,0:T(8,128)} %copy-done.12), channel_id=1, source_target_pairs={{0,160},{32,192},{64,224},{96,0},{128,32},{160,64},{192,96},{224,1... | collective-permute-start | bytes 835592 | tf_op jit(solution)/shard_map/ppermute | solution.py:627
  36.5 18.3 %collective-permute-start.4 = (f32[17,32,128]{2,1,0:T(8,128)}, f32[17,32,128]{2,1,0:T(8,128)S(1)}, u32[]{:S(2)}, u32[]{:S(2)}) collective-permute-start(f32[17,32,128]{2,1,0:T(8,128)} %copy-done.11), channel_id=1, source_target_pairs={{0,128},{32,160},{64,192},{96,224},{128,0},{160,32},{192,64},{224,... | collective-permute-start | bytes 835592 | tf_op jit(solution)/shard_map/ppermute | solution.py:627
  36.9 20.5 %collective-permute-start.5 = (f32[17,32,128]{2,1,0:T(8,128)}, f32[17,32,128]{2,1,0:T(8,128)S(1)}, u32[]{:S(2)}, u32[]{:S(2)}) collective-permute-start(f32[17,32,128]{2,1,0:T(8,128)} %copy-done.10), channel_id=1, source_target_pairs={{0,96},{32,128},{64,160},{96,192},{128,224},{160,0},{192,32},{224,... | collective-permute-start | bytes 835592 | tf_op jit(solution)/shard_map/ppermute | solution.py:627
  38.9 18.5 %collective-permute-start.7 = (f32[17,32,128]{2,1,0:T(8,128)S(1)}, f32[17,32,128]{2,1,0:T(8,128)S(1)}, u32[]{:S(2)}, u32[]{:S(2)}) collective-permute-start(f32[17,32,128]{2,1,0:T(8,128)S(1)} %get-tuple-element.109), channel_id=1, source_target_pairs={{0,32},{32,64},{64,96},{96,128},{128,160},{160,192},{192,224},{224... | collective-permute-start | bytes 835592 | tf_op jit(solution)/shard_map/ppermute | solution.py:627
  58.1 9.6 %all-to-all-start.3 = ((f32[8,48,128]{2,1,0:T(8,128)}), f32[8,48,128]{2,1,0:T(8,128)S(1)}, u32[]{:S(2)}, u32[]{:S(2)}) async-start(f32[8,48,128]{2,1,0:T(8,128)} %broadcast_in_dim.34), calls=%async_computation.3 | async-start | bytes 393216 | tf_op jit(solution)/shard_map/all_to_all | solution.py:622
  67.7 21.5 %collective-permute-start.8 = (f32[816,128]{1,0:T(8,128)}, f32[816,128]{1,0:T(8,128)S(1)}, u32[]{:S(2)}, u32[]{:S(2)}) collective-permute-start(f32[816,128]{1,0:T(8,128)} %copy-done.9), channel_id=1, source_target_pairs={{0,1},{1,2},{2,3},{3,4},{4,5},{5,6},{6,7},{7,8},{8,9},{9,10},{10,1... | collective-permute-start | bytes 1253384 | tf_op jit(solution)/shard_map/ppermute | solution.py:633
  70.8 18.4 %collective-permute-start.9 = (f32[816,128]{1,0:T(8,128)S(1)}, f32[816,128]{1,0:T(8,128)S(1)}, u32[]{:S(2)}, u32[]{:S(2)}) collective-permute-start(f32[816,128]{1,0:T(8,128)S(1)} %get-tuple-element.122), channel_id=1, source_target_pairs={{1,0},{2,1},{3,2},{4,3},{5,4},{6,5},{7,6},{8,7},{9,8},{10,9},{11,1... | collective-permute-start | bytes 1253384 | tf_op jit(solution)/shard_map/ppermute | solution.py:633
  96.2 22.0 %collective-permute-start.15 = (f32[512,128]{1,0:T(8,128)S(1)}, f32[512,128]{1,0:T(8,128)S(1)}, u32[]{:S(2)}, u32[]{:S(2)}) collective-permute-start(f32[512,128]{1,0:T(8,128)S(1)} %forecast.6), channel_id=1, source_target_pairs={{0,192},{32,224},{64,0},{96,32},{128,64},{160,96},{192,128},{224,1... | collective-permute-start | bytes 786440 | tf_op jit(solution)/shard_map/ppermute | solution.py:627
  98.7 19.9 %collective-permute-start.11 = (f32[512,128]{1,0:T(8,128)S(1)}, f32[512,128]{1,0:T(8,128)S(1)}, u32[]{:S(2)}, u32[]{:S(2)}) collective-permute-start(f32[512,128]{1,0:T(8,128)S(1)} %forecast.5), channel_id=1, source_target_pairs={{0,64},{32,96},{64,128},{96,160},{128,192},{160,224},{192,0},{224,... | collective-permute-start | bytes 786440 | tf_op jit(solution)/shard_map/ppermute | solution.py:627
  103.8 18.2 %collective-permute-start.12 = (f32[512,128]{1,0:T(8,128)S(1)}, f32[512,128]{1,0:T(8,128)S(1)}, u32[]{:S(2)}, u32[]{:S(2)}) collective-permute-start(f32[512,128]{1,0:T(8,128)S(1)} %get-tuple-element.162), channel_id=1, source_target_pairs={{0,96},{32,128},{64,160},{96,192},{128,224},{160,0},{192,32},{224,... | collective-permute-start | bytes 786440 | tf_op jit(solution)/shard_map/ppermute | solution.py:627
  105.1 16.9 %collective-permute-start.14 = (f32[512,128]{1,0:T(8,128)S(1)}, f32[512,128]{1,0:T(8,128)S(1)}, u32[]{:S(2)}, u32[]{:S(2)}) collective-permute-start(f32[512,128]{1,0:T(8,128)S(1)} %get-tuple-element.164), channel_id=1, source_target_pairs={{0,160},{32,192},{64,224},{96,0},{128,32},{160,64},{192,96},{224,1... | collective-permute-start | bytes 786440 | tf_op jit(solution)/shard_map/ppermute | solution.py:627
  116.9 6.4 %collective-permute-start.16 = (f32[512,128]{1,0:T(8,128)S(1)}, f32[512,128]{1,0:T(8,128)S(1)}, u32[]{:S(2)}, u32[]{:S(2)}) collective-permute-start(f32[512,128]{1,0:T(8,128)S(1)} %get-tuple-element.166), channel_id=1, source_target_pairs={{0,224},{32,0},{64,32},{96,64},{128,96},{160,128},{192,160},{224,1... | collective-permute-start | bytes 786440 | tf_op jit(solution)/shard_map/ppermute | solution.py:627
  118.2 5.0 %collective-permute-start.10 = (f32[512,128]{1,0:T(8,128)S(1)}, f32[512,128]{1,0:T(8,128)S(1)}, u32[]{:S(2)}, u32[]{:S(2)}) collective-permute-start(f32[512,128]{1,0:T(8,128)S(1)} %get-tuple-element.160), channel_id=1, source_target_pairs={{0,32},{32,64},{64,96},{96,128},{128,160},{160,192},{192,224},{224... | collective-permute-start | bytes 786440 | tf_op jit(solution)/shard_map/ppermute | solution.py:627
  118.7 12.7 %collective-permute-start.13 = (f32[512,128]{1,0:T(8,128)S(1)}, f32[512,128]{1,0:T(8,128)S(1)}, u32[]{:S(2)}, u32[]{:S(2)}) collective-permute-start(f32[512,128]{1,0:T(8,128)S(1)} %get-tuple-element.163), channel_id=1, source_target_pairs={{0,128},{32,160},{64,192},{96,224},{128,0},{160,32},{192,64},{224,... | collective-permute-start | bytes 786440 | tf_op jit(solution)/shard_map/ppermute | solution.py:627
  (12 other events, 46.7 us)

commit v3 on v2

--- a/solution.py
+++ b/solution.py
@@ -72,15 +72,15 @@
         picked += jnp.dot(high, chosen, preferred_element_type=F32)
         picked = picked.reshape(HELD, ROWS, step)
         rows = lax.broadcasted_iota(jnp.int32, (ROWS, step), 0)
-        seen_ref[:, first : first + step] = jnp.sum(
-            jnp.where((rows == row)[None], picked, 0.0), axis=1
-        )
-
-
-def observed(state, obs_index):
+        seen = jnp.sum(jnp.where((rows == row)[None], picked, 0.0), axis=1)
+        for copy in range(seen_ref.shape[0]):
+            seen_ref[copy, :, first : first + step] = seen
+
+
+def observed(state, obs_index, copies):
     return pl.pallas_call(
         observe_kernel,
-        out_shape=shape(HELD, obs_index.shape[1]),
+        out_shape=shape(copies, HELD, obs_index.shape[1]),
         in_specs=whole(2),
         out_specs=whole(1)[0],
         compiler_params=params(20),
@@ -200,22 +200,25 @@
         blocks.append((block - mean) * weight)
     innovation = scale * (value_ref[...] - mean)
     left = jnp.concatenate([blocks[0], jnp.broadcast_to(innovation, (8, mean.shape[1]))], axis=0)
-    out_ref[0:40] = dot(left, jnp.concatenate(blocks[:4], axis=0), ((1,), (1,)))
+    main = dot(left, jnp.concatenate(blocks[:4], axis=0), ((1,), (1,)))
     last = jnp.concatenate([blocks[4], jnp.zeros((96, mean.shape[1]), F32)], axis=0)
     opposite = dot(blocks[0], last, ((1,), (1,)))
     packed = opposite[0:8]
     for g in range(1, 4):
         packed += turned(opposite[8 * g : 8 * g + 8], HELD * g)
-    out_ref[40:48] = packed
-
-
-def gram_blocks(place, same, other, value, scale):
+    for copy in range(out_ref.shape[0]):
+        out_ref[copy, 0:40] = main
+        out_ref[copy, 40:48] = packed
+
+
+def gram_blocks(place, same, other, value, scale, copies):
     return pl.pallas_call(
         gram_kernel,
-        out_shape=shape(48, LANES),
+        out_shape=shape(copies, 48, LANES),
         in_specs=[SCALARS] + whole(4),
         out_specs=whole(1)[0],
         compiler_params=params(8),
+        cost_estimate=pl.CostEstimate(flops=10**10, bytes_accessed=10**6, transcendentals=0),
         name="gram",
     )(place, same, other, value, scale)
 
@@ -233,6 +236,13 @@
 
     small = product(0, 2) + product(2, 0) + product(1, 1)
     return (small + (product(0, 1) + product(1, 0))) + product(0, 0)
+
+
+def three_products(a, b):
+    def product(i, j):
+        return jnp.dot(a[i], b[j], preferred_element_type=F32)
+
+    return (product(0, 1) + product(1, 0)) + product(0, 0)
 
 
 def root_kernel(place_ref, parts_ref, out_ref, half_ref):
@@ -266,11 +276,11 @@
     lower_parts = middle_parts
     for _ in range(NS_ITERS - 2):
         upper_parts = thirds(upper)
-        middle_parts = thirds(1.5 * identity - 0.5 * six_products(lower_parts, upper_parts))
+        middle_parts = thirds(1.5 * identity - 0.5 * three_products(lower_parts, upper_parts))
         upper = six_products(upper_parts, middle_parts)
         lower = six_products(middle_parts, lower_parts)
         lower_parts = thirds(lower)
-    middle = 1.5 * identity - 0.5 * six_products(lower_parts, thirds(upper))
+    middle = 1.5 * identity - 0.5 * three_products(lower_parts, thirds(upper))
     root = six_products(thirds(middle), lower_parts) / jnp.sqrt(norm)
     weights = dot(dot(drive_row, root, ((1,), (1,))), root, ((1,), (1,)))
     out_ref[...] = root + weights[0:1] / jnp.sqrt(F32(MEMBERS - 1))
@@ -289,79 +299,11 @@
     )(place, parts)
 
 
-UNITS = ROWS + 5
-
-
-def halves(array):
-    high = array.astype(jnp.bfloat16)
-    return high, (array - high.astype(F32)).astype(jnp.bfloat16)
-
-
-def analyse_kernel(*refs):
-    transform_ref = refs[0]
-    piece_refs = refs[1 : 1 + OWNERS]
-    above_ref, below_ref = refs[1 + OWNERS : 3 + OWNERS]
-    out_refs = refs[3 + OWNERS :]
-    high, low = halves(transform_ref[...])
-    lane = lax.broadcasted_iota(jnp.int32, (MEMBERS, LANES), 1)
-
-    def joined(find):
-        return jnp.concatenate([find(i) for i in range(OWNERS)], axis=0)
-
-    def border(ref, n):
-        return joined(lambda i: ref[(i * 3 + n) * HELD : (i * 3 + n + 1) * HELD])
-
-    def cells(unit):
-        if unit > SENT_ROWS + 1:
-            return border(below_ref, unit - SENT_ROWS - 2)
-        if unit >= SENT_ROWS:
-            return border(above_ref, unit - SENT_ROWS + 1)
-        found = joined(lambda i: piece_refs[i][PLACE[unit]])
-        if unit == EDGE:
-            top = border(above_ref, 0)
-            bottom = border(below_ref, 2)
-            first = (lane < 2) | ((lane >= OWN) & (lane < OWN + 2))
-            last = 2 * ROWS + 2
-            final = ((lane >= last) & (lane < last + 2)) | (
-                (lane >= OWN + last) & (lane < OWN + last + 2)
-            )
-            found = jnp.where(first, turned(top, -2 * ROWS), found)
-            found = jnp.where(final, turned(bottom, 2 * ROWS), found)
-        return found
-
-    def product(a, b):
-        return jnp.dot(a, b, preferred_element_type=F32)
-
-    for first in range(0, UNITS, 2):
-        units = range(first, min(first + 2, UNITS))
-        found = [cells(u) for u in units]
-        state = found[0] if len(found) == 1 else jnp.concatenate(found, axis=1)
-        mean = jnp.sum(state, axis=0, keepdims=True) / MEMBERS
-        large, small = halves(state - mean)
-        result = product(low, large) + product(high, small) + product(high, large) + mean
-        for at, unit in enumerate(units):
-            for i in range(OWNERS):
-                out_refs[i][unit] = result[
-                    i * HELD : (i + 1) * HELD, at * LANES : (at + 1) * LANES
-                ]
-
-
-def analysed(transform, pieces, above, below):
-    return pl.pallas_call(
-        analyse_kernel,
-        out_shape=[shape(UNITS, HELD, LANES)] * OWNERS,
-        in_specs=whole(3 + OWNERS),
-        out_specs=whole(OWNERS),
-        compiler_params=params(14),
-        name="analyse",
-    )(transform, *pieces, above, below)
-
-
 FIELD_ROWS = 20
 NEAR_K, INNER_K, OUTER_K, NEAR_S, NEAR_R, NEAR_MASK = range(6)
 
 
-def field_kernel(place_ref, ksat_ref, storage_ref, recharge_ref, above_ref, below_ref, out_ref, edge_ref):
+def spread_fields(place_ref, ksat_ref, storage_ref, recharge_ref, above_ref, below_ref, out_ref, edge_ref):
     own = place_ref[0]
     lane = lane_ids(1)
     even = lane % 2 == 0
@@ -375,7 +317,7 @@
             r = place - 2
 
             def row_of(block):
-                line = (which * OWNERS + block) * 2
+                line = BORDER + (which * OWNERS + block) * 2
                 if r < 0:
                     return above_ref[pl.ds(line + r + 2, 1)]
                 if r >= ROWS:
@@ -415,21 +357,77 @@
     edge_ref[NEAR_MASK] = jnp.where((lane >= 2) & (lane < 2 * ROWS + 2), keep, 0.0)
 
 
-def block_fields(place, ksat, storage, recharge, above, below):
-    last = pl.BlockSpec((FIELD_LINES, LANES), lambda g: (BORDER // FIELD_LINES, 0))
-    mine = pl.BlockSpec((ROWS, OWNERS * LANES), lambda g: (0, 0))
-    return pl.pallas_call(
-        field_kernel,
-        grid=(1,),
-        out_shape=[shape(5, FIELD_ROWS, 8, LANES), shape(6, 8, LANES)],
-        in_specs=[SCALARS] + [mine] * 3 + [last] * 2,
-        out_specs=[
-            pl.BlockSpec((5, FIELD_ROWS, 8, LANES), lambda g: (0, 0, 0, 0)),
-            pl.BlockSpec((6, 8, LANES), lambda g: (0, 0, 0)),
-        ],
-        compiler_params=params(6),
-        name="fields",
-    )(place, ksat, storage, recharge, above, below)
+UNITS = ROWS + 5
+
+
+def halves(array):
+    high = array.astype(jnp.bfloat16)
+    return high, (array - high.astype(F32)).astype(jnp.bfloat16)
+
+
+def analyse_kernel(*refs):
+    place_ref, ksat_ref, storage_ref, recharge_ref, transform_ref = refs[:5]
+    piece_refs = refs[5 : 5 + OWNERS]
+    above_ref, below_ref, field_ref, edge_field_ref = refs[5 + OWNERS : 9 + OWNERS]
+    out_refs = refs[9 + OWNERS :]
+    spread_fields(
+        place_ref, ksat_ref, storage_ref, recharge_ref, above_ref, below_ref, field_ref, edge_field_ref
+    )
+    high, low = halves(transform_ref[...])
+    lane = lax.broadcasted_iota(jnp.int32, (MEMBERS, LANES), 1)
+
+    def joined(find):
+        return jnp.concatenate([find(i) for i in range(OWNERS)], axis=0)
+
+    def border(ref, n):
+        return joined(lambda i: ref[(i * 3 + n) * HELD : (i * 3 + n + 1) * HELD])
+
+    def cells(unit):
+        if unit > SENT_ROWS + 1:
+            return border(below_ref, unit - SENT_ROWS - 2)
+        if unit >= SENT_ROWS:
+            return border(above_ref, unit - SENT_ROWS + 1)
+        found = joined(lambda i: piece_refs[i][PLACE[unit]])
+        if unit == EDGE:
+            top = border(above_ref, 0)
+            bottom = border(below_ref, 2)
+            first = (lane < 2) | ((lane >= OWN) & (lane < OWN + 2))
+            last = 2 * ROWS + 2
+            final = ((lane >= last) & (lane < last + 2)) | (
+                (lane >= OWN + last) & (lane < OWN + last + 2)
+            )
+            found = jnp.where(first, turned(top, -2 * ROWS), found)
+            found = jnp.where(final, turned(bottom, 2 * ROWS), found)
+        return found
+
+    def product(a, b):
+        return jnp.dot(a, b, preferred_element_type=F32)
+
+    for first in range(0, UNITS, 2):
+        units = range(first, min(first + 2, UNITS))
+        found = [cells(u) for u in units]
+        state = found[0] if len(found) == 1 else jnp.concatenate(found, axis=1)
+        mean = jnp.sum(state, axis=0, keepdims=True) / MEMBERS
+        large, small = halves(state - mean)
+        result = product(low, large) + product(high, small) + product(high, large) + mean
+        for at, unit in enumerate(units):
+            for i in range(OWNERS):
+                out_refs[i][unit] = result[
+                    i * HELD : (i + 1) * HELD, at * LANES : (at + 1) * LANES
+                ]
+
+
+def analysed(place, cell_fields, transform, pieces, above, below):
+    found = pl.pallas_call(
+        analyse_kernel,
+        out_shape=[shape(5, FIELD_ROWS, 8, LANES), shape(6, 8, LANES)]
+        + [shape(UNITS, HELD, LANES)] * OWNERS,
+        in_specs=[SCALARS] + whole(6 + OWNERS),
+        out_specs=whole(2 + OWNERS),
+        compiler_params=params(14),
+        name="analyse",
+    )(place, *cell_fields, transform, *pieces, above, below)
+    return found[0], found[1], found[2:]
 
 
 def logistic(x):
@@ -593,33 +591,48 @@
     )(place, counts, wide_counts, fields, edge_fields, *cells)
 
 
-def unpack_kernel(place_ref, *refs):
-    own = place_ref[0]
-    pieces, out_ref = refs[:OWNERS], refs[OWNERS]
-    for i, piece in enumerate(pieces):
-        block = lax.rem(own - i + OWNERS, OWNERS)
-        start = pl.multiple_of(block * LANES, LANES)
-        out_ref[:, pl.ds(start, LANES)] = piece[...]
-
-
-def unpacked(place, pieces):
-    parts = 4
-    size = HELD * ROWS // parts
+def unpack_kernel(many, place_ref, *refs):
+    out_ref = refs[-1]
+    step = pl.program_id(0)
+    for n in range(many):
+
+        @pl.when(step == n)
+        def _():
+            out_ref[...] = refs[n][...]
+
+
+def unpacked(place, shifts, pieces, begun=None):
+    many = len(shifts)
+
+    def column(step, place_ref):
+        block = jnp.int32(0)
+        for n, shift in enumerate(shifts):
+            own = place_ref[0] - shift + OWNERS
+            block = jnp.where(step == n, lax.rem(own, OWNERS), block)
+        return 0, block
+
+    extra = [] if begun is None else [begun]
     return pl.pallas_call(
-        unpack_kernel,
-        grid=(parts,),
+        functools.partial(unpack_kernel, many),
+        grid_spec=pltpu.PrefetchScalarGridSpec(
+            num_scalar_prefetch=1,
+            grid=(many,),
+            in_specs=whole(many) + [pl.BlockSpec(memory_space=pl.ANY)] * len(extra),
+            out_specs=pl.BlockSpec((HELD * ROWS, LANES), column),
+        ),
         out_shape=shape(HELD * ROWS, OWNERS * LANES),
-        in_specs=[SCALARS] + [pl.BlockSpec((size, LANES), lambda g: (g, 0))] * OWNERS,
-        out_specs=pl.BlockSpec((size, OWNERS * LANES), lambda g: (g, 0)),
-        compiler_params=params(8),
+        input_output_aliases={1 + many: 0} if extra else {},
+        compiler_params=params(6),
         name="unpack",
-    )(place, *pieces)
+    )(place, *pieces, *extra)
+
+
+def exchanged(copies, axis):
+    return lax.all_to_all(copies, axis, split_axis=0, concat_axis=0, tiled=True)
 
 
 def shared(array, axis):
-    peers = lax.axis_size(axis)
-    copies = jnp.broadcast_to(array, (peers, *array.shape))
-    return lax.all_to_all(copies, axis, split_axis=0, concat_axis=0, tiled=True)
+    return exchanged(jnp.broadcast_to(array, (lax.axis_size(axis), *array.shape)), axis)
 
 
 def along(array, axis, step):
@@ -642,8 +655,8 @@
         [own, (strip > 0).astype(jnp.int32), (strip < lax.axis_size(SPACE) - 1).astype(jnp.int32)]
     ).astype(jnp.int32)
 
-    seen = observed(flat, obs_index[None])
-    same = shared(seen, MEMBER[0])
+    seen = observed(flat, obs_index[None], lax.axis_size(MEMBER[0]))
+    same = exchanged(seen, MEMBER[0])
 
     blocks = packed_blocks(place, flat, seen)
     wide_counts = jnp.broadcast_to(newton_counts[:, None], (MEMBERS, LANES))
@@ -651,23 +664,23 @@
     other = along(same, MEMBER[1], 1)
 
     pieces = [blocks[0]] + [None] * (OWNERS - 1)
-    for i in (2, 6):
+    for i in (2, 6, 3, 5):
         pieces[i] = along(blocks[i], MEMBER, -i)
-    part = gram_blocks(place, same, other, obs_value[None], obs_scale[None])
+    copies = lax.axis_size(SPACE[0])
+    part = gram_blocks(place, same, other, obs_value[None], obs_scale[None], copies)
     part, blocks = lax.optimization_barrier((part, blocks))
-    for i in (3, 5, 4, 1, 7):
+    for i in (4, 1, 7):
         pieces[i] = along(blocks[i], MEMBER, -i)
-    part = jnp.sum(shared(part, SPACE[0]), axis=0)
+    part = jnp.sum(exchanged(part, SPACE[0]), axis=0)
     part = jnp.sum(shared(part, SPACE[1]), axis=0)
-    part, pieces = lax.optimization_barrier((part, pieces))
     parts = shared(part, MEMBER)
-    down, up = borders(pieces, (ksat, storage, recharge))
+    cell_fields = (ksat, storage, recharge)
+    down, up = borders(pieces, cell_fields)
     parts, down, up = lax.optimization_barrier((parts, down, up))
     above = to_strips_beside(up, 1)
     below = to_strips_beside(down, -1)
     transform = transform_of(place, parts)
-    fields, edge_fields = block_fields(place, ksat, storage, recharge, above, below)
-    cells = analysed(transform, pieces, above, below)
+    fields, edge_fields, cells = analysed(place, cell_fields, transform, pieces, above, below)
 
     arrived = [None] * OWNERS
     for shifts in ((2,), (6,), (3, 5), (4, 1), (7, 0)):
@@ -677,7 +690,10 @@
         moved, cells = lax.optimization_barrier((moved, cells))
         for i, field in zip(shifts, moved):
             arrived[i] = along(field, MEMBER, i) if i else field
-    return unpacked(place, arrived).reshape(members, rows, columns)
+    early, late = (0, 2, 6, 3, 5), (4, 1, 7)
+    result = unpacked(place, early, [arrived[i] for i in early])
+    result = unpacked(place, late, [arrived[i] for i in late], result)
+    return result.reshape(members, rows, columns)
 
 
 def solution(mesh):

time: 134 us -> 137 us (1.022); the launches traced: 134 us -> 134 us
  local copies, waits for them, and re-layouts: 9.66 us -> 5.28 us
  Pallas kernels: 45.9 us -> 48.5 us
  waiting for transfers between devices: 25.2 us -> 26.8 us
    pallas_call x5, Pallas kernels: 9.82 us -> 13.5 us  [the longest x2 4.87 us: unpacked(): pl.pallas_call(functools.partial(unpack_kernel, many), grid_spec=pltpu.Pr...]
    unnamed x32 -> x28, local copies, waits for them, and re-layouts: 7.33 us -> 4.5 us
    pallas_call x1, Pallas kernels: 13.9 us -> 11.8 us  [transform_of(): pl.pallas_call(root_kernel, out_shape=shape(MEMBERS, MEMBERS), in_specs=[...]
    broadcast_in_dim x4 -> x2, local copies, waits for them, and re-layouts: 2.24 us -> 0.7 us  [shared(): jnp.broadcast_to(array, (lax.axis_size(axis), *array.shape))]
  transfers between devices with their start and end apart: 20 -> 20, of which waited for: 8 -> 7; matrix products, arithmetic and copies ran while one was open for 1% -> 1% of each run, Pallas kernels for 24% -> 25%
where the time goes in v3:
time: 137 us; the launch traced here: 134 us
  Pallas kernels  48.5 us (35%)
  starting transfers between devices  44.7 us (33%)
  waiting for transfers between devices  26.8 us (20%)
  blocking collectives  8.77 us (6%)
  local copies, waits for them, and re-layouts  5.28 us (4%)
    ppermute x15, starting transfers between devices, along(): lax.ppermute(array, axis, [(i, (i + step) % peers) for i in range(peers)])  20.4 us
    pallas_call x5, Pallas kernels, forecasts(): pl.pallas_call(functools.partial(forecast_kernel, shifts), out_shape=[sha...  19.8 us
    ppermute x15, waiting for transfers between devices, along(): lax.ppermute(array, axis, [(i, (i + step) % peers) for i in range(peers)])  18.4 us
    all_to_all x3, starting transfers between devices, exchanged(): return lax.all_to_all(copies, axis, split_axis=0, concat_axis=0, tiled=True)  16.7 us
    pallas_call x1, Pallas kernels, transform_of(): pl.pallas_call(root_kernel, out_shape=shape(MEMBERS, MEMBERS), in_specs=[...  11.8 us
    all_to_all x1, blocking collectives, exchanged(): return lax.all_to_all(copies, axis, split_axis=0, concat_axis=0, tiled=True)  8.77 us
    all_to_all x3, waiting for transfers between devices, exchanged(): return lax.all_to_all(copies, axis, split_axis=0, concat_axis=0, tiled=True)  8.42 us
    ppermute x2, starting transfers between devices, to_strips_beside(): return lax.ppermute(array, SPACE, pairs)  7.56 us
  transfers between devices with their start and end apart: 20, of which 7 were waited for; matrix products, arithmetic and copies ran while one was open for 1% of the time, Pallas kernels for 25%

profile of v3, /device:TPU:33, one launch (start us, length us, event | category | flops | bytes accessed | tf_op | source)
XLA Modules:
  0.0 134.3 jit_solution(18287277439036688495)
XLA Ops:
  2.3 4.5 %observe.1.after_ref = f32[4,32,1024]{2,1,0:T(8,128)} custom-call(s32[1,1024]{1,0:T(1,128)S(1)} %bitcast.10, f32[512,1024]{1,0:T(8,128)S(1)} %bitcast.8), custom_call_target="tpu_custom_call" | custom-call | tf_op jit(solution)/shard_map/observe/pallas_call | solution.py:81
  6.8 4.3 %all-to-all-start = ((f32[4,32,1024]{2,1,0:T(8,128)}), f32[4,32,1024]{2,1,0:T(8,128)S(1)}, u32[]{:S(2)}, u32[]{:S(2)}) async-start(f32[4,32,1024]{2,1,0:T(8,128)} %observe.1.after_ref), calls=%async_computation | async-start | bytes 1048576 | tf_op jit(solution)/shard_map/all_to_all | solution.py:631
  11.2 3.3 %pack.1 = (f32[17,32,128]{2,1,0:T(8,128)S(1)}, f32[17,32,128]{2,1,0:T(8,128)}, f32[17,32,128]{2,1,0:T(8,128)S(1)}, f32[17,32,128]{2,1,0:T(8,128)S(1)}, f32[17,32...) custom-call(s32[3]{0:T(128)S(1)} %pad_add_fusion.place_ref.refs_0_, ...), custom_call_target="tpu_custom_call" | custom-call | tf_op jit(solution)/shard_map/pack/pallas_call | solution.py:146
  15.9 3.4 %all-to-all-done.same_ref = f32[4,32,1024]{2,1,0:T(8,128)S(1)} async-done(((f32[4,32,1024]{2,1,0:T(8,128)}), f32[4,32,1024]{2,1,0:T(8,128)S(1)}, u32[]{:S(2)}, u32[]{:S(2)}) %all-to-all-start) | async-done | bytes 524320 | tf_op jit(solution)/shard_map/all_to_all | solution.py:631
  19.4 2.2 %collective-permute-start = (f32[4,32,1024]{2,1,0:T(8,128)S(1)}, f32[4,32,1024]{2,1,0:T(8,128)S(1)}, u32[]{:S(2)}, u32[]{:S(2)}) collective-permute-start(f32[4,32,1024]{2,1,0:T(8,128)S(1)} %all-to-all-done.same_ref), channel_id=1, source_target_pairs={{0,32},{32,0},{1,33},{33,1},{2,34},{34,2},{3,35},{35,3},{4,36},{36... | collective-permute-start | bytes 1572872 | tf_op jit(solution)/shard_map/ppermute | solution.py:640
  25.4 8.0 %all-to-all-start.1 = ((f32[8,48,128]{2,1,0:T(8,128)}), f32[8,48,128]{2,1,0:T(8,128)S(1)}, u32[]{:S(2)}, u32[]{:S(2)}) async-start(f32[8,48,128]{2,1,0:T(8,128)} %gram.1), calls=%async_computation.1 | async-start | bytes 393216 | tf_op jit(solution)/shard_map/all_to_all | solution.py:631
  35.2 2.3 %collective-permute-start.5 = (f32[17,32,128]{2,1,0:T(8,128)}, f32[17,32,128]{2,1,0:T(8,128)S(1)}, u32[]{:S(2)}, u32[]{:S(2)}) collective-permute-start(f32[17,32,128]{2,1,0:T(8,128)} %get-tuple-element.90), channel_id=1, source_target_pairs={{0,96},{32,128},{64,160},{96,192},{128,224},{160,0},{192,32},{224,... | collective-permute-start | bytes 835592 | tf_op jit(solution)/shard_map/ppermute | solution.py:640
  38.1 2.5 %collective-permute-done.2.refs_2_.refs_7_ = f32[17,32,128]{2,1,0:T(8,128)S(1)} collective-permute-done((f32[17,32,128]{2,1,0:T(8,128)S(1)}, f32[17,32,128]{2,1,0:T(8,128)S(1)}, u32[]{:S(2)}, u32[]{:S(2)}) %collective-permute-start.2) | collective-permute-done | bytes 278560 | tf_op jit(solution)/shard_map/ppermute | solution.py:640
  41.5 8.9 %collective-permute-done.3.refs_3_.refs_8_ = f32[17,32,128]{2,1,0:T(8,128)S(1)} collective-permute-done((f32[17,32,128]{2,1,0:T(8,128)S(1)}, f32[17,32,128]{2,1,0:T(8,128)S(1)}, u32[]{:S(2)}, u32[]{:S(2)}) %collective-permute-start.3) | collective-permute-done | bytes 278560 | tf_op jit(solution)/shard_map/ppermute | solution.py:640
  50.4 2.6 %collective-permute-start.7 = (f32[17,32,128]{2,1,0:T(8,128)S(1)}, f32[17,32,128]{2,1,0:T(8,128)S(1)}, u32[]{:S(2)}, u32[]{:S(2)}) collective-permute-start(f32[17,32,128]{2,1,0:T(8,128)S(1)} %get-tuple-element.96), channel_id=1, source_target_pairs={{0,32},{32,64},{64,96},{96,128},{128,160},{160,192},{192,224},{224... | collective-permute-start | bytes 835592 | tf_op jit(solution)/shard_map/ppermute | solution.py:640
  53.1 8.8 %all_to_all.20 = f32[4,48,128]{2,1,0:T(8,128)S(1)} all-to-all(f32[4,48,128]{2,1,0:T(8,128)S(1)} %broadcast_in_dim.25), channel_id=1, replica_groups=mesh['member_0'=4,'member_1'=2,'space_0'=8,'space_1'=4] {'space_1'}, dimensions={0} | all-to-all | bytes 196608 | tf_op jit(solution)/shard_map/all_to_all | solution.py:631
  62.5 4.3 %all-to-all-start.3 = ((f32[8,48,128]{2,1,0:T(8,128)}), f32[8,48,128]{2,1,0:T(8,128)S(1)}, u32[]{:S(2)}, u32[]{:S(2)}) async-start(f32[8,48,128]{2,1,0:T(8,128)} %broadcast_in_dim.26), calls=%async_computation.3 | async-start | bytes 393216 | tf_op jit(solution)/shard_map/all_to_all | solution.py:631
  67.8 5.0 %all-to-all-done.3.parts_ref = f32[8,48,128]{2,1,0:T(8,128)S(1)} async-done(((f32[8,48,128]{2,1,0:T(8,128)}), f32[8,48,128]{2,1,0:T(8,128)S(1)}, u32[]{:S(2)}, u32[]{:S(2)}) %all-to-all-start.3) | async-done | bytes 196640 | tf_op jit(solution)/shard_map/all_to_all | solution.py:631
  72.8 2.2 %collective-permute-start.8 = (f32[816,128]{1,0:T(8,128)}, f32[816,128]{1,0:T(8,128)S(1)}, u32[]{:S(2)}, u32[]{:S(2)}) collective-permute-start(f32[816,128]{1,0:T(8,128)} %copy-done.7), channel_id=1, source_target_pairs={{0,1},{1,2},{2,3},{3,4},{4,5},{5,6},{6,7},{7,8},{8,9},{9,10},{10,1... | collective-permute-start | bytes 1253384 | tf_op jit(solution)/shard_map/ppermute | solution.py:646
  75.0 5.4 %collective-permute-start.9 = (f32[816,128]{1,0:T(8,128)S(1)}, f32[816,128]{1,0:T(8,128)S(1)}, u32[]{:S(2)}, u32[]{:S(2)}) collective-permute-start(f32[816,128]{1,0:T(8,128)S(1)} %get-tuple-element.101), channel_id=1, source_target_pairs={{1,0},{2,1},{3,2},{4,3},{5,4},{6,5},{7,6},{8,7},{9,8},{10,9},{11,1... | collective-permute-start | bytes 1253384 | tf_op jit(solution)/shard_map/ppermute | solution.py:646
  80.3 11.8 %root.1.refs_4_ = f32[256,256]{1,0:T(8,128)S(1)} custom-call(s32[3]{0:T(128)S(1)} %pad_add_fusion.place_ref.refs_0_, f32[8,48,128]{2,1,0:T(8,128)S(1)} %all-to-all-done.3.parts_ref), custom_call_target="tpu_custom_call" | custom-call | flops 10000000000 | bytes 1000000 | tf_op jit(solution)/shard_map/root/pallas_call | solution.py:290
  94.2 2.4 %forecast.5 = f32[512,128]{1,0:T(8,128)S(1)} custom-call(s32[3]{0:T(128)S(1)} %pad_add_fusion.place_ref.refs_0_, s32[256]{0:T(256)S(1)} %copy-done.5, s32[256,128]{1,0:T(8,128)S(1)} %broadcast_in_dim.22.wide_ref, f32[5,20,8,128]{3,2,1,0:T(8,128)S(1)} %get-tuple-element.102.field_ref, f32[6,8,128]{2,1,0:T(8,128)S(1)} %get-tuple-element.103.edge_field_ref, ...), custom_call_target="tpu_custom_call" | custom-call | flops 1 | bytes 1 | tf_op jit(solution)/shard_map/forecast/pallas_call | solution.py:578
  96.6 2.4 %forecast.6 = f32[512,128]{1,0:T(8,128)S(1)} custom-call(s32[3]{0:T(128)S(1)} %pad_add_fusion.place_ref.refs_0_, s32[256]{0:T(256)S(1)} %copy-done.5, s32[256,128]{1,0:T(8,128)S(1)} %broadcast_in_dim.22.wide_ref, f32[5,20,8,128]{3,2,1,0:T(8,128)S(1)} %get-tuple-element.102.field_ref, f32[6,8,128]{2,1,0:T(8,128)S(1)} %get-tuple-element.103.edge_field_ref, ...), custom_call_target="tpu_custom_call" | custom-call | flops 1 | bytes 1 | tf_op jit(solution)/shard_map/forecast/pallas_call | solution.py:578
  100.8 5.8 %forecast.7 = (f32[512,128]{1,0:T(8,128)S(1)}, f32[512,128]{1,0:T(8,128)S(1)}) custom-call(s32[3]{0:T(128)S(1)} %pad_add_fusion.place_ref.refs_0_, s32[256]{0:T(256)S(1)} %copy-done.5, s32[256,128]{1,0:T(8,128)S(1)} %broadcast_in_dim.22.wide_ref, f32[5,20,8,128]{3,2,1,0:T(8,128)S(1)} %get-tuple-element.102.field_ref, ...), custom_call_target="tpu_custom_call" | custom-call | flops 1 | bytes 1 | tf_op jit(solution)/shard_map/forecast/pallas_call | solution.py:578
  106.6 2.5 %collective-permute-start.15 = (f32[512,128]{1,0:T(8,128)S(1)}, f32[512,128]{1,0:T(8,128)S(1)}, u32[]{:S(2)}, u32[]{:S(2)}) collective-permute-start(f32[512,128]{1,0:T(8,128)S(1)} %get-tuple-element.143), channel_id=1, source_target_pairs={{0,96},{32,128},{64,160},{96,192},{128,224},{160,0},{192,32},{224,... | collective-permute-start | bytes 786440 | tf_op jit(solution)/shard_map/ppermute | solution.py:640
  110.6 5.0 %forecast.8 = (f32[512,128]{1,0:T(8,128)S(1)}, f32[512,128]{1,0:T(8,128)S(1)}) custom-call(s32[3]{0:T(128)S(1)} %pad_add_fusion.place_ref.refs_0_, s32[256]{0:T(256)S(1)} %copy-done.5, s32[256,128]{1,0:T(8,128)S(1)} %broadcast_in_dim.22.wide_ref, f32[5,20,8,128]{3,2,1,0:T(8,128)S(1)} %get-tuple-element.102.field_ref, ...), custom_call_target="tpu_custom_call" | custom-call | flops 1 | bytes 1 | tf_op jit(solution)/shard_map/forecast/pallas_call | solution.py:578
  115.6 4.2 %forecast.9 = (f32[512,128]{1,0:T(8,128)S(1)}, f32[512,128]{1,0:T(8,128)S(1)}) custom-call(s32[3]{0:T(128)S(1)} %pad_add_fusion.place_ref.refs_0_, s32[256]{0:T(256)S(1)} %copy-done.5, s32[256,128]{1,0:T(8,128)S(1)} %broadcast_in_dim.22.wide_ref, f32[5,20,8,128]{3,2,1,0:T(8,128)S(1)} %get-tuple-element.102.field_ref, ...), custom_call_target="tpu_custom_call" | custom-call | flops 1 | bytes 1 | tf_op jit(solution)/shard_map/forecast/pallas_call | solution.py:578
  124.0 2.8 %unpack.2.refs_3_ = f32[512,1024]{1,0:T(8,128)} custom-call(s32[3]{0:T(128)S(1)} %pad_add_fusion.place_ref.refs_0_, f32[512,128]{1,0:T(8,128)S(1)} %get-tuple-element.140.refs_0_, f32[512,128]{1,0:T(8,128)S(1)} %collective-permute-done.13.refs_1_, f32[512,128]{1,0:T(8,128)S(1)} %collective-permute-done.14.refs_2_, ...), custom_call_target="tpu_custom_call" | custom-call | tf_op jit(solution)/shard_map/unpack/pallas_call | solution.py:615
  126.9 4.3 %collective-permute-done.10.refs_0_ = f32[512,128]{1,0:T(8,128)S(1)} collective-permute-done((f32[512,128]{1,0:T(8,128)S(1)}, f32[512,128]{1,0:T(8,128)S(1)}, u32[]{:S(2)}, u32[]{:S(2)}) %collective-permute-start.10) | collective-permute-done | bytes 262176 | tf_op jit(solution)/shard_map/ppermute | solution.py:640
  (64 shorter events, 25.0 us)
Async XLA Ops:
  6.8 16.5 %copy-start.13 = (f32[1024]{0:T(1024)S(1)}, f32[1024]{0:T(1024)}, u32[]{:S(2)}) copy-start(f32[1024]{0:T(1024)} %param.11) | copy-start | bytes 12292
  6.8 12.6 %all-to-all-start = ((f32[4,32,1024]{2,1,0:T(8,128)}), f32[4,32,1024]{2,1,0:T(8,128)S(1)}, u32[]{:S(2)}, u32[]{:S(2)}) async-start(f32[4,32,1024]{2,1,0:T(8,128)} %observe.1.after_ref), calls=%async_computation | async-start | bytes 1048576 | tf_op jit(solution)/shard_map/all_to_all | solution.py:631
  19.4 3.8 %collective-permute-start = (f32[4,32,1024]{2,1,0:T(8,128)S(1)}, f32[4,32,1024]{2,1,0:T(8,128)S(1)}, u32[]{:S(2)}, u32[]{:S(2)}) collective-permute-start(f32[4,32,1024]{2,1,0:T(8,128)S(1)} %all-to-all-done.same_ref), channel_id=1, source_target_pairs={{0,32},{32,0},{1,33},{33,1},{2,34},{34,2},{3,35},{35,3},{4,36},{36... | collective-permute-start | bytes 1572872 | tf_op jit(solution)/shard_map/ppermute | solution.py:640
  23.2 43.7 %copy-start.2 = (f32[16,1024]{1,0:T(8,128)S(1)}, f32[16,1024]{1,0:T(8,128)}, u32[]{:S(2)}) copy-start(f32[16,1024]{1,0:T(8,128)} %refs_1_.1) | copy-start | bytes 196612
  23.3 43.7 %copy-start.3 = (f32[16,1024]{1,0:T(8,128)S(1)}, f32[16,1024]{1,0:T(8,128)}, u32[]{:S(2)}) copy-start(f32[16,1024]{1,0:T(8,128)} %refs_2_.1) | copy-start | bytes 196612
  23.3 43.7 %copy-start.4 = (f32[16,1024]{1,0:T(8,128)S(1)}, f32[16,1024]{1,0:T(8,128)}, u32[]{:S(2)}) copy-start(f32[16,1024]{1,0:T(8,128)} %refs_3_.1) | copy-start | bytes 196612
  25.4 27.7 %all-to-all-start.1 = ((f32[8,48,128]{2,1,0:T(8,128)}), f32[8,48,128]{2,1,0:T(8,128)S(1)}, u32[]{:S(2)}, u32[]{:S(2)}) async-start(f32[8,48,128]{2,1,0:T(8,128)} %gram.1), calls=%async_computation.1 | async-start | bytes 393216 | tf_op jit(solution)/shard_map/all_to_all | solution.py:631
  33.4 7.2 %collective-permute-start.2 = (f32[17,32,128]{2,1,0:T(8,128)S(1)}, f32[17,32,128]{2,1,0:T(8,128)S(1)}, u32[]{:S(2)}, u32[]{:S(2)}) collective-permute-start(f32[17,32,128]{2,1,0:T(8,128)S(1)} %copy-done.11), channel_id=1, source_target_pairs={{0,192},{32,224},{64,0},{96,32},{128,64},{160,96},{192,128},{224,1... | collective-permute-start | bytes 835592 | tf_op jit(solution)/shard_map/ppermute | solution.py:640
  34.3 16.1 %collective-permute-start.3 = (f32[17,32,128]{2,1,0:T(8,128)S(1)}, f32[17,32,128]{2,1,0:T(8,128)S(1)}, u32[]{:S(2)}, u32[]{:S(2)}) collective-permute-start(f32[17,32,128]{2,1,0:T(8,128)S(1)} %copy-done.9), channel_id=1, source_target_pairs={{0,160},{32,192},{64,224},{96,0},{128,32},{160,64},{192,96},{224,1... | collective-permute-start | bytes 835592 | tf_op jit(solution)/shard_map/ppermute | solution.py:640
  35.2 31.7 %collective-permute-start.5 = (f32[17,32,128]{2,1,0:T(8,128)}, f32[17,32,128]{2,1,0:T(8,128)S(1)}, u32[]{:S(2)}, u32[]{:S(2)}) collective-permute-start(f32[17,32,128]{2,1,0:T(8,128)} %get-tuple-element.90), channel_id=1, source_target_pairs={{0,96},{32,128},{64,160},{96,192},{128,224},{160,0},{192,32},{224,... | collective-permute-start | bytes 835592 | tf_op jit(solution)/shard_map/ppermute | solution.py:640
  37.5 29.4 %collective-permute-start.6 = (f32[17,32,128]{2,1,0:T(8,128)}, f32[17,32,128]{2,1,0:T(8,128)S(1)}, u32[]{:S(2)}, u32[]{:S(2)}) collective-permute-start(f32[17,32,128]{2,1,0:T(8,128)} %get-tuple-element.91), channel_id=1, source_target_pairs={{0,64},{32,96},{64,128},{96,160},{128,192},{160,224},{192,0},{224,... | collective-permute-start | bytes 835592 | tf_op jit(solution)/shard_map/ppermute | solution.py:640
  38.1 28.8 %collective-permute-start.1 = (f32[17,32,128]{2,1,0:T(8,128)}, f32[17,32,128]{2,1,0:T(8,128)S(1)}, u32[]{:S(2)}, u32[]{:S(2)}) collective-permute-start(f32[17,32,128]{2,1,0:T(8,128)} %get-tuple-element.94), channel_id=1, source_target_pairs={{0,224},{32,0},{64,32},{96,64},{128,96},{160,128},{192,160},{224,1... | collective-permute-start | bytes 835592 | tf_op jit(solution)/shard_map/ppermute | solution.py:640
  40.6 26.3 %collective-permute-start.4 = (f32[17,32,128]{2,1,0:T(8,128)}, f32[17,32,128]{2,1,0:T(8,128)S(1)}, u32[]{:S(2)}, u32[]{:S(2)}) collective-permute-start(f32[17,32,128]{2,1,0:T(8,128)} %get-tuple-element.95), channel_id=1, source_target_pairs={{0,128},{32,160},{64,192},{96,224},{128,0},{160,32},{192,64},{224,... | collective-permute-start | bytes 835592 | tf_op jit(solution)/shard_map/ppermute | solution.py:640
  50.4 16.5 %collective-permute-start.7 = (f32[17,32,128]{2,1,0:T(8,128)S(1)}, f32[17,32,128]{2,1,0:T(8,128)S(1)}, u32[]{:S(2)}, u32[]{:S(2)}) collective-permute-start(f32[17,32,128]{2,1,0:T(8,128)S(1)} %get-tuple-element.96), channel_id=1, source_target_pairs={{0,32},{32,64},{64,96},{96,128},{128,160},{160,192},{192,224},{224... | collective-permute-start | bytes 835592 | tf_op jit(solution)/shard_map/ppermute | solution.py:640
  62.5 10.2 %all-to-all-start.3 = ((f32[8,48,128]{2,1,0:T(8,128)}), f32[8,48,128]{2,1,0:T(8,128)S(1)}, u32[]{:S(2)}, u32[]{:S(2)}) async-start(f32[8,48,128]{2,1,0:T(8,128)} %broadcast_in_dim.26), calls=%async_computation.3 | async-start | bytes 393216 | tf_op jit(solution)/shard_map/all_to_all | solution.py:631
  72.8 19.4 %collective-permute-start.8 = (f32[816,128]{1,0:T(8,128)}, f32[816,128]{1,0:T(8,128)S(1)}, u32[]{:S(2)}, u32[]{:S(2)}) collective-permute-start(f32[816,128]{1,0:T(8,128)} %copy-done.7), channel_id=1, source_target_pairs={{0,1},{1,2},{2,3},{3,4},{4,5},{5,6},{6,7},{7,8},{8,9},{9,10},{10,1... | collective-permute-start | bytes 1253384 | tf_op jit(solution)/shard_map/ppermute | solution.py:646
  75.0 17.2 %collective-permute-start.9 = (f32[816,128]{1,0:T(8,128)S(1)}, f32[816,128]{1,0:T(8,128)S(1)}, u32[]{:S(2)}, u32[]{:S(2)}) collective-permute-start(f32[816,128]{1,0:T(8,128)S(1)} %get-tuple-element.101), channel_id=1, source_target_pairs={{1,0},{2,1},{3,2},{4,3},{5,4},{6,5},{7,6},{8,7},{9,8},{10,9},{11,1... | collective-permute-start | bytes 1253384 | tf_op jit(solution)/shard_map/ppermute | solution.py:646
  99.0 22.8 %collective-permute-start.14 = (f32[512,128]{1,0:T(8,128)S(1)}, f32[512,128]{1,0:T(8,128)S(1)}, u32[]{:S(2)}, u32[]{:S(2)}) collective-permute-start(f32[512,128]{1,0:T(8,128)S(1)} %forecast.6), channel_id=1, source_target_pairs={{0,192},{32,224},{64,0},{96,32},{128,64},{160,96},{192,128},{224,1... | collective-permute-start | bytes 786440 | tf_op jit(solution)/shard_map/ppermute | solution.py:640
  100.8 22.5 %collective-permute-start.13 = (f32[512,128]{1,0:T(8,128)S(1)}, f32[512,128]{1,0:T(8,128)S(1)}, u32[]{:S(2)}, u32[]{:S(2)}) collective-permute-start(f32[512,128]{1,0:T(8,128)S(1)} %forecast.5), channel_id=1, source_target_pairs={{0,64},{32,96},{64,128},{96,160},{128,192},{160,224},{192,0},{224,... | collective-permute-start | bytes 786440 | tf_op jit(solution)/shard_map/ppermute | solution.py:640
  106.6 17.4 %collective-permute-start.15 = (f32[512,128]{1,0:T(8,128)S(1)}, f32[512,128]{1,0:T(8,128)S(1)}, u32[]{:S(2)}, u32[]{:S(2)}) collective-permute-start(f32[512,128]{1,0:T(8,128)S(1)} %get-tuple-element.143), channel_id=1, source_target_pairs={{0,96},{32,128},{64,160},{96,192},{128,224},{160,0},{192,32},{224,... | collective-permute-start | bytes 786440 | tf_op jit(solution)/shard_map/ppermute | solution.py:640
  109.0 15.0 %collective-permute-start.16 = (f32[512,128]{1,0:T(8,128)S(1)}, f32[512,128]{1,0:T(8,128)S(1)}, u32[]{:S(2)}, u32[]{:S(2)}) collective-permute-start(f32[512,128]{1,0:T(8,128)S(1)} %get-tuple-element.144), channel_id=1, source_target_pairs={{0,160},{32,192},{64,224},{96,0},{128,32},{160,64},{192,96},{224,1... | collective-permute-start | bytes 786440 | tf_op jit(solution)/shard_map/ppermute | solution.py:640
  119.9 7.0 %collective-permute-start.12 = (f32[512,128]{1,0:T(8,128)S(1)}, f32[512,128]{1,0:T(8,128)S(1)}, u32[]{:S(2)}, u32[]{:S(2)}) collective-permute-start(f32[512,128]{1,0:T(8,128)S(1)} %get-tuple-element.139), channel_id=1, source_target_pairs={{0,224},{32,0},{64,32},{96,64},{128,96},{160,128},{192,160},{224,1... | collective-permute-start | bytes 786440 | tf_op jit(solution)/shard_map/ppermute | solution.py:640
  121.8 9.4 %collective-permute-start.10 = (f32[512,128]{1,0:T(8,128)S(1)}, f32[512,128]{1,0:T(8,128)S(1)}, u32[]{:S(2)}, u32[]{:S(2)}) collective-permute-start(f32[512,128]{1,0:T(8,128)S(1)} %get-tuple-element.133), channel_id=1, source_target_pairs={{0,128},{32,160},{64,192},{96,224},{128,0},{160,32},{192,64},{224,... | collective-permute-start | bytes 786440 | tf_op jit(solution)/shard_map/ppermute | solution.py:640
  123.3 9.0 %collective-permute-start.11 = (f32[512,128]{1,0:T(8,128)S(1)}, f32[512,128]{1,0:T(8,128)S(1)}, u32[]{:S(2)}, u32[]{:S(2)}) collective-permute-start(f32[512,128]{1,0:T(8,128)S(1)} %get-tuple-element.134), channel_id=1, source_target_pairs={{0,32},{32,64},{64,96},{96,128},{128,160},{160,192},{192,224},{224... | collective-permute-start | bytes 786440 | tf_op jit(solution)/shard_map/ppermute | solution.py:640
  (10 other events, 63.6 us)

commit v4 on v3

--- a/solution.py
+++ b/solution.py
@@ -39,6 +39,13 @@
 
 
 SCALARS = pl.BlockSpec(memory_space=pltpu.SMEM)
+
+
+def relative(own, place, sign=1):
+    chip, core = lax.div(own, 2), lax.rem(own, 2)
+    chips = OWNERS // 2
+    other = lax.rem(chip + sign * (place // 2) + chips, chips)
+    return 2 * other + (1 - core if place % 2 else core)
 
 
 def lane_ids(rows=8):
@@ -94,7 +101,7 @@
 
 def pack_kernel(place_ref, state_ref, after_ref, *refs):
     own = place_ref[0]
-    sent_refs, column_ref = refs[:OWNERS], refs[OWNERS]
+    sent_refs, column_ref = refs[:2], refs[2]
     lane = lane_ids()
     even = lane % 2 == 0
     near_left = (lane < OUTER) & even
@@ -108,14 +115,14 @@
         members = pl.ds(pl.multiple_of(group * 8, 8), 8)
         lines = pl.ds(pl.multiple_of(group * 8 * ROWS, 8 * ROWS), 8 * ROWS)
         for slot in range(OWNERS):
-            block = lax.rem(own - slot + OWNERS, OWNERS)
+            block = relative(own, slot, -1)
             packed_near = jnp.zeros((8, LANES), F32)
             packed_far = jnp.zeros((8, LANES), F32)
             start = pl.multiple_of(block * LANES, LANES)
             column_ref[slot] = state_ref[lines, pl.ds(start, LANES)]
             for r in range(ROWS):
                 value = column_ref[slot, pl.ds(r, 8, stride=ROWS), :]
-                sent_refs[slot][PLACE[r], members] = value
+                sent_refs[slot % 2][slot // 2, PLACE[r], members] = value
                 at = 2 * (r + 1)
                 packed_near = jnp.where(
                     (lane == at) | (lane == at + 1), turned(value, at + 1), packed_near
@@ -127,16 +134,25 @@
             near.append(packed_near)
             far.append(packed_far)
         for slot in range(OWNERS):
-            block = lax.rem(own - slot + OWNERS, OWNERS)
-            left, right = (slot + 1) % OWNERS, (slot - 1) % OWNERS
+            block = relative(own, slot, -1)
+            odd = lax.rem(block, 2) == 1
+            beside, further = slot ^ 1, ((slot ^ 1) + 2) % OWNERS
+            nearer = ((slot ^ 1) - 2) % OWNERS
             has_left = (block > 0).astype(F32)
             has_right = (block < OWNERS - 1).astype(F32)
+
+            def left(packed):
+                return jnp.where(odd, packed[beside], packed[further]) * has_left
+
+            def right(packed):
+                return jnp.where(odd, packed[nearer], packed[beside]) * has_right
+
             edge = jnp.where(own_lanes, turned(near[slot], OWN), 0.0)
-            edge = jnp.where(near_left, near[left] * has_left, edge)
-            edge = jnp.where(far_left, far[left] * has_left, edge)
-            edge = jnp.where(near_right, near[right] * has_right, edge)
-            edge = jnp.where(far_right, far[right] * has_right, edge)
-            sent_refs[slot][PLACE[EDGE], members] = edge
+            edge = jnp.where(near_left, left(near), edge)
+            edge = jnp.where(far_left, left(far), edge)
+            edge = jnp.where(near_right, right(near), edge)
+            edge = jnp.where(far_right, right(far), edge)
+            sent_refs[slot % 2][slot // 2, PLACE[EDGE], members] = edge
         return carry
 
     lax.fori_loop(0, HELD // 8, one_group, 0)
@@ -145,9 +161,9 @@
 def packed_blocks(place, state, after):
     return pl.pallas_call(
         pack_kernel,
-        out_shape=[shape(SENT_ROWS, HELD, LANES)] * OWNERS,
+        out_shape=[shape(OWNERS // 2, SENT_ROWS, HELD, LANES)] * 2,
         in_specs=[SCALARS] + whole(1) + [pl.BlockSpec(memory_space=pl.ANY)],
-        out_specs=whole(OWNERS),
+        out_specs=whole(2),
         scratch_shapes=[pltpu.VMEM((OWNERS, 8 * ROWS, LANES), F32)],
         compiler_params=params(8),
         name="pack",
@@ -159,12 +175,14 @@
 
 
 def border_kernel(*refs):
-    pieces, fields = refs[:OWNERS], refs[OWNERS : OWNERS + 3]
-    down_ref, up_ref = refs[OWNERS + 3 :]
+    chips = OWNERS // 2
+    pieces, fields = refs[:chips], refs[chips : chips + 3]
+    down_ref, up_ref = refs[chips + 3 :]
     size = 3 * HELD
-    for i, piece in enumerate(pieces):
-        down_ref[i * size : (i + 1) * size] = piece[0:3].reshape(size, LANES)
-        up_ref[i * size : (i + 1) * size] = piece[2:5].reshape(size, LANES)
+    for i in range(OWNERS):
+        piece = pieces[i // 2]
+        down_ref[i * size : (i + 1) * size] = piece[i % 2, 0:3].reshape(size, LANES)
+        up_ref[i * size : (i + 1) * size] = piece[i % 2, 2:5].reshape(size, LANES)
     for which, ref in enumerate(fields):
         for block in range(OWNERS):
             at = BORDER + (which * OWNERS + block) * 2
@@ -179,7 +197,7 @@
         border_kernel,
         grid=(1,),
         out_shape=[shape(size, LANES)] * 2,
-        in_specs=[pl.BlockSpec((5, HELD, LANES), lambda g: (0, 0, 0))] * OWNERS
+        in_specs=[pl.BlockSpec((2, 5, HELD, LANES), lambda g: (0, 0, 0, 0))] * (OWNERS // 2)
         + [pl.BlockSpec((ROWS, OWNERS * LANES), lambda g: (0, 0))] * 3,
         out_specs=[pl.BlockSpec((size, LANES), lambda g: (0, 0))] * 2,
         compiler_params=params(6),
@@ -251,15 +269,14 @@
     drive_row = jnp.zeros((8, MEMBERS), F32)
     nothing = jnp.zeros((8, LANES), F32)
     for i in range(OWNERS):
-        at = lax.rem(own + i, OWNERS)
         for g in range(4):
-            rows = parts_ref[at, 8 * g : 8 * g + 8]
+            rows = parts_ref[i, 8 * g : 8 * g + 8]
             rows = jnp.where(lane < HELD, 0.5 * rows, rows)
-            fifth = turned(parts_ref[at, 40:48], -HELD * g)
+            fifth = turned(parts_ref[i, 40:48], -HELD * g)
             fifth = jnp.where(lane < HELD, 0.5 * fifth, 0.0)
             line = jnp.concatenate([rows, fifth], axis=1)
             half_ref[i * HELD + 8 * g : i * HELD + 8 * g + 8] = pltpu.roll(line, HELD * i, 1)
-        drive = jnp.where(lane < HELD, parts_ref[at, 32:40], 0.0)
+        drive = jnp.where(lane < HELD, parts_ref[relative(own, i), 32:40], 0.0)
         line = jnp.concatenate([drive, nothing], axis=1)
         drive_row += pltpu.roll(line, HELD * i, 1)
     half = half_ref[...]
@@ -282,6 +299,13 @@
         lower_parts = thirds(lower)
     middle = 1.5 * identity - 0.5 * three_products(lower_parts, thirds(upper))
     root = six_products(thirds(middle), lower_parts) / jnp.sqrt(norm)
+
+    def rows_in_order(matrix):
+        half_ref[...] = matrix
+        starts = [pl.multiple_of(relative(own, i) * HELD, HELD) for i in range(OWNERS)]
+        return jnp.concatenate([half_ref[pl.ds(start, HELD)] for start in starts], axis=0)
+
+    root = rows_in_order(rows_in_order(root).T)
     weights = dot(dot(drive_row, root, ((1,), (1,))), root, ((1,), (1,)))
     out_ref[...] = root + weights[0:1] / jnp.sqrt(F32(MEMBERS - 1))
 
@@ -367,9 +391,10 @@
 
 def analyse_kernel(*refs):
     place_ref, ksat_ref, storage_ref, recharge_ref, transform_ref = refs[:5]
-    piece_refs = refs[5 : 5 + OWNERS]
-    above_ref, below_ref, field_ref, edge_field_ref = refs[5 + OWNERS : 9 + OWNERS]
-    out_refs = refs[9 + OWNERS :]
+    chips = OWNERS // 2
+    piece_refs = refs[5 : 5 + chips]
+    above_ref, below_ref, field_ref, edge_field_ref = refs[5 + chips : 9 + chips]
+    out_refs = refs[9 + chips :]
     spread_fields(
         place_ref, ksat_ref, storage_ref, recharge_ref, above_ref, below_ref, field_ref, edge_field_ref
     )
@@ -387,7 +412,7 @@
             return border(below_ref, unit - SENT_ROWS - 2)
         if unit >= SENT_ROWS:
             return border(above_ref, unit - SENT_ROWS + 1)
-        found = joined(lambda i: piece_refs[i][PLACE[unit]])
+        found = joined(lambda i: piece_refs[i // 2][i % 2, PLACE[unit]])
         if unit == EDGE:
             top = border(above_ref, 0)
             bottom = border(below_ref, 2)
@@ -422,7 +447,7 @@
         analyse_kernel,
         out_shape=[shape(5, FIELD_ROWS, 8, LANES), shape(6, 8, LANES)]
         + [shape(UNITS, HELD, LANES)] * OWNERS,
-        in_specs=[SCALARS] + whole(6 + OWNERS),
+        in_specs=[SCALARS] + whole(6 + OWNERS // 2),
         out_specs=whole(2 + OWNERS),
         compiler_params=params(14),
         name="analyse",
@@ -461,7 +486,7 @@
 
     def one_batch(which, batch, carry):
         cells_ref, out_ref = cells_refs[which], out_refs[which]
-        owner = lax.rem(own + shifts[which], OWNERS)
+        owner = relative(own, shifts[which])
         first_member = owner * HELD + batch * BATCH
         most = counts_ref[first_member]
         for n in range(1, BATCH):
@@ -607,8 +632,7 @@
     def column(step, place_ref):
         block = jnp.int32(0)
         for n, shift in enumerate(shifts):
-            own = place_ref[0] - shift + OWNERS
-            block = jnp.where(step == n, lax.rem(own, OWNERS), block)
+            block = jnp.where(step == n, relative(place_ref[0], shift, -1), block)
         return 0, block
 
     extra = [] if begun is None else [begun]
@@ -640,6 +664,12 @@
     return lax.ppermute(array, axis, [(i, (i + step) % peers) for i in range(peers)])
 
 
+def to_owner(array, place):
+    chips = OWNERS // 2
+    pairs = [(i, 2 * ((i // 2 + place // 2) % chips) + (i % 2 ^ place % 2)) for i in range(OWNERS)]
+    return lax.ppermute(array, MEMBER, pairs)
+
+
 def to_strips_beside(array, step):
     peers = lax.axis_size(SPACE)
     pairs = [(i, i + step) for i in range(peers) if 0 <= i + step < peers]
@@ -658,19 +688,16 @@
     seen = observed(flat, obs_index[None], lax.axis_size(MEMBER[0]))
     same = exchanged(seen, MEMBER[0])
 
-    blocks = packed_blocks(place, flat, seen)
+    kept, given = packed_blocks(place, flat, seen)
     wide_counts = jnp.broadcast_to(newton_counts[:, None], (MEMBERS, LANES))
-    same, blocks, wide_counts = lax.optimization_barrier((same, blocks, wide_counts))
+    same, kept, given, wide_counts = lax.optimization_barrier((same, kept, given, wide_counts))
     other = along(same, MEMBER[1], 1)
-
-    pieces = [blocks[0]] + [None] * (OWNERS - 1)
-    for i in (2, 6, 3, 5):
-        pieces[i] = along(blocks[i], MEMBER, -i)
+    taken = along(given, MEMBER[1], 1)
+    joint = [jnp.stack([kept[n], taken[n]]) for n in range(OWNERS // 2)]
+
+    pieces = [joint[0]] + [along(joint[n], MEMBER[0], -n) for n in range(1, OWNERS // 2)]
     copies = lax.axis_size(SPACE[0])
     part = gram_blocks(place, same, other, obs_value[None], obs_scale[None], copies)
-    part, blocks = lax.optimization_barrier((part, blocks))
-    for i in (4, 1, 7):
-        pieces[i] = along(blocks[i], MEMBER, -i)
     part = jnp.sum(exchanged(part, SPACE[0]), axis=0)
     part = jnp.sum(shared(part, SPACE[1]), axis=0)
     parts = shared(part, MEMBER)
@@ -683,14 +710,14 @@
     fields, edge_fields, cells = analysed(place, cell_fields, transform, pieces, above, below)
 
     arrived = [None] * OWNERS
-    for shifts in ((2,), (6,), (3, 5), (4, 1), (7, 0)):
+    for shifts in ((2,), (6,), (4, 5), (3, 7), (1, 0)):
         moved = forecasts(
             shifts, place, newton_counts, wide_counts, fields, edge_fields, [cells[i] for i in shifts]
         )
         moved, cells = lax.optimization_barrier((moved, cells))
         for i, field in zip(shifts, moved):
-            arrived[i] = along(field, MEMBER, i) if i else field
-    early, late = (0, 2, 6, 3, 5), (4, 1, 7)
+            arrived[i] = to_owner(field, i) if i else field
+    early, late = (0, 2, 6, 4, 5), (3, 7, 1)
     result = unpacked(place, early, [arrived[i] for i in early])
     result = unpacked(place, late, [arrived[i] for i in late], result)
     return result.reshape(members, rows, columns)

time: 137 us -> 129 us (0.942); the launches traced: 134 us -> 128 us
  waiting for transfers between devices: 26.8 us -> 20.6 us
  starting transfers between devices: 44.7 us -> 41.1 us
  other arithmetic: 0.1 us -> 2.66 us
    ppermute x15 -> x5, starting transfers between devices: 20.4 us -> 4.42 us  [along(): lax.ppermute(array, axis, [(i, (i + step) % peers) for i in range(peers)])]
    ppermute x0 -> x7, starting transfers between devices: none -> 9.95 us  [to_owner(): return lax.ppermute(array, MEMBER, pairs)]
    ppermute x15 -> x5, waiting for transfers between devices: 18.4 us -> 9.73 us  [along(): lax.ppermute(array, axis, [(i, (i + step) % peers) for i in range(peers)])]
    ppermute x0 -> x7, waiting for transfers between devices: none -> 3.76 us  [to_owner(): return lax.ppermute(array, MEMBER, pairs)]
    another operation x0 -> x4, other arithmetic: none -> 2.56 us  [on_device(): joint = [jnp.stack([kept[n], taken[n]]) for n in range(OWNERS // 2)]]
    all_to_all x3, starting transfers between devices: 16.7 us -> 19.2 us  [exchanged(): return lax.all_to_all(copies, axis, split_axis=0, concat_axis=0, tiled=True)]
    unnamed x28 -> x22, local copies, waits for them, and re-layouts: 4.5 us -> 4.06 us
  transfers between devices with their start and end apart: 20 -> 17, of which waited for: 7 -> 6; matrix products, arithmetic and copies ran while one was open for 1% -> 4% of each run, Pallas kernels for 25% -> 27%
where the time goes in v4:
time: 129 us; the launch traced here: 128 us
  Pallas kernels  48 us (37%)
  starting transfers between devices  41.1 us (32%)
  waiting for transfers between devices  20.6 us (16%)
  blocking collectives  8.9 us (7%)
  local copies, waits for them, and re-layouts  6.22 us (5%)
  other arithmetic  2.66 us (2%)
    pallas_call x5, Pallas kernels, forecasts(): pl.pallas_call(functools.partial(forecast_kernel, shifts), out_shape=[sha...  19.5 us
    all_to_all x3, starting transfers between devices, exchanged(): return lax.all_to_all(copies, axis, split_axis=0, concat_axis=0, tiled=True)  19.2 us
    pallas_call x1, Pallas kernels, transform_of(): pl.pallas_call(root_kernel, out_shape=shape(MEMBERS, MEMBERS), in_specs=[...  12 us
    ppermute x7, starting transfers between devices, to_owner(): return lax.ppermute(array, MEMBER, pairs)  9.95 us
    ppermute x5, waiting for transfers between devices, along(): lax.ppermute(array, axis, [(i, (i + step) % peers) for i in range(peers)])  9.73 us
    all_to_all x1, blocking collectives, exchanged(): return lax.all_to_all(copies, axis, split_axis=0, concat_axis=0, tiled=True)  8.9 us
    ppermute x2, starting transfers between devices, to_strips_beside(): return lax.ppermute(array, SPACE, pairs)  7.56 us
    all_to_all x3, waiting for transfers between devices, exchanged(): return lax.all_to_all(copies, axis, split_axis=0, concat_axis=0, tiled=True)  7.08 us
  transfers between devices with their start and end apart: 17, of which 6 were waited for; matrix products, arithmetic and copies ran while one was open for 4% of the time, Pallas kernels for 27%

profile of v4, /device:TPU:33, one launch (start us, length us, event | category | flops | bytes accessed | tf_op | source)
XLA Modules:
  0.0 127.7 jit_solution(14834763397522435943)
XLA Ops:
  2.3 4.5 %observe.1.after_ref = f32[4,32,1024]{2,1,0:T(8,128)} custom-call(s32[1,1024]{1,0:T(1,128)S(1)} %bitcast.10, f32[512,1024]{1,0:T(8,128)S(1)} %bitcast.8), custom_call_target="tpu_custom_call" | custom-call | tf_op jit(solution)/shard_map/observe/pallas_call | solution.py:88
  6.7 4.2 %all-to-all-start = ((f32[4,32,1024]{2,1,0:T(8,128)}), f32[4,32,1024]{2,1,0:T(8,128)}, u32[]{:S(2)}, u32[]{:S(2)}) async-start(f32[4,32,1024]{2,1,0:T(8,128)} %observe.1.after_ref), calls=%async_computation | async-start | bytes 1048576 | tf_op jit(solution)/shard_map/all_to_all | solution.py:655
  11.0 2.4 %pack.1 = (f32[4,17,32,128]{3,2,1,0:T(8,128)S(1)}, f32[4,17,32,128]{3,2,1,0:T(8,128)S(1)}) custom-call(s32[3]{0:T(128)S(1)} %pad_add_fusion.place_ref.refs_0_, f32[512,1024]{1,0:T(8,128)S(1)} %bitcast.9, f32[4,32,1024]{2,1,0:T(8,128)} %observe.1.after_ref), custom_call_target="tpu_custom_call" | custom-call | tf_op jit(solution)/shard_map/pack/pallas_call | solution.py:162
  14.4 4.9 %all-to-all-done.same_ref = f32[4,32,1024]{2,1,0:T(8,128)} async-done(((f32[4,32,1024]{2,1,0:T(8,128)}), f32[4,32,1024]{2,1,0:T(8,128)}, u32[]{:S(2)}, u32[]{:S(2)}) %all-to-all-start) | async-done | bytes 524320 | tf_op jit(solution)/shard_map/all_to_all | solution.py:655
  19.4 2.2 %collective-permute-start = (f32[4,32,1024]{2,1,0:T(8,128)}, f32[4,32,1024]{2,1,0:T(8,128)S(1)}, u32[]{:S(2)}, u32[]{:S(2)}) collective-permute-start(f32[4,32,1024]{2,1,0:T(8,128)} %all-to-all-done.same_ref), channel_id=1, source_target_pairs={{0,32},{32,0},{1,33},{33,1},{2,34},{34,2},{3,35},{35,3},{4,36},{36... | collective-permute-start | bytes 1572872 | tf_op jit(solution)/shard_map/ppermute | solution.py:664
  23.4 2.6 %gram.1 = f32[8,48,128]{2,1,0:T(8,128)} custom-call(s32[3]{0:T(128)S(1)} %pad_add_fusion.place_ref.refs_0_, f32[4,32,1024]{2,1,0:T(8,128)} %all-to-all-done.same_ref, f32[4,32,1024]{2,1,0:T(8,128)S(1)} %collective-permute-done.other_ref, f32[1,1024]{1,0:T(1,128)S(1)} %bitcast.11, f32[1,1024]{1,0:T(1,128)S(1)} %bitcast.12), custom_call_target="tpu_custom_call" | custom-call | flops 10000000000 | bytes 1000000 | tf_op jit(solution)/shard_map/gram/pallas_call | solution.py:233
  26.1 8.0 %all-to-all-start.1 = ((f32[8,48,128]{2,1,0:T(8,128)}), f32[8,48,128]{2,1,0:T(8,128)S(1)}, u32[]{:S(2)}, u32[]{:S(2)}) async-start(f32[8,48,128]{2,1,0:T(8,128)} %gram.1), calls=%async_computation.1 | async-start | bytes 393216 | tf_op jit(solution)/shard_map/all_to_all | solution.py:655
  41.8 8.9 %all_to_all.20 = f32[4,48,128]{2,1,0:T(8,128)S(1)} all-to-all(f32[4,48,128]{2,1,0:T(8,128)S(1)} %broadcast_in_dim.25), channel_id=1, replica_groups=mesh['member_0'=4,'member_1'=2,'space_0'=8,'space_1'=4] {'space_1'}, dimensions={0} | all-to-all | bytes 196608 | tf_op jit(solution)/shard_map/all_to_all | solution.py:655
  51.4 7.0 %all-to-all-start.3 = ((f32[8,48,128]{2,1,0:T(8,128)}), f32[8,48,128]{2,1,0:T(8,128)S(1)}, u32[]{:S(2)}, u32[]{:S(2)}) async-start(f32[8,48,128]{2,1,0:T(8,128)} %broadcast_in_dim.26), calls=%async_computation.3 | async-start | bytes 393216 | tf_op jit(solution)/shard_map/all_to_all | solution.py:655
  58.5 8.2 %collective-permute-done.4.refs_3_.refs_8_ = f32[2,17,32,128]{3,2,1,0:T(8,128)S(1)} collective-permute-done((f32[2,17,32,128]{3,2,1,0:T(8,128)}, f32[2,17,32,128]{3,2,1,0:T(8,128)S(1)}, u32[]{:S(2)}, u32[]{:S(2)}) %collective-permute-start.4) | collective-permute-done | bytes 557088 | tf_op jit(solution)/shard_map/ppermute | solution.py:664
  67.8 3.1 %collective-permute-start.5 = (f32[816,128]{1,0:T(8,128)}, f32[816,128]{1,0:T(8,128)S(1)}, u32[]{:S(2)}, u32[]{:S(2)}) collective-permute-start(f32[816,128]{1,0:T(8,128)} %copy-done.8), channel_id=1, source_target_pairs={{0,1},{1,2},{2,3},{3,4},{4,5},{5,6},{6,7},{7,8},{8,9},{9,10},{10,1... | collective-permute-start | bytes 1253384 | tf_op jit(solution)/shard_map/ppermute | solution.py:676
  70.9 4.5 %collective-permute-start.6 = (f32[816,128]{1,0:T(8,128)S(1)}, f32[816,128]{1,0:T(8,128)S(1)}, u32[]{:S(2)}, u32[]{:S(2)}) collective-permute-start(f32[816,128]{1,0:T(8,128)S(1)} %get-tuple-element.69), channel_id=1, source_target_pairs={{1,0},{2,1},{3,2},{4,3},{5,4},{6,5},{7,6},{8,7},{9,8},{10,9},{11,1... | collective-permute-start | bytes 1253384 | tf_op jit(solution)/shard_map/ppermute | solution.py:676
  75.4 12.0 %root.1.refs_4_ = f32[256,256]{1,0:T(8,128)S(1)} custom-call(s32[3]{0:T(128)S(1)} %pad_add_fusion.place_ref.refs_0_, f32[8,48,128]{2,1,0:T(8,128)S(1)} %all-to-all-done.3.parts_ref), custom_call_target="tpu_custom_call" | custom-call | flops 10000000000 | bytes 1000000 | tf_op jit(solution)/shard_map/root/pallas_call | solution.py:314
  87.4 2.1 %analyse.1 = (f32[5,20,8,128]{3,2,1,0:T(8,128)S(1)}, f32[6,8,128]{2,1,0:T(8,128)S(1)}, f32[21,32,128]{2,1,0:T(8,128)S(1)}, f32[21,32,128]{2,1,0:T(8,128)S(1)}, f...) custom-call(s32[3]{0:T(128)S(1)} %pad_add_fusion.place_ref.refs_0_, ...), custom_call_target="tpu_custom_call" | custom-call | tf_op jit(solution)/shard_map/analyse/pallas_call | solution.py:446
  89.5 2.4 %forecast.5 = f32[512,128]{1,0:T(8,128)S(1)} custom-call(s32[3]{0:T(128)S(1)} %pad_add_fusion.place_ref.refs_0_, s32[256]{0:T(256)S(1)} %copy-done.5, s32[256,128]{1,0:T(8,128)S(1)} %broadcast_in_dim.22.wide_ref, f32[5,20,8,128]{3,2,1,0:T(8,128)S(1)} %get-tuple-element.70.field_ref, f32[6,8,128]{2,1,0:T(8,128)S(1)} %get-tuple-element.71.edge_field_ref, ...), custom_call_target="tpu_custom_call" | custom-call | flops 1 | bytes 1 | tf_op jit(solution)/shard_map/forecast/pallas_call | solution.py:603
  91.9 2.4 %forecast.6 = f32[512,128]{1,0:T(8,128)S(1)} custom-call(s32[3]{0:T(128)S(1)} %pad_add_fusion.place_ref.refs_0_, s32[256]{0:T(256)S(1)} %copy-done.5, s32[256,128]{1,0:T(8,128)S(1)} %broadcast_in_dim.22.wide_ref, f32[5,20,8,128]{3,2,1,0:T(8,128)S(1)} %get-tuple-element.70.field_ref, f32[6,8,128]{2,1,0:T(8,128)S(1)} %get-tuple-element.71.edge_field_ref, ...), custom_call_target="tpu_custom_call" | custom-call | flops 1 | bytes 1 | tf_op jit(solution)/shard_map/forecast/pallas_call | solution.py:603
  95.8 6.5 %forecast.7 = (f32[512,128]{1,0:T(8,128)S(1)}, f32[512,128]{1,0:T(8,128)S(1)}) custom-call(s32[3]{0:T(128)S(1)} %pad_add_fusion.place_ref.refs_0_, s32[256]{0:T(256)S(1)} %copy-done.5, s32[256,128]{1,0:T(8,128)S(1)} %broadcast_in_dim.22.wide_ref, f32[5,20,8,128]{3,2,1,0:T(8,128)S(1)} %get-tuple-element.70.field_ref, ...), custom_call_target="tpu_custom_call" | custom-call | flops 1 | bytes 1 | tf_op jit(solution)/shard_map/forecast/pallas_call | solution.py:603
  102.4 5.2 %collective-permute-start.13 = (f32[512,128]{1,0:T(8,128)S(1)}, f32[512,128]{1,0:T(8,128)S(1)}, u32[]{:S(2)}, u32[]{:S(2)}) collective-permute-start(f32[512,128]{1,0:T(8,128)S(1)} %get-tuple-element.112), channel_id=1, source_target_pairs={{0,160},{32,128},{64,224},{96,192},{128,32},{160,0},{192,96},{224,... | collective-permute-start | bytes 786440 | tf_op jit(solution)/shard_map/ppermute | solution.py:670
  107.6 4.2 %forecast.8 = (f32[512,128]{1,0:T(8,128)S(1)}, f32[512,128]{1,0:T(8,128)S(1)}) custom-call(s32[3]{0:T(128)S(1)} %pad_add_fusion.place_ref.refs_0_, s32[256]{0:T(256)S(1)} %copy-done.5, s32[256,128]{1,0:T(8,128)S(1)} %broadcast_in_dim.22.wide_ref, f32[5,20,8,128]{3,2,1,0:T(8,128)S(1)} %get-tuple-element.70.field_ref, ...), custom_call_target="tpu_custom_call" | custom-call | flops 1 | bytes 1 | tf_op jit(solution)/shard_map/forecast/pallas_call | solution.py:603
  111.8 4.2 %forecast.9 = (f32[512,128]{1,0:T(8,128)S(1)}, f32[512,128]{1,0:T(8,128)S(1)}) custom-call(s32[3]{0:T(128)S(1)} %pad_add_fusion.place_ref.refs_0_, s32[256]{0:T(256)S(1)} %copy-done.5, s32[256,128]{1,0:T(8,128)S(1)} %broadcast_in_dim.22.wide_ref, f32[5,20,8,128]{3,2,1,0:T(8,128)S(1)} %get-tuple-element.70.field_ref, ...), custom_call_target="tpu_custom_call" | custom-call | flops 1 | bytes 1 | tf_op jit(solution)/shard_map/forecast/pallas_call | solution.py:603
  116.1 2.9 %collective-permute-start.8 = (f32[512,128]{1,0:T(8,128)S(1)}, f32[512,128]{1,0:T(8,128)S(1)}, u32[]{:S(2)}, u32[]{:S(2)}) collective-permute-start(f32[512,128]{1,0:T(8,128)S(1)} %get-tuple-element.102), channel_id=1, source_target_pairs={{0,224},{32,192},{64,32},{96,0},{128,96},{160,64},{192,160},{224,1... | collective-permute-start | bytes 786440 | tf_op jit(solution)/shard_map/ppermute | solution.py:670
  119.1 2.8 %unpack.2.refs_3_ = f32[512,1024]{1,0:T(8,128)} custom-call(s32[3]{0:T(128)S(1)} %pad_add_fusion.place_ref.refs_0_, f32[512,128]{1,0:T(8,128)S(1)} %get-tuple-element.108.refs_0_, f32[512,128]{1,0:T(8,128)S(1)} %collective-permute-done.10.refs_1_, f32[512,128]{1,0:T(8,128)S(1)} %collective-permute-done.11.refs_2_, ...), custom_call_target="tpu_custom_call" | custom-call | tf_op jit(solution)/shard_map/unpack/pallas_call | solution.py:639
  121.9 3.7 %collective-permute-done.7.refs_0_ = f32[512,128]{1,0:T(8,128)S(1)} collective-permute-done((f32[512,128]{1,0:T(8,128)S(1)}, f32[512,128]{1,0:T(8,128)S(1)}, u32[]{:S(2)}, u32[]{:S(2)}) %collective-permute-start.7) | collective-permute-done | bytes 262176 | tf_op jit(solution)/shard_map/ppermute | solution.py:670
  125.7 2.1 %unpack.3 = f32[512,1024]{1,0:T(8,128)} custom-call(s32[3]{0:T(128)S(1)} %pad_add_fusion.place_ref.refs_0_, f32[512,128]{1,0:T(8,128)S(1)} %collective-permute-done.7.refs_0_, f32[512,128]{1,0:T(8,128)S(1)} %collective-permute-done.8.refs_1_, f32[512,128]{1,0:T(8,128)S(1)} %collective-permute-done.9.refs_2_, ...), custom_call_target="tpu_custom_call", output_to_operand_aliasing={{}: (4, {})} | custom-call | tf_op jit(solution)/shard_map/unpack/pallas_call | solution.py:639
  (58 shorter events, 16.7 us)
Async XLA Ops:
  2.3 8.7 %copy-start.1 = (f32[32,16,1024]{2,1,0:T(8,128)S(1)}, f32[32,16,1024]{2,1,0:T(8,128)}, u32[]{:S(2)}) copy-start(f32[32,16,1024]{2,1,0:T(8,128)} %param.8) | copy-start | bytes 6291460
  6.7 12.6 %all-to-all-start = ((f32[4,32,1024]{2,1,0:T(8,128)}), f32[4,32,1024]{2,1,0:T(8,128)}, u32[]{:S(2)}, u32[]{:S(2)}) async-start(f32[4,32,1024]{2,1,0:T(8,128)} %observe.1.after_ref), calls=%async_computation | async-start | bytes 1048576 | tf_op jit(solution)/shard_map/all_to_all | solution.py:655
  11.0 8.3 %copy-start.5 = (s32[256]{0:T(256)S(1)}, s32[256]{0:T(256)}, u32[]{:S(2)}) copy-start(s32[256]{0:T(256)} %counts_ref.9) | copy-start | bytes 3076
  19.4 4.0 %copy-start.9 = (f32[1024]{0:T(1024)S(1)}, f32[1024]{0:T(1024)}, u32[]{:S(2)}) copy-start(f32[1024]{0:T(1024)} %param.10) | copy-start | bytes 12292
  19.4 4.0 %copy-start.10 = (f32[1024]{0:T(1024)S(1)}, f32[1024]{0:T(1024)}, u32[]{:S(2)}) copy-start(f32[1024]{0:T(1024)} %param.11) | copy-start | bytes 12292
  19.4 4.0 %collective-permute-start = (f32[4,32,1024]{2,1,0:T(8,128)}, f32[4,32,1024]{2,1,0:T(8,128)S(1)}, u32[]{:S(2)}, u32[]{:S(2)}) collective-permute-start(f32[4,32,1024]{2,1,0:T(8,128)} %all-to-all-done.same_ref), channel_id=1, source_target_pairs={{0,32},{32,0},{1,33},{33,1},{2,34},{34,2},{3,35},{35,3},{4,36},{36... | collective-permute-start | bytes 1572872 | tf_op jit(solution)/shard_map/ppermute | solution.py:664
  21.7 12.4 %collective-permute-start.1 = (f32[4,17,32,128]{3,2,1,0:T(8,128)}, f32[4,17,32,128]{3,2,1,0:T(8,128)}, u32[]{:S(2)}, u32[]{:S(2)}) collective-permute-start(f32[4,17,32,128]{3,2,1,0:T(8,128)} %copy-done.7), channel_id=1, source_target_pairs={{0,32},{32,0},{1,33},{33,1},{2,34},{34,2},{3,35},{35,3},{4,36},{36... | collective-permute-start | bytes 3342344 | tf_op jit(solution)/shard_map/ppermute | solution.py:664
  26.1 15.7 %all-to-all-start.1 = ((f32[8,48,128]{2,1,0:T(8,128)}), f32[8,48,128]{2,1,0:T(8,128)S(1)}, u32[]{:S(2)}, u32[]{:S(2)}) async-start(f32[8,48,128]{2,1,0:T(8,128)} %gram.1), calls=%async_computation.1 | async-start | bytes 393216 | tf_op jit(solution)/shard_map/all_to_all | solution.py:655
  36.2 22.3 %collective-permute-start.2 = (f32[2,17,32,128]{3,2,1,0:T(8,128)}, f32[2,17,32,128]{3,2,1,0:T(8,128)S(1)}, u32[]{:S(2)}, u32[]{:S(2)}) collective-permute-start(f32[2,17,32,128]{3,2,1,0:T(8,128)} %pad_maximum_fusion.1), channel_id=1, source_target_pairs={{0,192},{64,0},{128,64},{192,128},{1,193},{65,1},{129,65},{193,129... | collective-permute-start | bytes 1671176 | tf_op jit(solution)/shard_map/ppermute | solution.py:664
  37.9 20.6 %collective-permute-start.3 = (f32[2,17,32,128]{3,2,1,0:T(8,128)}, f32[2,17,32,128]{3,2,1,0:T(8,128)S(1)}, u32[]{:S(2)}, u32[]{:S(2)}) collective-permute-start(f32[2,17,32,128]{3,2,1,0:T(8,128)} %pad_maximum_fusion.2), channel_id=1, source_target_pairs={{0,128},{64,192},{128,0},{192,64},{1,129},{65,193},{129,1},{193,65... | collective-permute-start | bytes 1671176 | tf_op jit(solution)/shard_map/ppermute | solution.py:664
  40.0 26.7 %collective-permute-start.4 = (f32[2,17,32,128]{3,2,1,0:T(8,128)}, f32[2,17,32,128]{3,2,1,0:T(8,128)S(1)}, u32[]{:S(2)}, u32[]{:S(2)}) collective-permute-start(f32[2,17,32,128]{3,2,1,0:T(8,128)} %pad_maximum_fusion.3), channel_id=1, source_target_pairs={{0,64},{64,128},{128,192},{192,0},{1,65},{65,129},{129,193},{193,1... | collective-permute-start | bytes 1671176 | tf_op jit(solution)/shard_map/ppermute | solution.py:664
  41.8 24.9 %copy-start.2 = (f32[16,1024]{1,0:T(8,128)S(1)}, f32[16,1024]{1,0:T(8,128)}, u32[]{:S(2)}) copy-start(f32[16,1024]{1,0:T(8,128)} %refs_1_.1) | copy-start | bytes 196612
  41.8 24.8 %copy-start.3 = (f32[16,1024]{1,0:T(8,128)S(1)}, f32[16,1024]{1,0:T(8,128)}, u32[]{:S(2)}) copy-start(f32[16,1024]{1,0:T(8,128)} %refs_2_.1) | copy-start | bytes 196612
  41.8 24.8 %copy-start.4 = (f32[16,1024]{1,0:T(8,128)S(1)}, f32[16,1024]{1,0:T(8,128)}, u32[]{:S(2)}) copy-start(f32[16,1024]{1,0:T(8,128)} %refs_3_.1) | copy-start | bytes 196612
  51.4 16.4 %all-to-all-start.3 = ((f32[8,48,128]{2,1,0:T(8,128)}), f32[8,48,128]{2,1,0:T(8,128)S(1)}, u32[]{:S(2)}, u32[]{:S(2)}) async-start(f32[8,48,128]{2,1,0:T(8,128)} %broadcast_in_dim.26), calls=%async_computation.3 | async-start | bytes 393216 | tf_op jit(solution)/shard_map/all_to_all | solution.py:655
  67.8 19.6 %collective-permute-start.5 = (f32[816,128]{1,0:T(8,128)}, f32[816,128]{1,0:T(8,128)S(1)}, u32[]{:S(2)}, u32[]{:S(2)}) collective-permute-start(f32[816,128]{1,0:T(8,128)} %copy-done.8), channel_id=1, source_target_pairs={{0,1},{1,2},{2,3},{3,4},{4,5},{5,6},{6,7},{7,8},{8,9},{9,10},{10,1... | collective-permute-start | bytes 1253384 | tf_op jit(solution)/shard_map/ppermute | solution.py:676
  70.9 16.5 %collective-permute-start.6 = (f32[816,128]{1,0:T(8,128)S(1)}, f32[816,128]{1,0:T(8,128)S(1)}, u32[]{:S(2)}, u32[]{:S(2)}) collective-permute-start(f32[816,128]{1,0:T(8,128)S(1)} %get-tuple-element.69), channel_id=1, source_target_pairs={{1,0},{2,1},{3,2},{4,3},{5,4},{6,5},{7,6},{8,7},{9,8},{10,9},{11,1... | collective-permute-start | bytes 1253384 | tf_op jit(solution)/shard_map/ppermute | solution.py:676
  94.2 21.8 %collective-permute-start.11 = (f32[512,128]{1,0:T(8,128)S(1)}, f32[512,128]{1,0:T(8,128)S(1)}, u32[]{:S(2)}, u32[]{:S(2)}) collective-permute-start(f32[512,128]{1,0:T(8,128)S(1)} %forecast.6), channel_id=1, source_target_pairs={{0,192},{32,224},{64,0},{96,32},{128,64},{160,96},{192,128},{224,1... | collective-permute-start | bytes 786440 | tf_op jit(solution)/shard_map/ppermute | solution.py:670
  95.7 20.5 %collective-permute-start.10 = (f32[512,128]{1,0:T(8,128)S(1)}, f32[512,128]{1,0:T(8,128)S(1)}, u32[]{:S(2)}, u32[]{:S(2)}) collective-permute-start(f32[512,128]{1,0:T(8,128)S(1)} %forecast.5), channel_id=1, source_target_pairs={{0,64},{32,96},{64,128},{96,160},{128,192},{160,224},{192,0},{224,... | collective-permute-start | bytes 786440 | tf_op jit(solution)/shard_map/ppermute | solution.py:670
  102.3 16.8 %collective-permute-start.12 = (f32[512,128]{1,0:T(8,128)S(1)}, f32[512,128]{1,0:T(8,128)S(1)}, u32[]{:S(2)}, u32[]{:S(2)}) collective-permute-start(f32[512,128]{1,0:T(8,128)S(1)} %get-tuple-element.111), channel_id=1, source_target_pairs={{0,128},{32,160},{64,192},{96,224},{128,0},{160,32},{192,64},{224,... | collective-permute-start | bytes 786440 | tf_op jit(solution)/shard_map/ppermute | solution.py:670
  102.4 16.7 %collective-permute-start.13 = (f32[512,128]{1,0:T(8,128)S(1)}, f32[512,128]{1,0:T(8,128)S(1)}, u32[]{:S(2)}, u32[]{:S(2)}) collective-permute-start(f32[512,128]{1,0:T(8,128)S(1)} %get-tuple-element.112), channel_id=1, source_target_pairs={{0,160},{32,128},{64,224},{96,192},{128,32},{160,0},{192,96},{224,... | collective-permute-start | bytes 786440 | tf_op jit(solution)/shard_map/ppermute | solution.py:670
  115.9 6.0 %collective-permute-start.9 = (f32[512,128]{1,0:T(8,128)S(1)}, f32[512,128]{1,0:T(8,128)S(1)}, u32[]{:S(2)}, u32[]{:S(2)}) collective-permute-start(f32[512,128]{1,0:T(8,128)S(1)} %get-tuple-element.107), channel_id=1, source_target_pairs={{0,32},{32,0},{64,96},{96,64},{128,160},{160,128},{192,224},{224,1... | collective-permute-start | bytes 786440 | tf_op jit(solution)/shard_map/ppermute | solution.py:670
  116.0 9.6 %collective-permute-start.7 = (f32[512,128]{1,0:T(8,128)S(1)}, f32[512,128]{1,0:T(8,128)S(1)}, u32[]{:S(2)}, u32[]{:S(2)}) collective-permute-start(f32[512,128]{1,0:T(8,128)S(1)} %get-tuple-element.101), channel_id=1, source_target_pairs={{0,96},{32,64},{64,160},{96,128},{128,224},{160,192},{192,32},{224... | collective-permute-start | bytes 786440 | tf_op jit(solution)/shard_map/ppermute | solution.py:670
  116.1 9.5 %collective-permute-start.8 = (f32[512,128]{1,0:T(8,128)S(1)}, f32[512,128]{1,0:T(8,128)S(1)}, u32[]{:S(2)}, u32[]{:S(2)}) collective-permute-start(f32[512,128]{1,0:T(8,128)S(1)} %get-tuple-element.102), channel_id=1, source_target_pairs={{0,224},{32,192},{64,32},{96,0},{128,96},{160,64},{192,160},{224,1... | collective-permute-start | bytes 786440 | tf_op jit(solution)/shard_map/ppermute | solution.py:670
  (4 other events, 4.0 us)

commit v5 on v4

--- a/solution.py
+++ b/solution.py
@@ -498,12 +498,14 @@
         def begun(level, flux, storage):
             bend = jnp.tanh(level)
             held = storage * bend
-            return level + DAMPING * flux / (1.0 + storage * (1.0 - bend * bend)), level + held + flux
+            derivative = (1.0 + storage) - held * bend
+            return level + DAMPING * flux / derivative, level + held + flux
 
         def swept(value, target, storage, sweep):
             bend = jnp.tanh(value)
-            derivative = 1.0 + storage * (1.0 - bend * bend)
-            moved = value - DAMPING * (value + storage * bend - target) / derivative
+            held = storage * bend
+            derivative = (1.0 + storage) - held * bend
+            moved = value - DAMPING * (value + held - target) / derivative
             return jnp.where(counts > sweep, moved, value)
 
         def unit_at(unit):
@@ -700,6 +702,7 @@
     part = gram_blocks(place, same, other, obs_value[None], obs_scale[None], copies)
     part = jnp.sum(exchanged(part, SPACE[0]), axis=0)
     part = jnp.sum(shared(part, SPACE[1]), axis=0)
+    part, pieces = lax.optimization_barrier((part, pieces))
     parts = shared(part, MEMBER)
     cell_fields = (ksat, storage, recharge)
     down, up = borders(pieces, cell_fields)
@@ -710,7 +713,7 @@
     fields, edge_fields, cells = analysed(place, cell_fields, transform, pieces, above, below)
 
     arrived = [None] * OWNERS
-    for shifts in ((2,), (6,), (4, 5), (3, 7), (1, 0)):
+    for shifts in ((2, 6), (4, 5), (3, 7), (1, 0)):
         moved = forecasts(
             shifts, place, newton_counts, wide_counts, fields, edge_fields, [cells[i] for i in shifts]
         )

time: 129 us -> 131 us (1.016)
  blocking collectives: 8.9 us -> 24.2 us
  starting transfers between devices: 41.1 us -> 35.9 us
  waiting for transfers between devices: 20.6 us -> 15.4 us
  Pallas kernels: 48 us -> 46.2 us
    all_to_all x1 -> x2, blocking collectives: 8.9 us -> 24.2 us  [exchanged(): return lax.all_to_all(copies, axis, split_axis=0, concat_axis=0, tiled=True)]
    ppermute x5, waiting for transfers between devices: 9.73 us -> 1.69 us  [along(): lax.ppermute(array, axis, [(i, (i + step) % peers) for i in range(peers)])]
    all_to_all x3 -> x2, starting transfers between devices: 19.2 us -> 12.7 us  [exchanged(): return lax.all_to_all(copies, axis, split_axis=0, concat_axis=0, tiled=True)]
    all_to_all x3 -> x2, waiting for transfers between devices: 7.08 us -> 9.98 us  [exchanged(): return lax.all_to_all(copies, axis, split_axis=0, concat_axis=0, tiled=True)]
    pallas_call x5 -> x4, Pallas kernels: 19.5 us -> 18.4 us  [forecasts(): pl.pallas_call(functools.partial(forecast_kernel, shifts), out_shape=[sha...]
    unnamed x22 -> x24, local copies, waits for them, and re-layouts: 4.06 us -> 4.06 us
  transfers between devices with their start and end apart: 17 -> 16, of which waited for: 6 -> 4; matrix products, arithmetic and copies ran while one was open for 4% -> 3% of each run, Pallas kernels for 27% -> 26%
where the time goes in v5:
time: 131 us; the launch traced here: 130 us
  Pallas kernels  46.2 us (35%)
  starting transfers between devices  35.9 us (27%)
  blocking collectives  24.2 us (18%)
  waiting for transfers between devices  15.4 us (12%)
  local copies, waits for them, and re-layouts  5.73 us (4%)
  other arithmetic  2.66 us (2%)
    all_to_all x2, blocking collectives, exchanged(): return lax.all_to_all(copies, axis, split_axis=0, concat_axis=0, tiled=True)  24.2 us
    pallas_call x4, Pallas kernels, forecasts(): pl.pallas_call(functools.partial(forecast_kernel, shifts), out_shape=[sha...  18.4 us
    all_to_all x2, starting transfers between devices, exchanged(): return lax.all_to_all(copies, axis, split_axis=0, concat_axis=0, tiled=True)  12.7 us
    pallas_call x1, Pallas kernels, transform_of(): pl.pallas_call(root_kernel, out_shape=shape(MEMBERS, MEMBERS), in_specs=[...  12 us
    ppermute x7, starting transfers between devices, to_owner(): return lax.ppermute(array, MEMBER, pairs)  11.2 us
    all_to_all x2, waiting for transfers between devices, exchanged(): return lax.all_to_all(copies, axis, split_axis=0, concat_axis=0, tiled=True)  9.98 us
    ppermute x2, starting transfers between devices, to_strips_beside(): return lax.ppermute(array, SPACE, pairs)  7.56 us
    pallas_call x2, Pallas kernels, unpacked(): pl.pallas_call(functools.partial(unpack_kernel, many), grid_spec=pltpu.Pr...  4.91 us
  transfers between devices with their start and end apart: 16, of which 4 were waited for; matrix products, arithmetic and copies ran while one was open for 3% of the time, Pallas kernels for 26%

profile of v5, /device:TPU:33, one launch (start us, length us, event | category | flops | bytes accessed | tf_op | source)
XLA Modules:
  0.0 130.4 jit_solution(2866445056625992519)
XLA Ops:
  2.3 4.5 %observe.1.after_ref = f32[4,32,1024]{2,1,0:T(8,128)} custom-call(s32[1,1024]{1,0:T(1,128)S(1)} %bitcast.10, f32[512,1024]{1,0:T(8,128)S(1)} %bitcast.8), custom_call_target="tpu_custom_call" | custom-call | tf_op jit(solution)/shard_map/observe/pallas_call | solution.py:88
  6.8 4.2 %all-to-all-start = ((f32[4,32,1024]{2,1,0:T(8,128)}), f32[4,32,1024]{2,1,0:T(8,128)}, u32[]{:S(2)}, u32[]{:S(2)}) async-start(f32[4,32,1024]{2,1,0:T(8,128)} %observe.1.after_ref), calls=%async_computation | async-start | bytes 1048576 | tf_op jit(solution)/shard_map/all_to_all | solution.py:657
  11.0 2.4 %pack.1 = (f32[4,17,32,128]{3,2,1,0:T(8,128)S(1)}, f32[4,17,32,128]{3,2,1,0:T(8,128)S(1)}) custom-call(s32[3]{0:T(128)S(1)} %pad_add_fusion.place_ref.refs_0_, f32[512,1024]{1,0:T(8,128)S(1)} %bitcast.9, f32[4,32,1024]{2,1,0:T(8,128)} %observe.1.after_ref), custom_call_target="tpu_custom_call" | custom-call | tf_op jit(solution)/shard_map/pack/pallas_call | solution.py:162
  14.4 4.9 %all-to-all-done.same_ref = f32[4,32,1024]{2,1,0:T(8,128)} async-done(((f32[4,32,1024]{2,1,0:T(8,128)}), f32[4,32,1024]{2,1,0:T(8,128)}, u32[]{:S(2)}, u32[]{:S(2)}) %all-to-all-start) | async-done | bytes 524320 | tf_op jit(solution)/shard_map/all_to_all | solution.py:657
  19.4 2.2 %collective-permute-start.1 = (f32[4,17,32,128]{3,2,1,0:T(8,128)}, f32[4,17,32,128]{3,2,1,0:T(8,128)S(1)}, u32[]{:S(2)}, u32[]{:S(2)}) collective-permute-start(f32[4,17,32,128]{3,2,1,0:T(8,128)} %copy-done.7), channel_id=1, source_target_pairs={{0,32},{32,0},{1,33},{33,1},{2,34},{34,2},{3,35},{35,3},{4,36},{36... | collective-permute-start | bytes 3342344 | tf_op jit(solution)/shard_map/ppermute | solution.py:666
  22.6 1.7 %collective-permute-done.1 = f32[4,17,32,128]{3,2,1,0:T(8,128)S(1)} collective-permute-done((f32[4,17,32,128]{3,2,1,0:T(8,128)}, f32[4,17,32,128]{3,2,1,0:T(8,128)S(1)}, u32[]{:S(2)}, u32[]{:S(2)}) %collective-permute-start.1) | collective-permute-done | bytes 1114144 | tf_op jit(solution)/shard_map/ppermute | solution.py:666
  29.0 1.9 %gram.1 = f32[8,48,128]{2,1,0:T(8,128)S(1)} custom-call(s32[3]{0:T(128)S(1)} %pad_add_fusion.place_ref.refs_0_, f32[4,32,1024]{2,1,0:T(8,128)} %all-to-all-done.same_ref, f32[4,32,1024]{2,1,0:T(8,128)S(1)} %collective-permute-done.other_ref, f32[1,1024]{1,0:T(1,128)S(1)} %bitcast.11, f32[1,1024]{1,0:T(1,128)S(1)} %bitcast.12), custom_call_target="tpu_custom_call" | custom-call | flops 10000000000 | bytes 1000000 | tf_op jit(solution)/shard_map/gram/pallas_call | solution.py:233
  30.9 15.6 %all_to_all.20 = f32[8,48,128]{2,1,0:T(8,128)S(1)} all-to-all(f32[8,48,128]{2,1,0:T(8,128)S(1)} %gram.1), channel_id=1, replica_groups=mesh['member_0'=4,'member_1'=2,'space_0'=8,'space_1'=4] {'space_0'}, dimensions={0} | all-to-all | bytes 393216 | tf_op jit(solution)/shard_map/all_to_all | solution.py:657
  46.6 8.6 %all_to_all.21 = f32[4,48,128]{2,1,0:T(8,128)S(1)} all-to-all(f32[4,48,128]{2,1,0:T(8,128)S(1)} %broadcast_in_dim.25), channel_id=1, replica_groups=mesh['member_0'=4,'member_1'=2,'space_0'=8,'space_1'=4] {'space_1'}, dimensions={0} | all-to-all | bytes 196608 | tf_op jit(solution)/shard_map/all_to_all | solution.py:657
  55.9 8.5 %all-to-all-start.3 = ((f32[8,48,128]{2,1,0:T(8,128)}), f32[8,48,128]{2,1,0:T(8,128)S(1)}, u32[]{:S(2)}, u32[]{:S(2)}) async-start(f32[8,48,128]{2,1,0:T(8,128)} %broadcast_in_dim.26), calls=%async_computation.3 | async-start | bytes 393216 | tf_op jit(solution)/shard_map/all_to_all | solution.py:657
  65.3 5.0 %all-to-all-done.3.parts_ref = f32[8,48,128]{2,1,0:T(8,128)S(1)} async-done(((f32[8,48,128]{2,1,0:T(8,128)}), f32[8,48,128]{2,1,0:T(8,128)S(1)}, u32[]{:S(2)}, u32[]{:S(2)}) %all-to-all-start.3) | async-done | bytes 196640 | tf_op jit(solution)/shard_map/all_to_all | solution.py:657
  70.4 2.2 %collective-permute-start.5 = (f32[816,128]{1,0:T(8,128)}, f32[816,128]{1,0:T(8,128)S(1)}, u32[]{:S(2)}, u32[]{:S(2)}) collective-permute-start(f32[816,128]{1,0:T(8,128)} %copy-done.8), channel_id=1, source_target_pairs={{0,1},{1,2},{2,3},{3,4},{4,5},{5,6},{6,7},{7,8},{8,9},{9,10},{10,1... | collective-permute-start | bytes 1253384 | tf_op jit(solution)/shard_map/ppermute | solution.py:678
  72.6 5.4 %collective-permute-start.6 = (f32[816,128]{1,0:T(8,128)S(1)}, f32[816,128]{1,0:T(8,128)S(1)}, u32[]{:S(2)}, u32[]{:S(2)}) collective-permute-start(f32[816,128]{1,0:T(8,128)S(1)} %get-tuple-element.74), channel_id=1, source_target_pairs={{1,0},{2,1},{3,2},{4,3},{5,4},{6,5},{7,6},{8,7},{9,8},{10,9},{11,1... | collective-permute-start | bytes 1253384 | tf_op jit(solution)/shard_map/ppermute | solution.py:678
  78.0 12.0 %root.1.refs_4_ = f32[256,256]{1,0:T(8,128)S(1)} custom-call(s32[3]{0:T(128)S(1)} %pad_add_fusion.place_ref.refs_0_, f32[8,48,128]{2,1,0:T(8,128)S(1)} %all-to-all-done.3.parts_ref), custom_call_target="tpu_custom_call" | custom-call | flops 10000000000 | bytes 1000000 | tf_op jit(solution)/shard_map/root/pallas_call | solution.py:314
  90.0 2.0 %analyse.1 = (f32[5,20,8,128]{3,2,1,0:T(8,128)S(1)}, f32[6,8,128]{2,1,0:T(8,128)S(1)}, f32[21,32,128]{2,1,0:T(8,128)S(1)}, f32[21,32,128]{2,1,0:T(8,128)S(1)}, f...) custom-call(s32[3]{0:T(128)S(1)} %pad_add_fusion.place_ref.refs_0_, ...), custom_call_target="tpu_custom_call" | custom-call | tf_op jit(solution)/shard_map/analyse/pallas_call | solution.py:446
  92.0 4.1 %forecast.4 = (f32[512,128]{1,0:T(8,128)S(1)}, f32[512,128]{1,0:T(8,128)S(1)}) custom-call(s32[3]{0:T(128)S(1)} %pad_add_fusion.place_ref.refs_0_, s32[256]{0:T(256)S(1)} %copy-done.5, s32[256,128]{1,0:T(8,128)S(1)} %broadcast_in_dim.22.wide_ref, f32[5,20,8,128]{3,2,1,0:T(8,128)S(1)} %get-tuple-element.75.field_ref, ...), custom_call_target="tpu_custom_call" | custom-call | flops 1 | bytes 1 | tf_op jit(solution)/shard_map/forecast/pallas_call | solution.py:605
  98.9 6.2 %forecast.5 = (f32[512,128]{1,0:T(8,128)S(1)}, f32[512,128]{1,0:T(8,128)S(1)}) custom-call(s32[3]{0:T(128)S(1)} %pad_add_fusion.place_ref.refs_0_, s32[256]{0:T(256)S(1)} %copy-done.5, s32[256,128]{1,0:T(8,128)S(1)} %broadcast_in_dim.22.wide_ref, f32[5,20,8,128]{3,2,1,0:T(8,128)S(1)} %get-tuple-element.75.field_ref, ...), custom_call_target="tpu_custom_call" | custom-call | flops 1 | bytes 1 | tf_op jit(solution)/shard_map/forecast/pallas_call | solution.py:605
  105.2 5.2 %collective-permute-start.13 = (f32[512,128]{1,0:T(8,128)S(1)}, f32[512,128]{1,0:T(8,128)S(1)}, u32[]{:S(2)}, u32[]{:S(2)}) collective-permute-start(f32[512,128]{1,0:T(8,128)S(1)} %get-tuple-element.112), channel_id=1, source_target_pairs={{0,160},{32,128},{64,224},{96,192},{128,32},{160,0},{192,96},{224,... | collective-permute-start | bytes 786440 | tf_op jit(solution)/shard_map/ppermute | solution.py:672
  110.4 4.1 %forecast.6 = (f32[512,128]{1,0:T(8,128)S(1)}, f32[512,128]{1,0:T(8,128)S(1)}) custom-call(s32[3]{0:T(128)S(1)} %pad_add_fusion.place_ref.refs_0_, s32[256]{0:T(256)S(1)} %copy-done.5, s32[256,128]{1,0:T(8,128)S(1)} %broadcast_in_dim.22.wide_ref, f32[5,20,8,128]{3,2,1,0:T(8,128)S(1)} %get-tuple-element.75.field_ref, ...), custom_call_target="tpu_custom_call" | custom-call | flops 1 | bytes 1 | tf_op jit(solution)/shard_map/forecast/pallas_call | solution.py:605
  114.5 4.1 %forecast.7 = (f32[512,128]{1,0:T(8,128)S(1)}, f32[512,128]{1,0:T(8,128)S(1)}) custom-call(s32[3]{0:T(128)S(1)} %pad_add_fusion.place_ref.refs_0_, s32[256]{0:T(256)S(1)} %copy-done.5, s32[256,128]{1,0:T(8,128)S(1)} %broadcast_in_dim.22.wide_ref, f32[5,20,8,128]{3,2,1,0:T(8,128)S(1)} %get-tuple-element.75.field_ref, ...), custom_call_target="tpu_custom_call" | custom-call | flops 1 | bytes 1 | tf_op jit(solution)/shard_map/forecast/pallas_call | solution.py:605
  118.8 2.9 %collective-permute-start.8 = (f32[512,128]{1,0:T(8,128)S(1)}, f32[512,128]{1,0:T(8,128)S(1)}, u32[]{:S(2)}, u32[]{:S(2)}) collective-permute-start(f32[512,128]{1,0:T(8,128)S(1)} %get-tuple-element.102), channel_id=1, source_target_pairs={{0,224},{32,192},{64,32},{96,0},{128,96},{160,64},{192,160},{224,1... | collective-permute-start | bytes 786440 | tf_op jit(solution)/shard_map/ppermute | solution.py:672
  121.7 2.8 %unpack.2.refs_3_ = f32[512,1024]{1,0:T(8,128)} custom-call(s32[3]{0:T(128)S(1)} %pad_add_fusion.place_ref.refs_0_, f32[512,128]{1,0:T(8,128)S(1)} %get-tuple-element.108.refs_0_, f32[512,128]{1,0:T(8,128)S(1)} %collective-permute-done.10.refs_1_, f32[512,128]{1,0:T(8,128)S(1)} %collective-permute-done.11.refs_2_, ...), custom_call_target="tpu_custom_call" | custom-call | tf_op jit(solution)/shard_map/unpack/pallas_call | solution.py:641
  124.6 3.7 %collective-permute-done.7.refs_0_ = f32[512,128]{1,0:T(8,128)S(1)} collective-permute-done((f32[512,128]{1,0:T(8,128)S(1)}, f32[512,128]{1,0:T(8,128)S(1)}, u32[]{:S(2)}, u32[]{:S(2)}) %collective-permute-start.7) | collective-permute-done | bytes 262176 | tf_op jit(solution)/shard_map/ppermute | solution.py:672
  128.3 2.1 %unpack.3 = f32[512,1024]{1,0:T(8,128)} custom-call(s32[3]{0:T(128)S(1)} %pad_add_fusion.place_ref.refs_0_, f32[512,128]{1,0:T(8,128)S(1)} %collective-permute-done.7.refs_0_, f32[512,128]{1,0:T(8,128)S(1)} %collective-permute-done.8.refs_1_, f32[512,128]{1,0:T(8,128)S(1)} %collective-permute-done.9.refs_2_, ...), custom_call_target="tpu_custom_call", output_to_operand_aliasing={{}: (4, {})} | custom-call | tf_op jit(solution)/shard_map/unpack/pallas_call | solution.py:641
  (58 shorter events, 13.8 us)
Async XLA Ops:
  2.3 8.7 %copy-start.1 = (f32[32,16,1024]{2,1,0:T(8,128)S(1)}, f32[32,16,1024]{2,1,0:T(8,128)}, u32[]{:S(2)}) copy-start(f32[32,16,1024]{2,1,0:T(8,128)} %param.8) | copy-start | bytes 6291460
  6.8 12.6 %all-to-all-start = ((f32[4,32,1024]{2,1,0:T(8,128)}), f32[4,32,1024]{2,1,0:T(8,128)}, u32[]{:S(2)}, u32[]{:S(2)}) async-start(f32[4,32,1024]{2,1,0:T(8,128)} %observe.1.after_ref), calls=%async_computation | async-start | bytes 1048576 | tf_op jit(solution)/shard_map/all_to_all | solution.py:657
  11.0 8.3 %copy-start.5 = (s32[256]{0:T(256)S(1)}, s32[256]{0:T(256)}, u32[]{:S(2)}) copy-start(s32[256]{0:T(256)} %counts_ref.7) | copy-start | bytes 3076
  19.4 4.8 %collective-permute-start.1 = (f32[4,17,32,128]{3,2,1,0:T(8,128)}, f32[4,17,32,128]{3,2,1,0:T(8,128)S(1)}, u32[]{:S(2)}, u32[]{:S(2)}) collective-permute-start(f32[4,17,32,128]{3,2,1,0:T(8,128)} %copy-done.7), channel_id=1, source_target_pairs={{0,32},{32,0},{1,33},{33,1},{2,34},{34,2},{3,35},{35,3},{4,36},{36... | collective-permute-start | bytes 3342344 | tf_op jit(solution)/shard_map/ppermute | solution.py:666
  21.7 7.3 %collective-permute-start = (f32[4,32,1024]{2,1,0:T(8,128)}, f32[4,32,1024]{2,1,0:T(8,128)S(1)}, u32[]{:S(2)}, u32[]{:S(2)}) collective-permute-start(f32[4,32,1024]{2,1,0:T(8,128)} %all-to-all-done.same_ref), channel_id=1, source_target_pairs={{0,32},{32,0},{1,33},{33,1},{2,34},{34,2},{3,35},{35,3},{4,36},{36... | collective-permute-start | bytes 1572872 | tf_op jit(solution)/shard_map/ppermute | solution.py:666
  25.2 30.0 %collective-permute-start.2 = (f32[2,17,32,128]{3,2,1,0:T(8,128)}, f32[2,17,32,128]{3,2,1,0:T(8,128)S(1)}, u32[]{:S(2)}, u32[]{:S(2)}) collective-permute-start(f32[2,17,32,128]{3,2,1,0:T(8,128)} %pad_maximum_fusion.1), channel_id=1, source_target_pairs={{0,192},{64,0},{128,64},{192,128},{1,193},{65,1},{129,65},{193,129... | collective-permute-start | bytes 1671176 | tf_op jit(solution)/shard_map/ppermute | solution.py:666
  26.1 2.9 %copy-start.9 = (f32[1024]{0:T(1024)S(1)}, f32[1024]{0:T(1024)}, u32[]{:S(2)}) copy-start(f32[1024]{0:T(1024)} %param.10) | copy-start | bytes 12292
  26.1 2.9 %copy-start.10 = (f32[1024]{0:T(1024)S(1)}, f32[1024]{0:T(1024)}, u32[]{:S(2)}) copy-start(f32[1024]{0:T(1024)} %param.11) | copy-start | bytes 12292
  26.9 28.3 %collective-permute-start.3 = (f32[2,17,32,128]{3,2,1,0:T(8,128)}, f32[2,17,32,128]{3,2,1,0:T(8,128)S(1)}, u32[]{:S(2)}, u32[]{:S(2)}) collective-permute-start(f32[2,17,32,128]{3,2,1,0:T(8,128)} %pad_maximum_fusion.2), channel_id=1, source_target_pairs={{0,128},{64,192},{128,0},{192,64},{1,129},{65,193},{129,1},{193,65... | collective-permute-start | bytes 1671176 | tf_op jit(solution)/shard_map/ppermute | solution.py:666
  29.0 26.3 %collective-permute-start.4 = (f32[2,17,32,128]{3,2,1,0:T(8,128)}, f32[2,17,32,128]{3,2,1,0:T(8,128)S(1)}, u32[]{:S(2)}, u32[]{:S(2)}) collective-permute-start(f32[2,17,32,128]{3,2,1,0:T(8,128)} %pad_maximum_fusion.3), channel_id=1, source_target_pairs={{0,64},{64,128},{128,192},{192,0},{1,65},{65,129},{129,193},{193,1... | collective-permute-start | bytes 1671176 | tf_op jit(solution)/shard_map/ppermute | solution.py:666
  30.9 24.3 %copy-start.11 = (f32[1,17,32,128]{3,2,1,0:T(8,128)S(1)}, f32[1,17,32,128]{3,2,1,0:T(8,128)}, u32[]{:S(2)}) copy-start(f32[1,17,32,128]{3,2,1,0:T(8,128)} %get-tuple-element.116) | copy-start | bytes 835588
  46.5 18.0 %copy-start.2 = (f32[16,1024]{1,0:T(8,128)S(1)}, f32[16,1024]{1,0:T(8,128)}, u32[]{:S(2)}) copy-start(f32[16,1024]{1,0:T(8,128)} %refs_1_.1) | copy-start | bytes 196612
  46.5 18.0 %copy-start.3 = (f32[16,1024]{1,0:T(8,128)S(1)}, f32[16,1024]{1,0:T(8,128)}, u32[]{:S(2)}) copy-start(f32[16,1024]{1,0:T(8,128)} %refs_2_.1) | copy-start | bytes 196612
  46.5 18.0 %copy-start.4 = (f32[16,1024]{1,0:T(8,128)S(1)}, f32[16,1024]{1,0:T(8,128)}, u32[]{:S(2)}) copy-start(f32[16,1024]{1,0:T(8,128)} %refs_3_.1) | copy-start | bytes 196612
  55.9 14.4 %all-to-all-start.3 = ((f32[8,48,128]{2,1,0:T(8,128)}), f32[8,48,128]{2,1,0:T(8,128)S(1)}, u32[]{:S(2)}, u32[]{:S(2)}) async-start(f32[8,48,128]{2,1,0:T(8,128)} %broadcast_in_dim.26), calls=%async_computation.3 | async-start | bytes 393216 | tf_op jit(solution)/shard_map/all_to_all | solution.py:657
  70.4 19.6 %collective-permute-start.5 = (f32[816,128]{1,0:T(8,128)}, f32[816,128]{1,0:T(8,128)S(1)}, u32[]{:S(2)}, u32[]{:S(2)}) collective-permute-start(f32[816,128]{1,0:T(8,128)} %copy-done.8), channel_id=1, source_target_pairs={{0,1},{1,2},{2,3},{3,4},{4,5},{5,6},{6,7},{7,8},{8,9},{9,10},{10,1... | collective-permute-start | bytes 1253384 | tf_op jit(solution)/shard_map/ppermute | solution.py:678
  72.6 17.4 %collective-permute-start.6 = (f32[816,128]{1,0:T(8,128)S(1)}, f32[816,128]{1,0:T(8,128)S(1)}, u32[]{:S(2)}, u32[]{:S(2)}) collective-permute-start(f32[816,128]{1,0:T(8,128)S(1)} %get-tuple-element.74), channel_id=1, source_target_pairs={{1,0},{2,1},{3,2},{4,3},{5,4},{6,5},{7,6},{8,7},{9,8},{10,9},{11,1... | collective-permute-start | bytes 1253384 | tf_op jit(solution)/shard_map/ppermute | solution.py:678
  96.1 22.5 %collective-permute-start.10 = (f32[512,128]{1,0:T(8,128)S(1)}, f32[512,128]{1,0:T(8,128)S(1)}, u32[]{:S(2)}, u32[]{:S(2)}) collective-permute-start(f32[512,128]{1,0:T(8,128)S(1)} %get-tuple-element.109), channel_id=1, source_target_pairs={{0,64},{32,96},{64,128},{96,160},{128,192},{160,224},{192,0},{224,... | collective-permute-start | bytes 786440 | tf_op jit(solution)/shard_map/ppermute | solution.py:672
  97.2 21.6 %collective-permute-start.11 = (f32[512,128]{1,0:T(8,128)S(1)}, f32[512,128]{1,0:T(8,128)S(1)}, u32[]{:S(2)}, u32[]{:S(2)}) collective-permute-start(f32[512,128]{1,0:T(8,128)S(1)} %get-tuple-element.110), channel_id=1, source_target_pairs={{0,192},{32,224},{64,0},{96,32},{128,64},{160,96},{192,128},{224,1... | collective-permute-start | bytes 786440 | tf_op jit(solution)/shard_map/ppermute | solution.py:672
  105.1 16.6 %collective-permute-start.12 = (f32[512,128]{1,0:T(8,128)S(1)}, f32[512,128]{1,0:T(8,128)S(1)}, u32[]{:S(2)}, u32[]{:S(2)}) collective-permute-start(f32[512,128]{1,0:T(8,128)S(1)} %get-tuple-element.111), channel_id=1, source_target_pairs={{0,128},{32,160},{64,192},{96,224},{128,0},{160,32},{192,64},{224,... | collective-permute-start | bytes 786440 | tf_op jit(solution)/shard_map/ppermute | solution.py:672
  105.2 16.5 %collective-permute-start.13 = (f32[512,128]{1,0:T(8,128)S(1)}, f32[512,128]{1,0:T(8,128)S(1)}, u32[]{:S(2)}, u32[]{:S(2)}) collective-permute-start(f32[512,128]{1,0:T(8,128)S(1)} %get-tuple-element.112), channel_id=1, source_target_pairs={{0,160},{32,128},{64,224},{96,192},{128,32},{160,0},{192,96},{224,... | collective-permute-start | bytes 786440 | tf_op jit(solution)/shard_map/ppermute | solution.py:672
  118.6 6.0 %collective-permute-start.9 = (f32[512,128]{1,0:T(8,128)S(1)}, f32[512,128]{1,0:T(8,128)S(1)}, u32[]{:S(2)}, u32[]{:S(2)}) collective-permute-start(f32[512,128]{1,0:T(8,128)S(1)} %get-tuple-element.107), channel_id=1, source_target_pairs={{0,32},{32,0},{64,96},{96,64},{128,160},{160,128},{192,224},{224,1... | collective-permute-start | bytes 786440 | tf_op jit(solution)/shard_map/ppermute | solution.py:672
  118.7 9.6 %collective-permute-start.7 = (f32[512,128]{1,0:T(8,128)S(1)}, f32[512,128]{1,0:T(8,128)S(1)}, u32[]{:S(2)}, u32[]{:S(2)}) collective-permute-start(f32[512,128]{1,0:T(8,128)S(1)} %get-tuple-element.101), channel_id=1, source_target_pairs={{0,96},{32,64},{64,160},{96,128},{128,224},{160,192},{192,32},{224... | collective-permute-start | bytes 786440 | tf_op jit(solution)/shard_map/ppermute | solution.py:672
  118.8 9.5 %collective-permute-start.8 = (f32[512,128]{1,0:T(8,128)S(1)}, f32[512,128]{1,0:T(8,128)S(1)}, u32[]{:S(2)}, u32[]{:S(2)}) collective-permute-start(f32[512,128]{1,0:T(8,128)S(1)} %get-tuple-element.102), channel_id=1, source_target_pairs={{0,224},{32,192},{64,32},{96,0},{128,96},{160,64},{192,160},{224,1... | collective-permute-start | bytes 786440 | tf_op jit(solution)/shard_map/ppermute | solution.py:672
  (4 other events, 4.0 us)

commit v6 on v5

--- a/solution.py
+++ b/solution.py
@@ -706,21 +706,24 @@
     parts = shared(part, MEMBER)
     cell_fields = (ksat, storage, recharge)
     down, up = borders(pieces, cell_fields)
-    parts, down, up = lax.optimization_barrier((parts, down, up))
     above = to_strips_beside(up, 1)
     below = to_strips_beside(down, -1)
     transform = transform_of(place, parts)
     fields, edge_fields, cells = analysed(place, cell_fields, transform, pieces, above, below)
 
     arrived = [None] * OWNERS
-    for shifts in ((2, 6), (4, 5), (3, 7), (1, 0)):
+    for shifts in ((4,), (2, 6), (5, 3), (7, 1), (0,)):
+        if shifts == (7, 1):
+            cells, arrived[4] = lax.optimization_barrier((cells, arrived[4]))
+        if shifts == (0,):
+            cells, arrived[2], arrived[6] = lax.optimization_barrier((cells, arrived[2], arrived[6]))
         moved = forecasts(
             shifts, place, newton_counts, wide_counts, fields, edge_fields, [cells[i] for i in shifts]
         )
         moved, cells = lax.optimization_barrier((moved, cells))
         for i, field in zip(shifts, moved):
             arrived[i] = to_owner(field, i) if i else field
-    early, late = (0, 2, 6, 4, 5), (3, 7, 1)
+    early, late = (0, 4, 2, 6), (5, 3, 7, 1)
     result = unpacked(place, early, [arrived[i] for i in early])
     result = unpacked(place, late, [arrived[i] for i in late], result)
     return result.reshape(members, rows, columns)

time: 131 us -> 124 us (0.947)
  waiting for transfers between devices: 15.4 us -> 9.11 us
    all_to_all x2, waiting for transfers between devices: 9.98 us -> 4.96 us  [exchanged(): return lax.all_to_all(copies, axis, split_axis=0, concat_axis=0, tiled=True)]
    unnamed x24 -> x22, local copies, waits for them, and re-layouts: 4.06 us -> 3.31 us
    pallas_call x4 -> x5, Pallas kernels: 18.4 us -> 19 us  [forecasts(): pl.pallas_call(functools.partial(forecast_kernel, shifts), out_shape=[sha...]
  transfers between devices with their start and end apart: 16 -> 16, of which waited for: 4 -> 3; matrix products, arithmetic and copies ran while one was open for 3% -> 3% of each run, Pallas kernels for 26% -> 29%
where the time goes in v6:
time: 124 us
  Pallas kernels  47.5 us (38%)
  starting transfers between devices  35.4 us (29%)
  blocking collectives  24.2 us (20%)
  waiting for transfers between devices  9.11 us (7%)
  local copies, waits for them, and re-layouts  4.99 us (4%)
  other arithmetic  2.68 us (2%)
    all_to_all x2, blocking collectives, exchanged(): return lax.all_to_all(copies, axis, split_axis=0, concat_axis=0, tiled=True)  24.2 us
    pallas_call x5, Pallas kernels, forecasts(): pl.pallas_call(functools.partial(forecast_kernel, shifts), out_shape=[sha...  19 us
    all_to_all x2, starting transfers between devices, exchanged(): return lax.all_to_all(copies, axis, split_axis=0, concat_axis=0, tiled=True)  12.7 us
    pallas_call x1, Pallas kernels, transform_of(): pl.pallas_call(root_kernel, out_shape=shape(MEMBERS, MEMBERS), in_specs=[...  12.4 us
    ppermute x7, starting transfers between devices, to_owner(): return lax.ppermute(array, MEMBER, pairs)  10.7 us
    ppermute x2, starting transfers between devices, to_strips_beside(): return lax.ppermute(array, SPACE, pairs)  7.56 us
    all_to_all x2, waiting for transfers between devices, exchanged(): return lax.all_to_all(copies, axis, split_axis=0, concat_axis=0, tiled=True)  4.96 us
    pallas_call x1, Pallas kernels, observed(): pl.pallas_call(observe_kernel, out_shape=shape(copies, HELD, obs_index.sh...  4.5 us
  transfers between devices with their start and end apart: 16, of which 3 were waited for; matrix products, arithmetic and copies ran while one was open for 3% of the time, Pallas kernels for 29%

profile of v6, /device:TPU:33, one launch (start us, length us, event | category | flops | bytes accessed | tf_op | source)
XLA Modules:
  0.0 124.1 jit_solution(11253227294361459527)
XLA Ops:
  2.3 4.5 %observe.1.after_ref = f32[4,32,1024]{2,1,0:T(8,128)} custom-call(s32[1,1024]{1,0:T(1,128)S(1)} %bitcast.10, f32[512,1024]{1,0:T(8,128)S(1)} %bitcast.8), custom_call_target="tpu_custom_call" | custom-call | tf_op jit(solution)/shard_map/observe/pallas_call | solution.py:88
  6.8 4.2 %all-to-all-start = ((f32[4,32,1024]{2,1,0:T(8,128)}), f32[4,32,1024]{2,1,0:T(8,128)}, u32[]{:S(2)}, u32[]{:S(2)}) async-start(f32[4,32,1024]{2,1,0:T(8,128)} %observe.1.after_ref), calls=%async_computation | async-start | bytes 1048576 | tf_op jit(solution)/shard_map/all_to_all | solution.py:657
  11.0 2.4 %pack.1 = (f32[4,17,32,128]{3,2,1,0:T(8,128)S(1)}, f32[4,17,32,128]{3,2,1,0:T(8,128)S(1)}) custom-call(s32[3]{0:T(128)S(1)} %pad_add_fusion.place_ref.refs_0_, f32[512,1024]{1,0:T(8,128)S(1)} %bitcast.9, f32[4,32,1024]{2,1,0:T(8,128)} %observe.1.after_ref), custom_call_target="tpu_custom_call" | custom-call | tf_op jit(solution)/shard_map/pack/pallas_call | solution.py:162
  14.4 5.0 %all-to-all-done.same_ref = f32[4,32,1024]{2,1,0:T(8,128)} async-done(((f32[4,32,1024]{2,1,0:T(8,128)}), f32[4,32,1024]{2,1,0:T(8,128)}, u32[]{:S(2)}, u32[]{:S(2)}) %all-to-all-start) | async-done | bytes 524320 | tf_op jit(solution)/shard_map/all_to_all | solution.py:657
  19.5 2.2 %collective-permute-start.1 = (f32[4,17,32,128]{3,2,1,0:T(8,128)}, f32[4,17,32,128]{3,2,1,0:T(8,128)S(1)}, u32[]{:S(2)}, u32[]{:S(2)}) collective-permute-start(f32[4,17,32,128]{3,2,1,0:T(8,128)} %copy-done.7), channel_id=1, source_target_pairs={{0,32},{32,0},{1,33},{33,1},{2,34},{34,2},{3,35},{35,3},{4,36},{36... | collective-permute-start | bytes 3342344 | tf_op jit(solution)/shard_map/ppermute | solution.py:666
  29.0 1.9 %gram.1 = f32[8,48,128]{2,1,0:T(8,128)S(1)} custom-call(s32[3]{0:T(128)S(1)} %pad_add_fusion.place_ref.refs_0_, f32[4,32,1024]{2,1,0:T(8,128)} %all-to-all-done.same_ref, f32[4,32,1024]{2,1,0:T(8,128)S(1)} %collective-permute-done.other_ref, f32[1,1024]{1,0:T(1,128)S(1)} %bitcast.11, f32[1,1024]{1,0:T(1,128)S(1)} %bitcast.12), custom_call_target="tpu_custom_call" | custom-call | flops 10000000000 | bytes 1000000 | tf_op jit(solution)/shard_map/gram/pallas_call | solution.py:233
  30.9 15.6 %all_to_all.20 = f32[8,48,128]{2,1,0:T(8,128)S(1)} all-to-all(f32[8,48,128]{2,1,0:T(8,128)S(1)} %gram.1), channel_id=1, replica_groups=mesh['member_0'=4,'member_1'=2,'space_0'=8,'space_1'=4] {'space_0'}, dimensions={0} | all-to-all | bytes 393216 | tf_op jit(solution)/shard_map/all_to_all | solution.py:657
  46.6 8.6 %all_to_all.21 = f32[4,48,128]{2,1,0:T(8,128)S(1)} all-to-all(f32[4,48,128]{2,1,0:T(8,128)S(1)} %broadcast_in_dim.25), channel_id=1, replica_groups=mesh['member_0'=4,'member_1'=2,'space_0'=8,'space_1'=4] {'space_1'}, dimensions={0} | all-to-all | bytes 196608 | tf_op jit(solution)/shard_map/all_to_all | solution.py:657
  55.9 8.5 %all-to-all-start.3 = ((f32[8,48,128]{2,1,0:T(8,128)}), f32[8,48,128]{2,1,0:T(8,128)}, u32[]{:S(2)}, u32[]{:S(2)}) async-start(f32[8,48,128]{2,1,0:T(8,128)} %broadcast_in_dim.26), calls=%async_computation.3 | async-start | bytes 393216 | tf_op jit(solution)/shard_map/all_to_all | solution.py:657
  65.5 2.2 %collective-permute-start.5 = (f32[816,128]{1,0:T(8,128)}, f32[816,128]{1,0:T(8,128)S(1)}, u32[]{:S(2)}, u32[]{:S(2)}) collective-permute-start(f32[816,128]{1,0:T(8,128)} %get-tuple-element.76), channel_id=1, source_target_pairs={{0,1},{1,2},{2,3},{3,4},{4,5},{5,6},{6,7},{7,8},{8,9},{9,10},{10,1... | collective-permute-start | bytes 1253384 | tf_op jit(solution)/shard_map/ppermute | solution.py:678
  67.7 5.4 %collective-permute-start.6 = (f32[816,128]{1,0:T(8,128)}, f32[816,128]{1,0:T(8,128)S(1)}, u32[]{:S(2)}, u32[]{:S(2)}) collective-permute-start(f32[816,128]{1,0:T(8,128)} %get-tuple-element.77), channel_id=1, source_target_pairs={{1,0},{2,1},{3,2},{4,3},{5,4},{6,5},{7,6},{8,7},{9,8},{10,9},{11,1... | collective-permute-start | bytes 1253384 | tf_op jit(solution)/shard_map/ppermute | solution.py:678
  73.1 12.4 %root.1.refs_4_ = f32[256,256]{1,0:T(8,128)S(1)} custom-call(s32[3]{0:T(128)S(1)} %pad_add_fusion.place_ref.refs_0_, f32[8,48,128]{2,1,0:T(8,128)} %all-to-all-done.3.parts_ref), custom_call_target="tpu_custom_call" | custom-call | flops 10000000000 | bytes 1000000 | tf_op jit(solution)/shard_map/root/pallas_call | solution.py:314
  85.5 2.0 %analyse.1 = (f32[5,20,8,128]{3,2,1,0:T(8,128)S(1)}, f32[6,8,128]{2,1,0:T(8,128)S(1)}, f32[21,32,128]{2,1,0:T(8,128)S(1)}, f32[21,32,128]{2,1,0:T(8,128)S(1)}, f...) custom-call(s32[3]{0:T(128)S(1)} %pad_add_fusion.place_ref.refs_0_, ...), custom_call_target="tpu_custom_call" | custom-call | tf_op jit(solution)/shard_map/analyse/pallas_call | solution.py:446
  87.5 2.3 %forecast.5 = f32[512,128]{1,0:T(8,128)S(1)} custom-call(s32[3]{0:T(128)S(1)} %pad_add_fusion.place_ref.refs_0_, s32[256]{0:T(256)S(1)} %copy-done.5, s32[256,128]{1,0:T(8,128)S(1)} %broadcast_in_dim.22.wide_ref, f32[5,20,8,128]{3,2,1,0:T(8,128)S(1)} %get-tuple-element.78.field_ref, f32[6,8,128]{2,1,0:T(8,128)S(1)} %get-tuple-element.79.edge_field_ref, ...), custom_call_target="tpu_custom_call" | custom-call | flops 1 | bytes 1 | tf_op jit(solution)/shard_map/forecast/pallas_call | solution.py:605
  89.8 3.0 %collective-permute-start.9 = (f32[512,128]{1,0:T(8,128)S(1)}, f32[512,128]{1,0:T(8,128)S(1)}, u32[]{:S(2)}, u32[]{:S(2)}) collective-permute-start(f32[512,128]{1,0:T(8,128)S(1)} %forecast.5), channel_id=1, source_target_pairs={{0,128},{32,160},{64,192},{96,224},{128,0},{160,32},{192,64},{224,... | collective-permute-start | bytes 786440 | tf_op jit(solution)/shard_map/ppermute | solution.py:672
  92.8 4.8 %forecast.6 = (f32[512,128]{1,0:T(8,128)S(1)}, f32[512,128]{1,0:T(8,128)S(1)}) custom-call(s32[3]{0:T(128)S(1)} %pad_add_fusion.place_ref.refs_0_, s32[256]{0:T(256)S(1)} %copy-done.5, s32[256,128]{1,0:T(8,128)S(1)} %broadcast_in_dim.22.wide_ref, f32[5,20,8,128]{3,2,1,0:T(8,128)S(1)} %get-tuple-element.78.field_ref, ...), custom_call_target="tpu_custom_call" | custom-call | flops 1 | bytes 1 | tf_op jit(solution)/shard_map/forecast/pallas_call | solution.py:605
  98.0 2.4 %collective-permute-start.13 = (f32[512,128]{1,0:T(8,128)S(1)}, f32[512,128]{1,0:T(8,128)S(1)}, u32[]{:S(2)}, u32[]{:S(2)}) collective-permute-start(f32[512,128]{1,0:T(8,128)S(1)} %get-tuple-element.119), channel_id=1, source_target_pairs={{0,192},{32,224},{64,0},{96,32},{128,64},{160,96},{192,128},{224,1... | collective-permute-start | bytes 786440 | tf_op jit(solution)/shard_map/ppermute | solution.py:672
  100.4 5.5 %forecast.7 = (f32[512,128]{1,0:T(8,128)S(1)}, f32[512,128]{1,0:T(8,128)S(1)}) custom-call(s32[3]{0:T(128)S(1)} %pad_add_fusion.place_ref.refs_0_, s32[256]{0:T(256)S(1)} %copy-done.5, s32[256,128]{1,0:T(8,128)S(1)} %broadcast_in_dim.22.wide_ref, f32[5,20,8,128]{3,2,1,0:T(8,128)S(1)} %get-tuple-element.78.field_ref, ...), custom_call_target="tpu_custom_call" | custom-call | flops 1 | bytes 1 | tf_op jit(solution)/shard_map/forecast/pallas_call | solution.py:605
  106.8 4.1 %forecast.8 = (f32[512,128]{1,0:T(8,128)S(1)}, f32[512,128]{1,0:T(8,128)S(1)}) custom-call(s32[3]{0:T(128)S(1)} %pad_add_fusion.place_ref.refs_0_, s32[256]{0:T(256)S(1)} %copy-done.5, s32[256,128]{1,0:T(8,128)S(1)} %broadcast_in_dim.22.wide_ref, f32[5,20,8,128]{3,2,1,0:T(8,128)S(1)} %get-tuple-element.78.field_ref, ...), custom_call_target="tpu_custom_call" | custom-call | flops 1 | bytes 1 | tf_op jit(solution)/shard_map/forecast/pallas_call | solution.py:605
  110.9 2.5 %collective-permute-start.10 = (f32[512,128]{1,0:T(8,128)S(1)}, f32[512,128]{1,0:T(8,128)S(1)}, u32[]{:S(2)}, u32[]{:S(2)}) collective-permute-start(f32[512,128]{1,0:T(8,128)S(1)} %get-tuple-element.115), channel_id=1, source_target_pairs={{0,224},{32,192},{64,32},{96,0},{128,96},{160,64},{192,160},{224,1... | collective-permute-start | bytes 786440 | tf_op jit(solution)/shard_map/ppermute | solution.py:672
  115.0 2.3 %forecast.9.refs_0_ = f32[512,128]{1,0:T(8,128)S(1)} custom-call(s32[3]{0:T(128)S(1)} %pad_add_fusion.place_ref.refs_0_, s32[256]{0:T(256)S(1)} %copy-done.5, s32[256,128]{1,0:T(8,128)S(1)} %broadcast_in_dim.22.wide_ref, f32[5,20,8,128]{3,2,1,0:T(8,128)S(1)} %get-tuple-element.78.field_ref, f32[6,8,128]{2,1,0:T(8,128)S(1)} %get-tuple-element.79.edge_field_ref, ...), custom_call_target="tpu_custom_call" | custom-call | flops 1 | bytes 1 | tf_op jit(solution)/shard_map/forecast/pallas_call | solution.py:605
  117.3 2.2 %unpack.2.refs_4_ = f32[512,1024]{1,0:T(8,128)} custom-call(s32[3]{0:T(128)S(1)} %pad_add_fusion.place_ref.refs_0_, f32[512,128]{1,0:T(8,128)S(1)} %forecast.9.refs_0_, f32[512,128]{1,0:T(8,128)S(1)} %collective-permute-done.9.refs_1_, f32[512,128]{1,0:T(8,128)S(1)} %collective-permute-done.12.refs_2_, f32[512,128]{1,0:T(8,128)S(1)} %collective-permute-done.13.refs_3_), custom_call_target="tpu_custom_call" | custom-call | tf_op jit(solution)/shard_map/unpack/pallas_call | solution.py:641
  119.5 2.4 %collective-permute-done.8.refs_1_ = f32[512,128]{1,0:T(8,128)S(1)} collective-permute-done((f32[512,128]{1,0:T(8,128)S(1)}, f32[512,128]{1,0:T(8,128)S(1)}, u32[]{:S(2)}, u32[]{:S(2)}) %collective-permute-start.8) | collective-permute-done | bytes 262176 | tf_op jit(solution)/shard_map/ppermute | solution.py:672
  121.9 2.2 %unpack.3 = f32[512,1024]{1,0:T(8,128)} custom-call(s32[3]{0:T(128)S(1)} %pad_add_fusion.place_ref.refs_0_, f32[512,128]{1,0:T(8,128)S(1)} %collective-permute-done.7.refs_0_, f32[512,128]{1,0:T(8,128)S(1)} %collective-permute-done.8.refs_1_, f32[512,128]{1,0:T(8,128)S(1)} %collective-permute-done.10.refs_2_, ...), custom_call_target="tpu_custom_call", output_to_operand_aliasing={{}: (5, {})} | custom-call | tf_op jit(solution)/shard_map/unpack/pallas_call | solution.py:641
  (57 shorter events, 15.3 us)
Async XLA Ops:
  2.3 8.8 %copy-start.1 = (f32[32,16,1024]{2,1,0:T(8,128)S(1)}, f32[32,16,1024]{2,1,0:T(8,128)}, u32[]{:S(2)}) copy-start(f32[32,16,1024]{2,1,0:T(8,128)} %param.8) | copy-start | bytes 6291460
  6.8 12.6 %all-to-all-start = ((f32[4,32,1024]{2,1,0:T(8,128)}), f32[4,32,1024]{2,1,0:T(8,128)}, u32[]{:S(2)}, u32[]{:S(2)}) async-start(f32[4,32,1024]{2,1,0:T(8,128)} %observe.1.after_ref), calls=%async_computation | async-start | bytes 1048576 | tf_op jit(solution)/shard_map/all_to_all | solution.py:657
  11.0 8.3 %copy-start.5 = (s32[256]{0:T(256)S(1)}, s32[256]{0:T(256)}, u32[]{:S(2)}) copy-start(s32[256]{0:T(256)} %counts_ref.9) | copy-start | bytes 3076
  19.5 4.8 %collective-permute-start.1 = (f32[4,17,32,128]{3,2,1,0:T(8,128)}, f32[4,17,32,128]{3,2,1,0:T(8,128)S(1)}, u32[]{:S(2)}, u32[]{:S(2)}) collective-permute-start(f32[4,17,32,128]{3,2,1,0:T(8,128)} %copy-done.7), channel_id=1, source_target_pairs={{0,32},{32,0},{1,33},{33,1},{2,34},{34,2},{3,35},{35,3},{4,36},{36... | collective-permute-start | bytes 3342344 | tf_op jit(solution)/shard_map/ppermute | solution.py:666
  21.7 7.3 %collective-permute-start = (f32[4,32,1024]{2,1,0:T(8,128)}, f32[4,32,1024]{2,1,0:T(8,128)S(1)}, u32[]{:S(2)}, u32[]{:S(2)}) collective-permute-start(f32[4,32,1024]{2,1,0:T(8,128)} %all-to-all-done.same_ref), channel_id=1, source_target_pairs={{0,32},{32,0},{1,33},{33,1},{2,34},{34,2},{3,35},{35,3},{4,36},{36... | collective-permute-start | bytes 1572872 | tf_op jit(solution)/shard_map/ppermute | solution.py:666
  25.2 30.0 %collective-permute-start.2 = (f32[2,17,32,128]{3,2,1,0:T(8,128)}, f32[2,17,32,128]{3,2,1,0:T(8,128)S(1)}, u32[]{:S(2)}, u32[]{:S(2)}) collective-permute-start(f32[2,17,32,128]{3,2,1,0:T(8,128)} %pad_maximum_fusion.1), channel_id=1, source_target_pairs={{0,192},{64,0},{128,64},{192,128},{1,193},{65,1},{129,65},{193,129... | collective-permute-start | bytes 1671176 | tf_op jit(solution)/shard_map/ppermute | solution.py:666
  26.1 2.9 %copy-start.8 = (f32[1024]{0:T(1024)S(1)}, f32[1024]{0:T(1024)}, u32[]{:S(2)}) copy-start(f32[1024]{0:T(1024)} %param.10) | copy-start | bytes 12292
  26.1 2.9 %copy-start.9 = (f32[1024]{0:T(1024)S(1)}, f32[1024]{0:T(1024)}, u32[]{:S(2)}) copy-start(f32[1024]{0:T(1024)} %param.11) | copy-start | bytes 12292
  26.9 28.3 %collective-permute-start.3 = (f32[2,17,32,128]{3,2,1,0:T(8,128)}, f32[2,17,32,128]{3,2,1,0:T(8,128)S(1)}, u32[]{:S(2)}, u32[]{:S(2)}) collective-permute-start(f32[2,17,32,128]{3,2,1,0:T(8,128)} %pad_maximum_fusion.2), channel_id=1, source_target_pairs={{0,128},{64,192},{128,0},{192,64},{1,129},{65,193},{129,1},{193,65... | collective-permute-start | bytes 1671176 | tf_op jit(solution)/shard_map/ppermute | solution.py:666
  29.0 26.3 %collective-permute-start.4 = (f32[2,17,32,128]{3,2,1,0:T(8,128)}, f32[2,17,32,128]{3,2,1,0:T(8,128)S(1)}, u32[]{:S(2)}, u32[]{:S(2)}) collective-permute-start(f32[2,17,32,128]{3,2,1,0:T(8,128)} %pad_maximum_fusion.3), channel_id=1, source_target_pairs={{0,64},{64,128},{128,192},{192,0},{1,65},{65,129},{129,193},{193,1... | collective-permute-start | bytes 1671176 | tf_op jit(solution)/shard_map/ppermute | solution.py:666
  30.9 24.3 %copy-start.10 = (f32[1,17,32,128]{3,2,1,0:T(8,128)S(1)}, f32[1,17,32,128]{3,2,1,0:T(8,128)}, u32[]{:S(2)}) copy-start(f32[1,17,32,128]{3,2,1,0:T(8,128)} %get-tuple-element.128) | copy-start | bytes 835588
  46.5 18.0 %copy-start.2 = (f32[16,1024]{1,0:T(8,128)S(1)}, f32[16,1024]{1,0:T(8,128)}, u32[]{:S(2)}) copy-start(f32[16,1024]{1,0:T(8,128)} %refs_1_.1) | copy-start | bytes 196612
  46.5 18.0 %copy-start.3 = (f32[16,1024]{1,0:T(8,128)S(1)}, f32[16,1024]{1,0:T(8,128)}, u32[]{:S(2)}) copy-start(f32[16,1024]{1,0:T(8,128)} %refs_2_.1) | copy-start | bytes 196612
  46.5 18.0 %copy-start.4 = (f32[16,1024]{1,0:T(8,128)S(1)}, f32[16,1024]{1,0:T(8,128)}, u32[]{:S(2)}) copy-start(f32[16,1024]{1,0:T(8,128)} %refs_3_.1) | copy-start | bytes 196612
  55.9 17.1 %all-to-all-start.3 = ((f32[8,48,128]{2,1,0:T(8,128)}), f32[8,48,128]{2,1,0:T(8,128)}, u32[]{:S(2)}, u32[]{:S(2)}) async-start(f32[8,48,128]{2,1,0:T(8,128)} %broadcast_in_dim.26), calls=%async_computation.3 | async-start | bytes 393216 | tf_op jit(solution)/shard_map/all_to_all | solution.py:657
  65.5 20.0 %collective-permute-start.5 = (f32[816,128]{1,0:T(8,128)}, f32[816,128]{1,0:T(8,128)S(1)}, u32[]{:S(2)}, u32[]{:S(2)}) collective-permute-start(f32[816,128]{1,0:T(8,128)} %get-tuple-element.76), channel_id=1, source_target_pairs={{0,1},{1,2},{2,3},{3,4},{4,5},{5,6},{6,7},{7,8},{8,9},{9,10},{10,1... | collective-permute-start | bytes 1253384 | tf_op jit(solution)/shard_map/ppermute | solution.py:678
  67.7 17.8 %collective-permute-start.6 = (f32[816,128]{1,0:T(8,128)}, f32[816,128]{1,0:T(8,128)S(1)}, u32[]{:S(2)}, u32[]{:S(2)}) collective-permute-start(f32[816,128]{1,0:T(8,128)} %get-tuple-element.77), channel_id=1, source_target_pairs={{1,0},{2,1},{3,2},{4,3},{5,4},{6,5},{7,6},{8,7},{9,8},{10,9},{11,1... | collective-permute-start | bytes 1253384 | tf_op jit(solution)/shard_map/ppermute | solution.py:678
  89.8 17.0 %collective-permute-start.9 = (f32[512,128]{1,0:T(8,128)S(1)}, f32[512,128]{1,0:T(8,128)S(1)}, u32[]{:S(2)}, u32[]{:S(2)}) collective-permute-start(f32[512,128]{1,0:T(8,128)S(1)} %forecast.5), channel_id=1, source_target_pairs={{0,128},{32,160},{64,192},{96,224},{128,0},{160,32},{192,64},{224,... | collective-permute-start | bytes 786440 | tf_op jit(solution)/shard_map/ppermute | solution.py:672
  97.6 15.9 %collective-permute-start.12 = (f32[512,128]{1,0:T(8,128)S(1)}, f32[512,128]{1,0:T(8,128)S(1)}, u32[]{:S(2)}, u32[]{:S(2)}) collective-permute-start(f32[512,128]{1,0:T(8,128)S(1)} %get-tuple-element.118), channel_id=1, source_target_pairs={{0,64},{32,96},{64,128},{96,160},{128,192},{160,224},{192,0},{224,... | collective-permute-start | bytes 786440 | tf_op jit(solution)/shard_map/ppermute | solution.py:672
  98.0 17.0 %collective-permute-start.13 = (f32[512,128]{1,0:T(8,128)S(1)}, f32[512,128]{1,0:T(8,128)S(1)}, u32[]{:S(2)}, u32[]{:S(2)}) collective-permute-start(f32[512,128]{1,0:T(8,128)S(1)} %get-tuple-element.119), channel_id=1, source_target_pairs={{0,192},{32,224},{64,0},{96,32},{128,64},{160,96},{192,128},{224,1... | collective-permute-start | bytes 786440 | tf_op jit(solution)/shard_map/ppermute | solution.py:672
  105.9 13.6 %collective-permute-start.7 = (f32[512,128]{1,0:T(8,128)S(1)}, f32[512,128]{1,0:T(8,128)S(1)}, u32[]{:S(2)}, u32[]{:S(2)}) collective-permute-start(f32[512,128]{1,0:T(8,128)S(1)} %get-tuple-element.104), channel_id=1, source_target_pairs={{0,160},{32,128},{64,224},{96,192},{128,32},{160,0},{192,96},{224,... | collective-permute-start | bytes 786440 | tf_op jit(solution)/shard_map/ppermute | solution.py:672
  106.4 15.6 %collective-permute-start.8 = (f32[512,128]{1,0:T(8,128)S(1)}, f32[512,128]{1,0:T(8,128)S(1)}, u32[]{:S(2)}, u32[]{:S(2)}) collective-permute-start(f32[512,128]{1,0:T(8,128)S(1)} %get-tuple-element.105), channel_id=1, source_target_pairs={{0,96},{32,64},{64,160},{96,128},{128,224},{160,192},{192,32},{224... | collective-permute-start | bytes 786440 | tf_op jit(solution)/shard_map/ppermute | solution.py:672
  110.9 11.0 %collective-permute-start.10 = (f32[512,128]{1,0:T(8,128)S(1)}, f32[512,128]{1,0:T(8,128)S(1)}, u32[]{:S(2)}, u32[]{:S(2)}) collective-permute-start(f32[512,128]{1,0:T(8,128)S(1)} %get-tuple-element.115), channel_id=1, source_target_pairs={{0,224},{32,192},{64,32},{96,0},{128,96},{160,64},{192,160},{224,1... | collective-permute-start | bytes 786440 | tf_op jit(solution)/shard_map/ppermute | solution.py:672
  113.5 8.4 %collective-permute-start.11 = (f32[512,128]{1,0:T(8,128)S(1)}, f32[512,128]{1,0:T(8,128)S(1)}, u32[]{:S(2)}, u32[]{:S(2)}) collective-permute-start(f32[512,128]{1,0:T(8,128)S(1)} %get-tuple-element.116), channel_id=1, source_target_pairs={{0,32},{32,0},{64,96},{96,64},{128,160},{160,128},{192,224},{224,1... | collective-permute-start | bytes 786440 | tf_op jit(solution)/shard_map/ppermute | solution.py:672
  (3 other events, 3.3 us)

commit v7 on v6

--- a/solution.py
+++ b/solution.py
@@ -101,7 +101,15 @@
 
 def pack_kernel(place_ref, state_ref, after_ref, *refs):
     own = place_ref[0]
-    sent_refs, column_ref = refs[:2], refs[2]
+    chips = OWNERS // 2
+    joint_refs, given_ref, column_ref = refs[:chips], refs[chips], refs[chips + 1]
+
+    def put(slot, row, members, value):
+        if slot % 2:
+            given_ref[slot // 2, row, members] = value
+        else:
+            joint_refs[slot // 2][0, row, members] = value
+
     lane = lane_ids()
     even = lane % 2 == 0
     near_left = (lane < OUTER) & even
@@ -122,7 +130,7 @@
             column_ref[slot] = state_ref[lines, pl.ds(start, LANES)]
             for r in range(ROWS):
                 value = column_ref[slot, pl.ds(r, 8, stride=ROWS), :]
-                sent_refs[slot % 2][slot // 2, PLACE[r], members] = value
+                put(slot, PLACE[r], members, value)
                 at = 2 * (r + 1)
                 packed_near = jnp.where(
                     (lane == at) | (lane == at + 1), turned(value, at + 1), packed_near
@@ -152,22 +160,53 @@
             edge = jnp.where(far_left, left(far), edge)
             edge = jnp.where(near_right, right(near), edge)
             edge = jnp.where(far_right, right(far), edge)
-            sent_refs[slot % 2][slot // 2, PLACE[EDGE], members] = edge
+            put(slot, PLACE[EDGE], members, edge)
         return carry
 
     lax.fori_loop(0, HELD // 8, one_group, 0)
 
 
 def packed_blocks(place, state, after):
-    return pl.pallas_call(
+    chips = OWNERS // 2
+    packed = pl.pallas_call(
         pack_kernel,
-        out_shape=[shape(OWNERS // 2, SENT_ROWS, HELD, LANES)] * 2,
+        out_shape=[shape(2, SENT_ROWS, HELD, LANES)] * chips
+        + [shape(chips, SENT_ROWS, HELD, LANES)],
         in_specs=[SCALARS] + whole(1) + [pl.BlockSpec(memory_space=pl.ANY)],
-        out_specs=whole(2),
+        out_specs=whole(chips + 1),
         scratch_shapes=[pltpu.VMEM((OWNERS, 8 * ROWS, LANES), F32)],
         compiler_params=params(8),
         name="pack",
     )(place, state, after)
+    return packed[:chips], packed[chips]
+
+
+def fill_kernel(taken_ref, *refs):
+    chips = OWNERS // 2
+    joint_refs, sems = refs[chips : 2 * chips], refs[2 * chips]
+    copies = [
+        pltpu.make_async_copy(taken_ref.at[n], joint_refs[n].at[1], sems.at[n])
+        for n in range(chips)
+    ]
+    for copy in copies:
+        copy.start()
+    for copy in copies:
+        copy.wait()
+
+
+def filled(taken, joint):
+    chips = OWNERS // 2
+    anywhere = [pl.BlockSpec(memory_space=pl.ANY)]
+    return pl.pallas_call(
+        fill_kernel,
+        out_shape=[shape(2, SENT_ROWS, HELD, LANES)] * chips,
+        in_specs=whole(1) + anywhere * chips,
+        out_specs=anywhere * chips,
+        input_output_aliases={1 + n: n for n in range(chips)},
+        scratch_shapes=[pltpu.SemaphoreType.DMA((chips,))],
+        compiler_params=params(4),
+        name="fill",
+    )(taken, *joint)
 
 
 BORDER = OWNERS * 3 * HELD
@@ -618,37 +657,31 @@
     )(place, counts, wide_counts, fields, edge_fields, *cells)
 
 
-def unpack_kernel(many, place_ref, *refs):
-    out_ref = refs[-1]
-    step = pl.program_id(0)
-    for n in range(many):
-
-        @pl.when(step == n)
-        def _():
-            out_ref[...] = refs[n][...]
+def unpack_kernel(shifts, place_ref, *refs):
+    out_ref, sems = refs[-2], refs[-1]
+    copies = []
+    for n, shift in enumerate(shifts):
+        block = relative(place_ref[0], shift, -1)
+        lanes = pl.ds(pl.multiple_of(block * LANES, LANES), LANES)
+        copies.append(pltpu.make_async_copy(refs[n], out_ref.at[:, lanes], sems.at[n]))
+    for copy in copies:
+        copy.start()
+    for copy in copies:
+        copy.wait()
 
 
 def unpacked(place, shifts, pieces, begun=None):
     many = len(shifts)
-
-    def column(step, place_ref):
-        block = jnp.int32(0)
-        for n, shift in enumerate(shifts):
-            block = jnp.where(step == n, relative(place_ref[0], shift, -1), block)
-        return 0, block
-
+    anywhere = pl.BlockSpec(memory_space=pl.ANY)
     extra = [] if begun is None else [begun]
     return pl.pallas_call(
-        functools.partial(unpack_kernel, many),
-        grid_spec=pltpu.PrefetchScalarGridSpec(
-            num_scalar_prefetch=1,
-            grid=(many,),
-            in_specs=whole(many) + [pl.BlockSpec(memory_space=pl.ANY)] * len(extra),
-            out_specs=pl.BlockSpec((HELD * ROWS, LANES), column),
-        ),
+        functools.partial(unpack_kernel, shifts),
         out_shape=shape(HELD * ROWS, OWNERS * LANES),
+        in_specs=[SCALARS] + whole(many) + [anywhere] * len(extra),
+        out_specs=anywhere,
         input_output_aliases={1 + many: 0} if extra else {},
-        compiler_params=params(6),
+        scratch_shapes=[pltpu.SemaphoreType.DMA((many,))],
+        compiler_params=params(4),
         name="unpack",
     )(place, *pieces, *extra)
 
@@ -690,12 +723,12 @@
     seen = observed(flat, obs_index[None], lax.axis_size(MEMBER[0]))
     same = exchanged(seen, MEMBER[0])
 
-    kept, given = packed_blocks(place, flat, seen)
+    joint, given = packed_blocks(place, flat, seen)
     wide_counts = jnp.broadcast_to(newton_counts[:, None], (MEMBERS, LANES))
-    same, kept, given, wide_counts = lax.optimization_barrier((same, kept, given, wide_counts))
+    same, joint, given, wide_counts = lax.optimization_barrier((same, joint, given, wide_counts))
     other = along(same, MEMBER[1], 1)
     taken = along(given, MEMBER[1], 1)
-    joint = [jnp.stack([kept[n], taken[n]]) for n in range(OWNERS // 2)]
+    joint = filled(taken, joint)
 
     pieces = [joint[0]] + [along(joint[n], MEMBER[0], -n) for n in range(1, OWNERS // 2)]
     copies = lax.axis_size(SPACE[0])

time: 124 us -> 122 us (0.984); the launches traced: 124 us -> 121 us
  other arithmetic: 2.68 us -> 0.1 us
    another operation x4 -> x0, other arithmetic: 2.58 us -> none  [on_device(): joint = [jnp.stack([kept[n], taken[n]]) for n in range(OWNERS // 2)]]
    ppermute x5, waiting for transfers between devices: 1.68 us -> 3.49 us  [along(): lax.ppermute(array, axis, [(i, (i + step) % peers) for i in range(peers)])]
    pallas_call x3 -> x4, Pallas kernels: 6.71 us -> 7.39 us  [the longest x1 3.35 us: packed_blocks(): pl.pallas_call(pack_kernel, out_shape=[shape(2, SENT_ROWS, HELD, LANES)]...]
    unnamed x22 -> x20, local copies, waits for them, and re-layouts: 3.31 us -> 3.3 us
  transfers between devices with their start and end apart: 16 -> 16, of which waited for: 3 -> 4; matrix products, arithmetic and copies ran while one was open for 3% -> 0% of each run, Pallas kernels for 29% -> 30%
where the time goes in v7:
time: 122 us; the launch traced here: 121 us
  Pallas kernels  48.3 us (40%)
  starting transfers between devices  34.6 us (28%)
  blocking collectives  23.9 us (20%)
  waiting for transfers between devices  9.13 us (7%)
  local copies, waits for them, and re-layouts  4.09 us (3%)
    all_to_all x2, blocking collectives, exchanged(): return lax.all_to_all(copies, axis, split_axis=0, concat_axis=0, tiled=True)  23.9 us
    pallas_call x5, Pallas kernels, forecasts(): pl.pallas_call(functools.partial(forecast_kernel, shifts), out_shape=[sha...  19 us
    pallas_call x1, Pallas kernels, transform_of(): pl.pallas_call(root_kernel, out_shape=shape(MEMBERS, MEMBERS), in_specs=[...  12.4 us
    all_to_all x2, starting transfers between devices, exchanged(): return lax.all_to_all(copies, axis, split_axis=0, concat_axis=0, tiled=True)  11.9 us
    ppermute x7, starting transfers between devices, to_owner(): return lax.ppermute(array, MEMBER, pairs)  10.7 us
    ppermute x2, starting transfers between devices, to_strips_beside(): return lax.ppermute(array, SPACE, pairs)  7.56 us
    ppermute x5, starting transfers between devices, along(): lax.ppermute(array, axis, [(i, (i + step) % peers) for i in range(peers)])  4.5 us
    pallas_call x1, Pallas kernels, observed(): pl.pallas_call(observe_kernel, out_shape=shape(copies, HELD, obs_index.sh...  4.47 us
  transfers between devices with their start and end apart: 16, of which 4 were waited for; matrix products, arithmetic and copies ran while one was open for 0% of the time, Pallas kernels for 30%

profile of v7, /device:TPU:33, one launch (start us, length us, event | category | flops | bytes accessed | tf_op | source)
XLA Modules:
  0.0 120.5 jit_solution(17850290827310528690)
XLA Ops:
  0.0 1.6 %copy-done = f32[32,16,1024]{2,1,0:T(8,128)S(1)} copy-done((f32[32,16,1024]{2,1,0:T(8,128)S(1)}, f32[32,16,1024]{2,1,0:T(8,128)}, u32[]{:S(2)}) %copy-start) | copy-done | bytes 2097176
  2.3 4.5 %observe.1.after_ref = f32[4,32,1024]{2,1,0:T(8,128)} custom-call(s32[1,1024]{1,0:T(1,128)S(1)} %bitcast.10, f32[512,1024]{1,0:T(8,128)S(1)} %bitcast.8), custom_call_target="tpu_custom_call" | custom-call | tf_op jit(solution)/shard_map/observe/pallas_call | solution.py:88
  6.8 4.3 %all-to-all-start = ((f32[4,32,1024]{2,1,0:T(8,128)}), f32[4,32,1024]{2,1,0:T(8,128)}, u32[]{:S(2)}, u32[]{:S(2)}) async-start(f32[4,32,1024]{2,1,0:T(8,128)} %observe.1.after_ref), calls=%async_computation | async-start | bytes 1048576 | tf_op jit(solution)/shard_map/all_to_all | solution.py:690
  11.2 3.3 %pack.1 = (f32[2,17,32,128]{3,2,1,0:T(8,128)S(1)}, f32[2,17,32,128]{3,2,1,0:T(8,128)S(1)}, f32[2,17,32,128]{3,2,1,0:T(8,128)}, f32[2,17,32,128]{3,2,1,0:T(8,128)}, f32[4,17,32,128]{3,2,1,0:T(8,128)S(1)}) custom-call(s32[3]{0:T(128)S(1)} %pad_add_fusion.place_ref.refs_0_, f32[512,1024]{1,0:T(8,128)S(1)} %bitcast.9, f32[4,32,1024]{2,1,0:T(8,128)} %observe.1.after_ref), custom_call_target="tpu_custom_call" | custom-call | tf_op jit(solution)/shard_map/pack/pallas_call | solution.py:171
  15.5 4.0 %all-to-all-done.same_ref = f32[4,32,1024]{2,1,0:T(8,128)} async-done(((f32[4,32,1024]{2,1,0:T(8,128)}), f32[4,32,1024]{2,1,0:T(8,128)}, u32[]{:S(2)}, u32[]{:S(2)}) %all-to-all-start) | async-done | bytes 524320 | tf_op jit(solution)/shard_map/all_to_all | solution.py:690
  19.5 2.2 %collective-permute-start.1 = (f32[4,17,32,128]{3,2,1,0:T(8,128)}, f32[4,17,32,128]{3,2,1,0:T(8,128)S(1)}, u32[]{:S(2)}, u32[]{:S(2)}) collective-permute-start(f32[4,17,32,128]{3,2,1,0:T(8,128)} %copy-done.7), channel_id=1, source_target_pairs={{0,32},{32,0},{1,33},{33,1},{2,34},{34,2},{3,35},{35,3},{4,36},{36... | collective-permute-start | bytes 3342344 | tf_op jit(solution)/shard_map/ppermute | solution.py:699
  21.9 2.5 %collective-permute-done.1.taken_ref = f32[4,17,32,128]{3,2,1,0:T(8,128)S(1)} collective-permute-done((f32[4,17,32,128]{3,2,1,0:T(8,128)}, f32[4,17,32,128]{3,2,1,0:T(8,128)S(1)}, u32[]{:S(2)}, u32[]{:S(2)}) %collective-permute-start.1) | collective-permute-done | bytes 1114144 | tf_op jit(solution)/shard_map/ppermute | solution.py:699
  27.6 2.0 %gram.1 = f32[8,48,128]{2,1,0:T(8,128)S(1)} custom-call(s32[3]{0:T(128)S(1)} %pad_add_fusion.place_ref.refs_0_, f32[4,32,1024]{2,1,0:T(8,128)} %all-to-all-done.same_ref, f32[4,32,1024]{2,1,0:T(8,128)S(1)} %collective-permute-done.other_ref, f32[1,1024]{1,0:T(1,128)S(1)} %bitcast.11, f32[1,1024]{1,0:T(1,128)S(1)} %bitcast.12), custom_call_target="tpu_custom_call" | custom-call | flops 10000000000 | bytes 1000000 | tf_op jit(solution)/shard_map/gram/pallas_call | solution.py:272
  29.5 15.4 %all_to_all.20 = f32[8,48,128]{2,1,0:T(8,128)S(1)} all-to-all(f32[8,48,128]{2,1,0:T(8,128)S(1)} %gram.1), channel_id=1, replica_groups=mesh['member_0'=4,'member_1'=2,'space_0'=8,'space_1'=4] {'space_0'}, dimensions={0} | all-to-all | bytes 393216 | tf_op jit(solution)/shard_map/all_to_all | solution.py:690
  45.0 8.5 %all_to_all.21 = f32[4,48,128]{2,1,0:T(8,128)S(1)} all-to-all(f32[4,48,128]{2,1,0:T(8,128)S(1)} %broadcast_in_dim.25), channel_id=1, replica_groups=mesh['member_0'=4,'member_1'=2,'space_0'=8,'space_1'=4] {'space_1'}, dimensions={0} | all-to-all | bytes 196608 | tf_op jit(solution)/shard_map/all_to_all | solution.py:690
  55.2 7.6 %all-to-all-start.3 = ((f32[8,48,128]{2,1,0:T(8,128)}), f32[8,48,128]{2,1,0:T(8,128)}, u32[]{:S(2)}, u32[]{:S(2)}) async-start(f32[8,48,128]{2,1,0:T(8,128)} %broadcast_in_dim.26), calls=%async_computation.3 | async-start | bytes 393216 | tf_op jit(solution)/shard_map/all_to_all | solution.py:690
  63.8 2.2 %collective-permute-start.5 = (f32[816,128]{1,0:T(8,128)}, f32[816,128]{1,0:T(8,128)S(1)}, u32[]{:S(2)}, u32[]{:S(2)}) collective-permute-start(f32[816,128]{1,0:T(8,128)} %get-tuple-element.96), channel_id=1, source_target_pairs={{0,1},{1,2},{2,3},{3,4},{4,5},{5,6},{6,7},{7,8},{8,9},{9,10},{10,1... | collective-permute-start | bytes 1253384 | tf_op jit(solution)/shard_map/ppermute | solution.py:711
  66.0 5.4 %collective-permute-start.6 = (f32[816,128]{1,0:T(8,128)}, f32[816,128]{1,0:T(8,128)S(1)}, u32[]{:S(2)}, u32[]{:S(2)}) collective-permute-start(f32[816,128]{1,0:T(8,128)} %get-tuple-element.97), channel_id=1, source_target_pairs={{1,0},{2,1},{3,2},{4,3},{5,4},{6,5},{7,6},{8,7},{9,8},{10,9},{11,1... | collective-permute-start | bytes 1253384 | tf_op jit(solution)/shard_map/ppermute | solution.py:711
  71.4 12.4 %root.1.refs_4_ = f32[256,256]{1,0:T(8,128)S(1)} custom-call(s32[3]{0:T(128)S(1)} %pad_add_fusion.place_ref.refs_0_, f32[8,48,128]{2,1,0:T(8,128)} %all-to-all-done.3.parts_ref), custom_call_target="tpu_custom_call" | custom-call | flops 10000000000 | bytes 1000000 | tf_op jit(solution)/shard_map/root/pallas_call | solution.py:353
  83.8 2.0 %analyse.1 = (f32[5,20,8,128]{3,2,1,0:T(8,128)S(1)}, f32[6,8,128]{2,1,0:T(8,128)S(1)}, f32[21,32,128]{2,1,0:T(8,128)S(1)}, f32[21,32,128]{2,1,0:T(8,128)S(1)}, f...) custom-call(s32[3]{0:T(128)S(1)} %pad_add_fusion.place_ref.refs_0_, ...), custom_call_target="tpu_custom_call" | custom-call | tf_op jit(solution)/shard_map/analyse/pallas_call | solution.py:485
  85.8 3.7 %forecast.5 = f32[512,128]{1,0:T(8,128)S(1)} custom-call(s32[3]{0:T(128)S(1)} %pad_add_fusion.place_ref.refs_0_, s32[256]{0:T(256)S(1)} %copy-done.5, s32[256,128]{1,0:T(8,128)S(1)} %broadcast_in_dim.22.wide_ref, f32[5,20,8,128]{3,2,1,0:T(8,128)S(1)} %get-tuple-element.98.field_ref, f32[6,8,128]{2,1,0:T(8,128)S(1)} %get-tuple-element.99.edge_field_ref, ...), custom_call_target="tpu_custom_call" | custom-call | flops 1 | bytes 1 | tf_op jit(solution)/shard_map/forecast/pallas_call | solution.py:644
  89.6 1.6 %collective-permute-start.9 = (f32[512,128]{1,0:T(8,128)S(1)}, f32[512,128]{1,0:T(8,128)S(1)}, u32[]{:S(2)}, u32[]{:S(2)}) collective-permute-start(f32[512,128]{1,0:T(8,128)S(1)} %forecast.5), channel_id=1, source_target_pairs={{0,128},{32,160},{64,192},{96,224},{128,0},{160,32},{192,64},{224,... | collective-permute-start | bytes 786440 | tf_op jit(solution)/shard_map/ppermute | solution.py:705
  91.2 4.1 %forecast.6 = (f32[512,128]{1,0:T(8,128)S(1)}, f32[512,128]{1,0:T(8,128)S(1)}) custom-call(s32[3]{0:T(128)S(1)} %pad_add_fusion.place_ref.refs_0_, s32[256]{0:T(256)S(1)} %copy-done.5, s32[256,128]{1,0:T(8,128)S(1)} %broadcast_in_dim.22.wide_ref, f32[5,20,8,128]{3,2,1,0:T(8,128)S(1)} %get-tuple-element.98.field_ref, ...), custom_call_target="tpu_custom_call" | custom-call | flops 1 | bytes 1 | tf_op jit(solution)/shard_map/forecast/pallas_call | solution.py:644
  95.2 1.8 %collective-permute-start.12 = (f32[512,128]{1,0:T(8,128)S(1)}, f32[512,128]{1,0:T(8,128)S(1)}, u32[]{:S(2)}, u32[]{:S(2)}) collective-permute-start(f32[512,128]{1,0:T(8,128)S(1)} %get-tuple-element.138), channel_id=1, source_target_pairs={{0,64},{32,96},{64,128},{96,160},{128,192},{160,224},{192,0},{224,... | collective-permute-start | bytes 786440 | tf_op jit(solution)/shard_map/ppermute | solution.py:705
  98.0 4.8 %forecast.7 = (f32[512,128]{1,0:T(8,128)S(1)}, f32[512,128]{1,0:T(8,128)S(1)}) custom-call(s32[3]{0:T(128)S(1)} %pad_add_fusion.place_ref.refs_0_, s32[256]{0:T(256)S(1)} %copy-done.5, s32[256,128]{1,0:T(8,128)S(1)} %broadcast_in_dim.22.wide_ref, f32[5,20,8,128]{3,2,1,0:T(8,128)S(1)} %get-tuple-element.98.field_ref, ...), custom_call_target="tpu_custom_call" | custom-call | flops 1 | bytes 1 | tf_op jit(solution)/shard_map/forecast/pallas_call | solution.py:644
  105.1 4.1 %forecast.8 = (f32[512,128]{1,0:T(8,128)S(1)}, f32[512,128]{1,0:T(8,128)S(1)}) custom-call(s32[3]{0:T(128)S(1)} %pad_add_fusion.place_ref.refs_0_, s32[256]{0:T(256)S(1)} %copy-done.5, s32[256,128]{1,0:T(8,128)S(1)} %broadcast_in_dim.22.wide_ref, f32[5,20,8,128]{3,2,1,0:T(8,128)S(1)} %get-tuple-element.98.field_ref, ...), custom_call_target="tpu_custom_call" | custom-call | flops 1 | bytes 1 | tf_op jit(solution)/shard_map/forecast/pallas_call | solution.py:644
  109.2 3.3 %collective-permute-start.10 = (f32[512,128]{1,0:T(8,128)S(1)}, f32[512,128]{1,0:T(8,128)S(1)}, u32[]{:S(2)}, u32[]{:S(2)}) collective-permute-start(f32[512,128]{1,0:T(8,128)S(1)} %get-tuple-element.135), channel_id=1, source_target_pairs={{0,224},{32,192},{64,32},{96,0},{128,96},{160,64},{192,160},{224,1... | collective-permute-start | bytes 786440 | tf_op jit(solution)/shard_map/ppermute | solution.py:705
  113.3 2.3 %forecast.9.refs_0_ = f32[512,128]{1,0:T(8,128)S(1)} custom-call(s32[3]{0:T(128)S(1)} %pad_add_fusion.place_ref.refs_0_, s32[256]{0:T(256)S(1)} %copy-done.5, s32[256,128]{1,0:T(8,128)S(1)} %broadcast_in_dim.22.wide_ref, f32[5,20,8,128]{3,2,1,0:T(8,128)S(1)} %get-tuple-element.98.field_ref, f32[6,8,128]{2,1,0:T(8,128)S(1)} %get-tuple-element.99.edge_field_ref, ...), custom_call_target="tpu_custom_call" | custom-call | flops 1 | bytes 1 | tf_op jit(solution)/shard_map/forecast/pallas_call | solution.py:644
  117.2 1.7 %collective-permute-done.8.refs_1_ = f32[512,128]{1,0:T(8,128)S(1)} collective-permute-done((f32[512,128]{1,0:T(8,128)S(1)}, f32[512,128]{1,0:T(8,128)S(1)}, u32[]{:S(2)}, u32[]{:S(2)}) %collective-permute-start.8) | collective-permute-done | bytes 262176 | tf_op jit(solution)/shard_map/ppermute | solution.py:705
  (50 shorter events, 15.0 us)
Async XLA Ops:
  0.0 1.6 %copy-start = (f32[32,16,1024]{2,1,0:T(8,128)S(1)}, f32[32,16,1024]{2,1,0:T(8,128)}, u32[]{:S(2)}) copy-start(f32[32,16,1024]{2,1,0:T(8,128)} %param.8) | copy-start | bytes 6291460
  2.3 8.9 %copy-start.1 = (f32[32,16,1024]{2,1,0:T(8,128)S(1)}, f32[32,16,1024]{2,1,0:T(8,128)}, u32[]{:S(2)}) copy-start(f32[32,16,1024]{2,1,0:T(8,128)} %param.8) | copy-start | bytes 6291460
  6.8 12.7 %copy-start.5 = (s32[256]{0:T(256)S(1)}, s32[256]{0:T(256)}, u32[]{:S(2)}) copy-start(s32[256]{0:T(256)} %counts_ref.9) | copy-start | bytes 3076
  6.8 12.7 %all-to-all-start = ((f32[4,32,1024]{2,1,0:T(8,128)}), f32[4,32,1024]{2,1,0:T(8,128)}, u32[]{:S(2)}, u32[]{:S(2)}) async-start(f32[4,32,1024]{2,1,0:T(8,128)} %observe.1.after_ref), calls=%async_computation | async-start | bytes 1048576 | tf_op jit(solution)/shard_map/all_to_all | solution.py:690
  15.5 12.0 %copy-start.8 = (f32[1024]{0:T(1024)S(1)}, f32[1024]{0:T(1024)}, u32[]{:S(2)}) copy-start(f32[1024]{0:T(1024)} %param.10) | copy-start | bytes 12292
  15.5 12.0 %copy-start.9 = (f32[1024]{0:T(1024)S(1)}, f32[1024]{0:T(1024)}, u32[]{:S(2)}) copy-start(f32[1024]{0:T(1024)} %param.11) | copy-start | bytes 12292
  19.5 4.8 %collective-permute-start.1 = (f32[4,17,32,128]{3,2,1,0:T(8,128)}, f32[4,17,32,128]{3,2,1,0:T(8,128)S(1)}, u32[]{:S(2)}, u32[]{:S(2)}) collective-permute-start(f32[4,17,32,128]{3,2,1,0:T(8,128)} %copy-done.7), channel_id=1, source_target_pairs={{0,32},{32,0},{1,33},{33,1},{2,34},{34,2},{3,35},{35,3},{4,36},{36... | collective-permute-start | bytes 3342344 | tf_op jit(solution)/shard_map/ppermute | solution.py:699
  21.8 5.7 %collective-permute-start = (f32[4,32,1024]{2,1,0:T(8,128)}, f32[4,32,1024]{2,1,0:T(8,128)S(1)}, u32[]{:S(2)}, u32[]{:S(2)}) collective-permute-start(f32[4,32,1024]{2,1,0:T(8,128)} %all-to-all-done.same_ref), channel_id=1, source_target_pairs={{0,32},{32,0},{1,33},{33,1},{2,34},{34,2},{3,35},{35,3},{4,36},{36... | collective-permute-start | bytes 1572872 | tf_op jit(solution)/shard_map/ppermute | solution.py:699
  25.3 28.2 %collective-permute-start.2 = (f32[2,17,32,128]{3,2,1,0:T(8,128)S(1)}, f32[2,17,32,128]{3,2,1,0:T(8,128)S(1)}, u32[]{:S(2)}, u32[]{:S(2)}) collective-permute-start(f32[2,17,32,128]{3,2,1,0:T(8,128)S(1)} %get-tuple-element.88), channel_id=1, source_target_pairs={{0,192},{64,0},{128,64},{192,128},{1,193},{65,1},{129,65},{193,129... | collective-permute-start | bytes 1671176 | tf_op jit(solution)/shard_map/ppermute | solution.py:699
  26.3 27.2 %collective-permute-start.3 = (f32[2,17,32,128]{3,2,1,0:T(8,128)}, f32[2,17,32,128]{3,2,1,0:T(8,128)S(1)}, u32[]{:S(2)}, u32[]{:S(2)}) collective-permute-start(f32[2,17,32,128]{3,2,1,0:T(8,128)} %get-tuple-element.89), channel_id=1, source_target_pairs={{0,128},{64,192},{128,0},{192,64},{1,129},{65,193},{129,1},{193,65... | collective-permute-start | bytes 1671176 | tf_op jit(solution)/shard_map/ppermute | solution.py:699
  27.5 27.0 %collective-permute-start.4 = (f32[2,17,32,128]{3,2,1,0:T(8,128)}, f32[2,17,32,128]{3,2,1,0:T(8,128)S(1)}, u32[]{:S(2)}, u32[]{:S(2)}) collective-permute-start(f32[2,17,32,128]{3,2,1,0:T(8,128)} %get-tuple-element.90), channel_id=1, source_target_pairs={{0,64},{64,128},{128,192},{192,0},{1,65},{65,129},{129,193},{193,1... | collective-permute-start | bytes 1671176 | tf_op jit(solution)/shard_map/ppermute | solution.py:699
  27.5 35.3 %copy-start.2 = (f32[16,1024]{1,0:T(8,128)S(1)}, f32[16,1024]{1,0:T(8,128)}, u32[]{:S(2)}) copy-start(f32[16,1024]{1,0:T(8,128)} %refs_1_.1) | copy-start | bytes 196612
  27.5 35.2 %copy-start.3 = (f32[16,1024]{1,0:T(8,128)S(1)}, f32[16,1024]{1,0:T(8,128)}, u32[]{:S(2)}) copy-start(f32[16,1024]{1,0:T(8,128)} %refs_2_.1) | copy-start | bytes 196612
  27.5 35.2 %copy-start.4 = (f32[16,1024]{1,0:T(8,128)S(1)}, f32[16,1024]{1,0:T(8,128)}, u32[]{:S(2)}) copy-start(f32[16,1024]{1,0:T(8,128)} %refs_3_.1) | copy-start | bytes 196612
  55.2 16.1 %all-to-all-start.3 = ((f32[8,48,128]{2,1,0:T(8,128)}), f32[8,48,128]{2,1,0:T(8,128)}, u32[]{:S(2)}, u32[]{:S(2)}) async-start(f32[8,48,128]{2,1,0:T(8,128)} %broadcast_in_dim.26), calls=%async_computation.3 | async-start | bytes 393216 | tf_op jit(solution)/shard_map/all_to_all | solution.py:690
  63.8 20.0 %collective-permute-start.5 = (f32[816,128]{1,0:T(8,128)}, f32[816,128]{1,0:T(8,128)S(1)}, u32[]{:S(2)}, u32[]{:S(2)}) collective-permute-start(f32[816,128]{1,0:T(8,128)} %get-tuple-element.96), channel_id=1, source_target_pairs={{0,1},{1,2},{2,3},{3,4},{4,5},{5,6},{6,7},{7,8},{8,9},{9,10},{10,1... | collective-permute-start | bytes 1253384 | tf_op jit(solution)/shard_map/ppermute | solution.py:711
  66.0 17.8 %collective-permute-start.6 = (f32[816,128]{1,0:T(8,128)}, f32[816,128]{1,0:T(8,128)S(1)}, u32[]{:S(2)}, u32[]{:S(2)}) collective-permute-start(f32[816,128]{1,0:T(8,128)} %get-tuple-element.97), channel_id=1, source_target_pairs={{1,0},{2,1},{3,2},{4,3},{5,4},{6,5},{7,6},{8,7},{9,8},{10,9},{11,1... | collective-permute-start | bytes 1253384 | tf_op jit(solution)/shard_map/ppermute | solution.py:711
  89.6 15.5 %collective-permute-start.9 = (f32[512,128]{1,0:T(8,128)S(1)}, f32[512,128]{1,0:T(8,128)S(1)}, u32[]{:S(2)}, u32[]{:S(2)}) collective-permute-start(f32[512,128]{1,0:T(8,128)S(1)} %forecast.5), channel_id=1, source_target_pairs={{0,128},{32,160},{64,192},{96,224},{128,0},{160,32},{192,64},{224,... | collective-permute-start | bytes 786440 | tf_op jit(solution)/shard_map/ppermute | solution.py:705
  95.2 17.3 %collective-permute-start.12 = (f32[512,128]{1,0:T(8,128)S(1)}, f32[512,128]{1,0:T(8,128)S(1)}, u32[]{:S(2)}, u32[]{:S(2)}) collective-permute-start(f32[512,128]{1,0:T(8,128)S(1)} %get-tuple-element.138), channel_id=1, source_target_pairs={{0,64},{32,96},{64,128},{96,160},{128,192},{160,224},{192,0},{224,... | collective-permute-start | bytes 786440 | tf_op jit(solution)/shard_map/ppermute | solution.py:705
  97.0 16.2 %collective-permute-start.13 = (f32[512,128]{1,0:T(8,128)S(1)}, f32[512,128]{1,0:T(8,128)S(1)}, u32[]{:S(2)}, u32[]{:S(2)}) collective-permute-start(f32[512,128]{1,0:T(8,128)S(1)} %get-tuple-element.139), channel_id=1, source_target_pairs={{0,192},{32,224},{64,0},{96,32},{128,64},{160,96},{192,128},{224,1... | collective-permute-start | bytes 786440 | tf_op jit(solution)/shard_map/ppermute | solution.py:705
  102.8 14.4 %collective-permute-start.7 = (f32[512,128]{1,0:T(8,128)S(1)}, f32[512,128]{1,0:T(8,128)S(1)}, u32[]{:S(2)}, u32[]{:S(2)}) collective-permute-start(f32[512,128]{1,0:T(8,128)S(1)} %get-tuple-element.124), channel_id=1, source_target_pairs={{0,160},{32,128},{64,224},{96,192},{128,32},{160,0},{192,96},{224,... | collective-permute-start | bytes 786440 | tf_op jit(solution)/shard_map/ppermute | solution.py:705
  103.9 14.9 %collective-permute-start.8 = (f32[512,128]{1,0:T(8,128)S(1)}, f32[512,128]{1,0:T(8,128)S(1)}, u32[]{:S(2)}, u32[]{:S(2)}) collective-permute-start(f32[512,128]{1,0:T(8,128)S(1)} %get-tuple-element.125), channel_id=1, source_target_pairs={{0,96},{32,64},{64,160},{96,128},{128,224},{160,192},{192,32},{224... | collective-permute-start | bytes 786440 | tf_op jit(solution)/shard_map/ppermute | solution.py:705
  109.2 9.6 %collective-permute-start.10 = (f32[512,128]{1,0:T(8,128)S(1)}, f32[512,128]{1,0:T(8,128)S(1)}, u32[]{:S(2)}, u32[]{:S(2)}) collective-permute-start(f32[512,128]{1,0:T(8,128)S(1)} %get-tuple-element.135), channel_id=1, source_target_pairs={{0,224},{32,192},{64,32},{96,0},{128,96},{160,64},{192,160},{224,1... | collective-permute-start | bytes 786440 | tf_op jit(solution)/shard_map/ppermute | solution.py:705
  112.5 6.3 %collective-permute-start.11 = (f32[512,128]{1,0:T(8,128)S(1)}, f32[512,128]{1,0:T(8,128)S(1)}, u32[]{:S(2)}, u32[]{:S(2)}) collective-permute-start(f32[512,128]{1,0:T(8,128)S(1)} %get-tuple-element.136), channel_id=1, source_target_pairs={{0,32},{32,0},{64,96},{96,64},{128,160},{160,128},{192,224},{224,1... | collective-permute-start | bytes 786440 | tf_op jit(solution)/shard_map/ppermute | solution.py:705
  (2 other events, 1.7 us)

commit v8 on v7

--- a/solution.py
+++ b/solution.py
@@ -66,6 +66,7 @@
     rest = values - high.astype(F32)
     middle = rest.astype(jnp.bfloat16)
     low = (rest - middle.astype(F32)).astype(jnp.bfloat16)
+    parts = jnp.concatenate([low, middle, high], axis=0)
     width = values.shape[1]
     step = 256
     for first in range(0, index_ref.shape[1], step):
@@ -74,10 +75,8 @@
         column = cell - row * width
         places = lax.broadcasted_iota(jnp.int32, (width, step), 0)
         chosen = (places == column).astype(F32).astype(jnp.bfloat16)
-        picked = jnp.dot(low, chosen, preferred_element_type=F32)
-        picked += jnp.dot(middle, chosen, preferred_element_type=F32)
-        picked += jnp.dot(high, chosen, preferred_element_type=F32)
-        picked = picked.reshape(HELD, ROWS, step)
+        terms = jnp.dot(parts, chosen, preferred_element_type=F32).reshape(3, HELD, ROWS, step)
+        picked = (terms[0] + terms[1]) + terms[2]
         rows = lax.broadcasted_iota(jnp.int32, (ROWS, step), 0)
         seen = jnp.sum(jnp.where((rows == row)[None], picked, 0.0), axis=1)
         for copy in range(seen_ref.shape[0]):
@@ -690,8 +689,21 @@
     return lax.all_to_all(copies, axis, split_axis=0, concat_axis=0, tiled=True)
 
 
-def shared(array, axis):
-    return exchanged(jnp.broadcast_to(array, (lax.axis_size(axis), *array.shape)), axis)
+def total_kernel(parts_ref, out_ref):
+    total = jnp.sum(parts_ref[...], axis=0)
+    for copy in range(out_ref.shape[0]):
+        out_ref[copy] = total
+
+
+def totals(parts, copies):
+    return pl.pallas_call(
+        total_kernel,
+        out_shape=shape(copies, *parts.shape[1:]),
+        in_specs=whole(1),
+        out_specs=whole(1)[0],
+        compiler_params=params(4),
+        name="total",
+    )(parts)
 
 
 def along(array, axis, step):
@@ -733,10 +745,10 @@
     pieces = [joint[0]] + [along(joint[n], MEMBER[0], -n) for n in range(1, OWNERS // 2)]
     copies = lax.axis_size(SPACE[0])
     part = gram_blocks(place, same, other, obs_value[None], obs_scale[None], copies)
-    part = jnp.sum(exchanged(part, SPACE[0]), axis=0)
-    part = jnp.sum(shared(part, SPACE[1]), axis=0)
+    part = exchanged(totals(exchanged(part, SPACE[0]), lax.axis_size(SPACE[1])), SPACE[1])
+    part = totals(part, OWNERS)
     part, pieces = lax.optimization_barrier((part, pieces))
-    parts = shared(part, MEMBER)
+    parts = exchanged(part, MEMBER)
     cell_fields = (ksat, storage, recharge)
     down, up = borders(pieces, cell_fields)
     above = to_strips_beside(up, 1)

time: 122 us -> 122 us (level); the launches traced: 121 us -> 122 us
    ppermute x7, waiting for transfers between devices: 1.67 us -> 3.06 us  [to_owner(): return lax.ppermute(array, MEMBER, pairs)]
  transfers between devices with their start and end apart: 16 -> 16, of which waited for: 4 -> 4; matrix products, arithmetic and copies ran while one was open for 0% -> 0% of each run, Pallas kernels for 30% -> 32%
where the time goes in v8:
time: 122 us
  Pallas kernels  48.9 us (40%)
  starting transfers between devices  35.3 us (29%)
  blocking collectives  23.9 us (20%)
  waiting for transfers between devices  9.83 us (8%)
  local copies, waits for them, and re-layouts  3.39 us (3%)
    all_to_all x2, blocking collectives, exchanged(): return lax.all_to_all(copies, axis, split_axis=0, concat_axis=0, tiled=True)  23.9 us
    pallas_call x5, Pallas kernels, forecasts(): pl.pallas_call(functools.partial(forecast_kernel, shifts), out_shape=[sha...  19.1 us
    all_to_all x2, starting transfers between devices, exchanged(): return lax.all_to_all(copies, axis, split_axis=0, concat_axis=0, tiled=True)  12.5 us
    pallas_call x1, Pallas kernels, transform_of(): pl.pallas_call(root_kernel, out_shape=shape(MEMBERS, MEMBERS), in_specs=[...  12.4 us
    ppermute x7, starting transfers between devices, to_owner(): return lax.ppermute(array, MEMBER, pairs)  10.7 us
    ppermute x2, starting transfers between devices, to_strips_beside(): return lax.ppermute(array, SPACE, pairs)  7.56 us
    ppermute x5, starting transfers between devices, along(): lax.ppermute(array, axis, [(i, (i + step) % peers) for i in range(peers)])  4.51 us
    pallas_call x1, Pallas kernels, observed(): pl.pallas_call(observe_kernel, out_shape=shape(copies, HELD, obs_index.sh...  4.29 us
  transfers between devices with their start and end apart: 16, of which 4 were waited for; matrix products, arithmetic and copies ran while one was open for 0% of the time, Pallas kernels for 32%

profile of v8, /device:TPU:33, one launch (start us, length us, event | category | flops | bytes accessed | tf_op | source)
XLA Modules:
  0.0 121.8 jit_solution(7036635218566286776)
XLA Ops:
  0.0 1.6 %copy-done = f32[32,16,1024]{2,1,0:T(8,128)S(1)} copy-done((f32[32,16,1024]{2,1,0:T(8,128)S(1)}, f32[32,16,1024]{2,1,0:T(8,128)}, u32[]{:S(2)}) %copy-start) | copy-done | bytes 2097176
  2.3 4.3 %observe.1.after_ref = f32[4,32,1024]{2,1,0:T(8,128)} custom-call(s32[1,1024]{1,0:T(1,128)S(1)} %bitcast.10, f32[512,1024]{1,0:T(8,128)S(1)} %bitcast.8), custom_call_target="tpu_custom_call" | custom-call | tf_op jit(solution)/shard_map/observe/pallas_call | solution.py:87
  6.6 4.3 %all-to-all-start = ((f32[4,32,1024]{2,1,0:T(8,128)}), f32[4,32,1024]{2,1,0:T(8,128)}, u32[]{:S(2)}, u32[]{:S(2)}) async-start(f32[4,32,1024]{2,1,0:T(8,128)} %observe.1.after_ref), calls=%async_computation | async-start | bytes 1048576 | tf_op jit(solution)/shard_map/all_to_all | solution.py:689
  11.0 3.4 %pack.1 = (f32[2,17,32,128]{3,2,1,0:T(8,128)S(1)}, f32[2,17,32,128]{3,2,1,0:T(8,128)S(1)}, f32[2,17,32,128]{3,2,1,0:T(8,128)}, f32[2,17,32,128]{3,2,1,0:T(8,128)}, f32[4,17,32,128]{3,2,1,0:T(8,128)S(1)}) custom-call(s32[3]{0:T(128)S(1)} %pad_add_fusion.place_ref.refs_0_, f32[512,1024]{1,0:T(8,128)S(1)} %bitcast.9, f32[4,32,1024]{2,1,0:T(8,128)} %observe.1.after_ref), custom_call_target="tpu_custom_call" | custom-call | tf_op jit(solution)/shard_map/pack/pallas_call | solution.py:170
  15.3 3.9 %all-to-all-done.same_ref = f32[4,32,1024]{2,1,0:T(8,128)} async-done(((f32[4,32,1024]{2,1,0:T(8,128)}), f32[4,32,1024]{2,1,0:T(8,128)}, u32[]{:S(2)}, u32[]{:S(2)}) %all-to-all-start) | async-done | bytes 524320 | tf_op jit(solution)/shard_map/all_to_all | solution.py:689
  19.4 2.3 %collective-permute-start.1 = (f32[4,17,32,128]{3,2,1,0:T(8,128)}, f32[4,17,32,128]{3,2,1,0:T(8,128)S(1)}, u32[]{:S(2)}, u32[]{:S(2)}) collective-permute-start(f32[4,17,32,128]{3,2,1,0:T(8,128)} %copy-done.7), channel_id=1, source_target_pairs={{0,32},{32,0},{1,33},{33,1},{2,34},{34,2},{3,35},{35,3},{4,36},{36... | collective-permute-start | bytes 3342344 | tf_op jit(solution)/shard_map/ppermute | solution.py:711
  21.7 2.5 %collective-permute-done.1.taken_ref = f32[4,17,32,128]{3,2,1,0:T(8,128)S(1)} collective-permute-done((f32[4,17,32,128]{3,2,1,0:T(8,128)}, f32[4,17,32,128]{3,2,1,0:T(8,128)S(1)}, u32[]{:S(2)}, u32[]{:S(2)}) %collective-permute-start.1) | collective-permute-done | bytes 1114144 | tf_op jit(solution)/shard_map/ppermute | solution.py:711
  27.4 2.0 %gram.1 = f32[8,48,128]{2,1,0:T(8,128)S(1)} custom-call(s32[3]{0:T(128)S(1)} %pad_add_fusion.place_ref.refs_0_, f32[4,32,1024]{2,1,0:T(8,128)} %all-to-all-done.same_ref, f32[4,32,1024]{2,1,0:T(8,128)S(1)} %collective-permute-done.other_ref, f32[1,1024]{1,0:T(1,128)S(1)} %bitcast.11, f32[1,1024]{1,0:T(1,128)S(1)} %bitcast.12), custom_call_target="tpu_custom_call" | custom-call | flops 10000000000 | bytes 1000000 | tf_op jit(solution)/shard_map/gram/pallas_call | solution.py:271
  29.3 15.4 %all_to_all.20.parts_ref = f32[8,48,128]{2,1,0:T(8,128)S(1)} all-to-all(f32[8,48,128]{2,1,0:T(8,128)S(1)} %gram.1), channel_id=1, replica_groups=mesh['member_0'=4,'member_1'=2,'space_0'=8,'space_1'=4] {'space_0'}, dimensions={0} | all-to-all | bytes 393216 | tf_op jit(solution)/shard_map/all_to_all | solution.py:689
  44.8 8.5 %all_to_all.21.parts_ref = f32[4,48,128]{2,1,0:T(8,128)S(1)} all-to-all(f32[4,48,128]{2,1,0:T(8,128)S(1)} %total.2), channel_id=1, replica_groups=mesh['member_0'=4,'member_1'=2,'space_0'=8,'space_1'=4] {'space_1'}, dimensions={0} | all-to-all | bytes 196608 | tf_op jit(solution)/shard_map/all_to_all | solution.py:689
  54.3 8.2 %all-to-all-start.3 = ((f32[8,48,128]{2,1,0:T(8,128)}), f32[8,48,128]{2,1,0:T(8,128)}, u32[]{:S(2)}, u32[]{:S(2)}) async-start(f32[8,48,128]{2,1,0:T(8,128)} %total.3), calls=%async_computation.3 | async-start | bytes 393216 | tf_op jit(solution)/shard_map/all_to_all | solution.py:689
  63.5 2.2 %collective-permute-start.5 = (f32[816,128]{1,0:T(8,128)}, f32[816,128]{1,0:T(8,128)S(1)}, u32[]{:S(2)}, u32[]{:S(2)}) collective-permute-start(f32[816,128]{1,0:T(8,128)} %get-tuple-element.96), channel_id=1, source_target_pairs={{0,1},{1,2},{2,3},{3,4},{4,5},{5,6},{6,7},{7,8},{8,9},{9,10},{10,1... | collective-permute-start | bytes 1253384 | tf_op jit(solution)/shard_map/ppermute | solution.py:723
  65.7 5.4 %collective-permute-start.6 = (f32[816,128]{1,0:T(8,128)}, f32[816,128]{1,0:T(8,128)S(1)}, u32[]{:S(2)}, u32[]{:S(2)}) collective-permute-start(f32[816,128]{1,0:T(8,128)} %get-tuple-element.97), channel_id=1, source_target_pairs={{1,0},{2,1},{3,2},{4,3},{5,4},{6,5},{7,6},{8,7},{9,8},{10,9},{11,1... | collective-permute-start | bytes 1253384 | tf_op jit(solution)/shard_map/ppermute | solution.py:723
  71.1 12.4 %root.1.refs_4_ = f32[256,256]{1,0:T(8,128)S(1)} custom-call(s32[3]{0:T(128)S(1)} %pad_add_fusion.place_ref.refs_0_, f32[8,48,128]{2,1,0:T(8,128)} %all-to-all-done.3.parts_ref), custom_call_target="tpu_custom_call" | custom-call | flops 10000000000 | bytes 1000000 | tf_op jit(solution)/shard_map/root/pallas_call | solution.py:352
  83.5 2.0 %analyse.1 = (f32[5,20,8,128]{3,2,1,0:T(8,128)S(1)}, f32[6,8,128]{2,1,0:T(8,128)S(1)}, f32[21,32,128]{2,1,0:T(8,128)S(1)}, f32[21,32,128]{2,1,0:T(8,128)S(1)}, f...) custom-call(s32[3]{0:T(128)S(1)} %pad_add_fusion.place_ref.refs_0_, ...), custom_call_target="tpu_custom_call" | custom-call | tf_op jit(solution)/shard_map/analyse/pallas_call | solution.py:484
  85.6 2.3 %forecast.5 = f32[512,128]{1,0:T(8,128)S(1)} custom-call(s32[3]{0:T(128)S(1)} %pad_add_fusion.place_ref.refs_0_, s32[256]{0:T(256)S(1)} %copy-done.5, s32[256,128]{1,0:T(8,128)S(1)} %broadcast_in_dim.16.wide_ref, f32[5,20,8,128]{3,2,1,0:T(8,128)S(1)} %get-tuple-element.98.field_ref, f32[6,8,128]{2,1,0:T(8,128)S(1)} %get-tuple-element.99.edge_field_ref, ...), custom_call_target="tpu_custom_call" | custom-call | flops 1 | bytes 1 | tf_op jit(solution)/shard_map/forecast/pallas_call | solution.py:643
  87.9 3.0 %collective-permute-start.9 = (f32[512,128]{1,0:T(8,128)S(1)}, f32[512,128]{1,0:T(8,128)S(1)}, u32[]{:S(2)}, u32[]{:S(2)}) collective-permute-start(f32[512,128]{1,0:T(8,128)S(1)} %forecast.5), channel_id=1, source_target_pairs={{0,128},{32,160},{64,192},{96,224},{128,0},{160,32},{192,64},{224,... | collective-permute-start | bytes 786440 | tf_op jit(solution)/shard_map/ppermute | solution.py:717
  90.9 4.8 %forecast.6 = (f32[512,128]{1,0:T(8,128)S(1)}, f32[512,128]{1,0:T(8,128)S(1)}) custom-call(s32[3]{0:T(128)S(1)} %pad_add_fusion.place_ref.refs_0_, s32[256]{0:T(256)S(1)} %copy-done.5, s32[256,128]{1,0:T(8,128)S(1)} %broadcast_in_dim.16.wide_ref, f32[5,20,8,128]{3,2,1,0:T(8,128)S(1)} %get-tuple-element.98.field_ref, ...), custom_call_target="tpu_custom_call" | custom-call | flops 1 | bytes 1 | tf_op jit(solution)/shard_map/forecast/pallas_call | solution.py:643
  96.1 2.4 %collective-permute-start.13 = (f32[512,128]{1,0:T(8,128)S(1)}, f32[512,128]{1,0:T(8,128)S(1)}, u32[]{:S(2)}, u32[]{:S(2)}) collective-permute-start(f32[512,128]{1,0:T(8,128)S(1)} %get-tuple-element.139), channel_id=1, source_target_pairs={{0,192},{32,224},{64,0},{96,32},{128,64},{160,96},{192,128},{224,1... | collective-permute-start | bytes 786440 | tf_op jit(solution)/shard_map/ppermute | solution.py:717
  98.5 5.5 %forecast.7 = (f32[512,128]{1,0:T(8,128)S(1)}, f32[512,128]{1,0:T(8,128)S(1)}) custom-call(s32[3]{0:T(128)S(1)} %pad_add_fusion.place_ref.refs_0_, s32[256]{0:T(256)S(1)} %copy-done.5, s32[256,128]{1,0:T(8,128)S(1)} %broadcast_in_dim.16.wide_ref, f32[5,20,8,128]{3,2,1,0:T(8,128)S(1)} %get-tuple-element.98.field_ref, ...), custom_call_target="tpu_custom_call" | custom-call | flops 1 | bytes 1 | tf_op jit(solution)/shard_map/forecast/pallas_call | solution.py:643
  105.0 4.1 %forecast.8 = (f32[512,128]{1,0:T(8,128)S(1)}, f32[512,128]{1,0:T(8,128)S(1)}) custom-call(s32[3]{0:T(128)S(1)} %pad_add_fusion.place_ref.refs_0_, s32[256]{0:T(256)S(1)} %copy-done.5, s32[256,128]{1,0:T(8,128)S(1)} %broadcast_in_dim.16.wide_ref, f32[5,20,8,128]{3,2,1,0:T(8,128)S(1)} %get-tuple-element.98.field_ref, ...), custom_call_target="tpu_custom_call" | custom-call | flops 1 | bytes 1 | tf_op jit(solution)/shard_map/forecast/pallas_call | solution.py:643
  109.1 2.5 %collective-permute-start.10 = (f32[512,128]{1,0:T(8,128)S(1)}, f32[512,128]{1,0:T(8,128)S(1)}, u32[]{:S(2)}, u32[]{:S(2)}) collective-permute-start(f32[512,128]{1,0:T(8,128)S(1)} %get-tuple-element.135), channel_id=1, source_target_pairs={{0,224},{32,192},{64,32},{96,0},{128,96},{160,64},{192,160},{224,1... | collective-permute-start | bytes 786440 | tf_op jit(solution)/shard_map/ppermute | solution.py:717
  113.1 2.3 %forecast.9.refs_0_ = f32[512,128]{1,0:T(8,128)S(1)} custom-call(s32[3]{0:T(128)S(1)} %pad_add_fusion.place_ref.refs_0_, s32[256]{0:T(256)S(1)} %copy-done.5, s32[256,128]{1,0:T(8,128)S(1)} %broadcast_in_dim.16.wide_ref, f32[5,20,8,128]{3,2,1,0:T(8,128)S(1)} %get-tuple-element.98.field_ref, f32[6,8,128]{2,1,0:T(8,128)S(1)} %get-tuple-element.99.edge_field_ref, ...), custom_call_target="tpu_custom_call" | custom-call | flops 1 | bytes 1 | tf_op jit(solution)/shard_map/forecast/pallas_call | solution.py:643
  117.0 3.0 %collective-permute-done.8.refs_1_ = f32[512,128]{1,0:T(8,128)S(1)} collective-permute-done((f32[512,128]{1,0:T(8,128)S(1)}, f32[512,128]{1,0:T(8,128)S(1)}, u32[]{:S(2)}, u32[]{:S(2)}) %collective-permute-start.8) | collective-permute-done | bytes 262176 | tf_op jit(solution)/shard_map/ppermute | solution.py:717
  (48 shorter events, 13.0 us)
Async XLA Ops:
  0.0 1.6 %copy-start = (f32[32,16,1024]{2,1,0:T(8,128)S(1)}, f32[32,16,1024]{2,1,0:T(8,128)}, u32[]{:S(2)}) copy-start(f32[32,16,1024]{2,1,0:T(8,128)} %param.8) | copy-start | bytes 6291460
  2.3 8.7 %copy-start.1 = (f32[32,16,1024]{2,1,0:T(8,128)S(1)}, f32[32,16,1024]{2,1,0:T(8,128)}, u32[]{:S(2)}) copy-start(f32[32,16,1024]{2,1,0:T(8,128)} %param.8) | copy-start | bytes 6291460
  6.6 12.7 %copy-start.5 = (s32[256]{0:T(256)S(1)}, s32[256]{0:T(256)}, u32[]{:S(2)}) copy-start(s32[256]{0:T(256)} %counts_ref.9) | copy-start | bytes 3076
  6.6 12.7 %all-to-all-start = ((f32[4,32,1024]{2,1,0:T(8,128)}), f32[4,32,1024]{2,1,0:T(8,128)}, u32[]{:S(2)}, u32[]{:S(2)}) async-start(f32[4,32,1024]{2,1,0:T(8,128)} %observe.1.after_ref), calls=%async_computation | async-start | bytes 1048576 | tf_op jit(solution)/shard_map/all_to_all | solution.py:689
  15.3 12.0 %copy-start.8 = (f32[1024]{0:T(1024)S(1)}, f32[1024]{0:T(1024)}, u32[]{:S(2)}) copy-start(f32[1024]{0:T(1024)} %param.10) | copy-start | bytes 12292
  15.3 12.0 %copy-start.9 = (f32[1024]{0:T(1024)S(1)}, f32[1024]{0:T(1024)}, u32[]{:S(2)}) copy-start(f32[1024]{0:T(1024)} %param.11) | copy-start | bytes 12292
  19.4 4.8 %collective-permute-start.1 = (f32[4,17,32,128]{3,2,1,0:T(8,128)}, f32[4,17,32,128]{3,2,1,0:T(8,128)S(1)}, u32[]{:S(2)}, u32[]{:S(2)}) collective-permute-start(f32[4,17,32,128]{3,2,1,0:T(8,128)} %copy-done.7), channel_id=1, source_target_pairs={{0,32},{32,0},{1,33},{33,1},{2,34},{34,2},{3,35},{35,3},{4,36},{36... | collective-permute-start | bytes 3342344 | tf_op jit(solution)/shard_map/ppermute | solution.py:711
  21.6 5.7 %collective-permute-start = (f32[4,32,1024]{2,1,0:T(8,128)}, f32[4,32,1024]{2,1,0:T(8,128)S(1)}, u32[]{:S(2)}, u32[]{:S(2)}) collective-permute-start(f32[4,32,1024]{2,1,0:T(8,128)} %all-to-all-done.same_ref), channel_id=1, source_target_pairs={{0,32},{32,0},{1,33},{33,1},{2,34},{34,2},{3,35},{35,3},{4,36},{36... | collective-permute-start | bytes 1572872 | tf_op jit(solution)/shard_map/ppermute | solution.py:711
  25.1 28.8 %collective-permute-start.2 = (f32[2,17,32,128]{3,2,1,0:T(8,128)S(1)}, f32[2,17,32,128]{3,2,1,0:T(8,128)S(1)}, u32[]{:S(2)}, u32[]{:S(2)}) collective-permute-start(f32[2,17,32,128]{3,2,1,0:T(8,128)S(1)} %get-tuple-element.88), channel_id=1, source_target_pairs={{0,192},{64,0},{128,64},{192,128},{1,193},{65,1},{129,65},{193,129... | collective-permute-start | bytes 1671176 | tf_op jit(solution)/shard_map/ppermute | solution.py:711
  26.1 27.9 %collective-permute-start.3 = (f32[2,17,32,128]{3,2,1,0:T(8,128)}, f32[2,17,32,128]{3,2,1,0:T(8,128)S(1)}, u32[]{:S(2)}, u32[]{:S(2)}) collective-permute-start(f32[2,17,32,128]{3,2,1,0:T(8,128)} %get-tuple-element.89), channel_id=1, source_target_pairs={{0,128},{64,192},{128,0},{192,64},{1,129},{65,193},{129,1},{193,65... | collective-permute-start | bytes 1671176 | tf_op jit(solution)/shard_map/ppermute | solution.py:711
  27.3 27.0 %collective-permute-start.4 = (f32[2,17,32,128]{3,2,1,0:T(8,128)}, f32[2,17,32,128]{3,2,1,0:T(8,128)S(1)}, u32[]{:S(2)}, u32[]{:S(2)}) collective-permute-start(f32[2,17,32,128]{3,2,1,0:T(8,128)} %get-tuple-element.90), channel_id=1, source_target_pairs={{0,64},{64,128},{128,192},{192,0},{1,65},{65,129},{129,193},{193,1... | collective-permute-start | bytes 1671176 | tf_op jit(solution)/shard_map/ppermute | solution.py:711
  27.3 35.2 %copy-start.2 = (f32[16,1024]{1,0:T(8,128)S(1)}, f32[16,1024]{1,0:T(8,128)}, u32[]{:S(2)}) copy-start(f32[16,1024]{1,0:T(8,128)} %refs_1_.1) | copy-start | bytes 196612
  27.3 35.2 %copy-start.3 = (f32[16,1024]{1,0:T(8,128)S(1)}, f32[16,1024]{1,0:T(8,128)}, u32[]{:S(2)}) copy-start(f32[16,1024]{1,0:T(8,128)} %refs_2_.1) | copy-start | bytes 196612
  27.3 35.2 %copy-start.4 = (f32[16,1024]{1,0:T(8,128)S(1)}, f32[16,1024]{1,0:T(8,128)}, u32[]{:S(2)}) copy-start(f32[16,1024]{1,0:T(8,128)} %refs_3_.1) | copy-start | bytes 196612
  54.3 16.8 %all-to-all-start.3 = ((f32[8,48,128]{2,1,0:T(8,128)}), f32[8,48,128]{2,1,0:T(8,128)}, u32[]{:S(2)}, u32[]{:S(2)}) async-start(f32[8,48,128]{2,1,0:T(8,128)} %total.3), calls=%async_computation.3 | async-start | bytes 393216 | tf_op jit(solution)/shard_map/all_to_all | solution.py:689
  63.5 20.0 %collective-permute-start.5 = (f32[816,128]{1,0:T(8,128)}, f32[816,128]{1,0:T(8,128)S(1)}, u32[]{:S(2)}, u32[]{:S(2)}) collective-permute-start(f32[816,128]{1,0:T(8,128)} %get-tuple-element.96), channel_id=1, source_target_pairs={{0,1},{1,2},{2,3},{3,4},{4,5},{5,6},{6,7},{7,8},{8,9},{9,10},{10,1... | collective-permute-start | bytes 1253384 | tf_op jit(solution)/shard_map/ppermute | solution.py:723
  65.7 17.8 %collective-permute-start.6 = (f32[816,128]{1,0:T(8,128)}, f32[816,128]{1,0:T(8,128)S(1)}, u32[]{:S(2)}, u32[]{:S(2)}) collective-permute-start(f32[816,128]{1,0:T(8,128)} %get-tuple-element.97), channel_id=1, source_target_pairs={{1,0},{2,1},{3,2},{4,3},{5,4},{6,5},{7,6},{8,7},{9,8},{10,9},{11,1... | collective-permute-start | bytes 1253384 | tf_op jit(solution)/shard_map/ppermute | solution.py:723
  87.9 17.0 %collective-permute-start.9 = (f32[512,128]{1,0:T(8,128)S(1)}, f32[512,128]{1,0:T(8,128)S(1)}, u32[]{:S(2)}, u32[]{:S(2)}) collective-permute-start(f32[512,128]{1,0:T(8,128)S(1)} %forecast.5), channel_id=1, source_target_pairs={{0,128},{32,160},{64,192},{96,224},{128,0},{160,32},{192,64},{224,... | collective-permute-start | bytes 786440 | tf_op jit(solution)/shard_map/ppermute | solution.py:717
  95.7 15.9 %collective-permute-start.12 = (f32[512,128]{1,0:T(8,128)S(1)}, f32[512,128]{1,0:T(8,128)S(1)}, u32[]{:S(2)}, u32[]{:S(2)}) collective-permute-start(f32[512,128]{1,0:T(8,128)S(1)} %get-tuple-element.138), channel_id=1, source_target_pairs={{0,64},{32,96},{64,128},{96,160},{128,192},{160,224},{192,0},{224,... | collective-permute-start | bytes 786440 | tf_op jit(solution)/shard_map/ppermute | solution.py:717
  96.1 17.0 %collective-permute-start.13 = (f32[512,128]{1,0:T(8,128)S(1)}, f32[512,128]{1,0:T(8,128)S(1)}, u32[]{:S(2)}, u32[]{:S(2)}) collective-permute-start(f32[512,128]{1,0:T(8,128)S(1)} %get-tuple-element.139), channel_id=1, source_target_pairs={{0,192},{32,224},{64,0},{96,32},{128,64},{160,96},{192,128},{224,1... | collective-permute-start | bytes 786440 | tf_op jit(solution)/shard_map/ppermute | solution.py:717
  104.0 13.0 %collective-permute-start.7 = (f32[512,128]{1,0:T(8,128)S(1)}, f32[512,128]{1,0:T(8,128)S(1)}, u32[]{:S(2)}, u32[]{:S(2)}) collective-permute-start(f32[512,128]{1,0:T(8,128)S(1)} %get-tuple-element.124), channel_id=1, source_target_pairs={{0,160},{32,128},{64,224},{96,192},{128,32},{160,0},{192,96},{224,... | collective-permute-start | bytes 786440 | tf_op jit(solution)/shard_map/ppermute | solution.py:717
  104.5 15.6 %collective-permute-start.8 = (f32[512,128]{1,0:T(8,128)S(1)}, f32[512,128]{1,0:T(8,128)S(1)}, u32[]{:S(2)}, u32[]{:S(2)}) collective-permute-start(f32[512,128]{1,0:T(8,128)S(1)} %get-tuple-element.125), channel_id=1, source_target_pairs={{0,96},{32,64},{64,160},{96,128},{128,224},{160,192},{192,32},{224... | collective-permute-start | bytes 786440 | tf_op jit(solution)/shard_map/ppermute | solution.py:717
  109.1 11.0 %collective-permute-start.10 = (f32[512,128]{1,0:T(8,128)S(1)}, f32[512,128]{1,0:T(8,128)S(1)}, u32[]{:S(2)}, u32[]{:S(2)}) collective-permute-start(f32[512,128]{1,0:T(8,128)S(1)} %get-tuple-element.135), channel_id=1, source_target_pairs={{0,224},{32,192},{64,32},{96,0},{128,96},{160,64},{192,160},{224,1... | collective-permute-start | bytes 786440 | tf_op jit(solution)/shard_map/ppermute | solution.py:717
  111.6 8.4 %collective-permute-start.11 = (f32[512,128]{1,0:T(8,128)S(1)}, f32[512,128]{1,0:T(8,128)S(1)}, u32[]{:S(2)}, u32[]{:S(2)}) collective-permute-start(f32[512,128]{1,0:T(8,128)S(1)} %get-tuple-element.136), channel_id=1, source_target_pairs={{0,32},{32,0},{64,96},{96,64},{128,160},{160,128},{192,224},{224,1... | collective-permute-start | bytes 786440 | tf_op jit(solution)/shard_map/ppermute | solution.py:717
  (2 other events, 1.7 us)
